TPU v7x, 32 devices: a whole 2x2x4 slice. The times are simulated.
32 devices in a mesh: freq: 4 (over z), rcv: 8 (over y, x, core).
Axes of the slice: x: 2, y: 2, z: 4, core: 2. Of those that a mesh axis runs over, the one named last changes fastest.
Arguments:
- spectra: float32 [64, 2, 512, 512], P('freq', None, 'rcv'), may hold values from -0.5 to 0.5
- counts: int32 [4], replicated, may hold values from 1 to 16, 32 in all
- partner: int32 [512], replicated, may hold values from 0 to 511, as said below
- recorded: float32 [512, 512, 512], P('freq', 'rcv'), may hold values from -3 to 3
- gain_index: int32 [512, 512], P('freq', 'rcv'), may hold values from 0 to 15
- gain_table: float32 [2, 16], replicated, may hold values from 0.5 to 1.5
Outputs:
- primaries: float32 [512, 512, 512], P('freq', 'rcv')
Inputs may be any that keep to these rules, and one draw needn't show every extreme that they name: `counts`: the bands hold 32 frequencies together, and some band holds exactly 16. `partner`: A permutation that maps each aligned block of 64 indices onto itself.
All inputs are finite; a program needn't handle non-finite values.
Results may differ from a plain program's by a relative error of at most 0.00005.
Values sent between devices are 32-bit elements; how exact they have to be, the bound alone decides.
No kernel may reach another device: no remote copies, remote signals or barrier semaphores. Data moves between devices by JAX's collectives and lax.ppermute only.
A program may use at most 128 MiB of HBM per device.

v0:
```python
import functools

import jax
import jax.numpy as jnp
from jax import lax
from jax.experimental import pallas as pl
from jax.experimental.pallas import tpu as pltpu
from jax.sharding import PartitionSpec as P

LEVELS = 16
PICK = 256
LANES = 128
ROWS = 8


def time_table(bin_numbers, samples):
    phases = bin_numbers[:, None] * jnp.arange(samples, dtype=jnp.int32)[None, :] % samples
    angles = 2.0 * jnp.pi / samples * phases.astype(jnp.float32)
    return jnp.stack([jnp.cos(angles), -jnp.sin(angles)], axis=1)


def split(values):
    high = values.astype(jnp.bfloat16)
    return high, (values - high.astype(jnp.float32)).astype(jnp.bfloat16)


def mm(left, right):
    return jnp.dot(left, right, preferred_element_type=jnp.float32)


def gather_table(partner_column, start, size):
    columns = lax.broadcasted_iota(jnp.int32, (size, size), 1) + start
    return jnp.where(partner_column == columns, 1.0, 0.0).astype(jnp.bfloat16)


def scatter_table(partner_row, start, size):
    rows = lax.broadcasted_iota(jnp.int32, (size, size), 0) + start
    return jnp.where(partner_row == rows, 1.0, 0.0).astype(jnp.bfloat16)


def gains_kernel(table_ref, near_ref, far_ref, column_ref, out_ref, tiles_ref, *, source_tiles):
    receiver_tile, source_tile = near_ref.shape[2:]
    side = source_tiles * source_tile
    receiver_tiles = side // receiver_tile
    for half, ref in enumerate((near_ref, far_ref)):
        for h in range(ref.shape[0]):
            for e in range(source_tiles):
                tile = (lax.axis_index("freq") ^ e) * receiver_tiles + (lax.axis_index("rcv") ^ (2 * h + half))
                tiles_ref[tile] = ref[h, e].astype(jnp.float32)
    pick = min(PICK, side)
    for start in range(0, side, pick):
        rows = slice(start, start + pick)
        table = gather_table(column_ref[rows, :], start, pick)
        first_tile = start // receiver_tile
        for a in range(source_tiles):
            cols = slice(a * source_tile, (a + 1) * source_tile)
            lo = a * receiver_tiles + first_tile
            natural = tiles_ref[lo : lo + pick // receiver_tile].reshape(pick, source_tile)
            levels = mm(table, natural.astype(jnp.bfloat16))
            first = jnp.zeros_like(levels)
            second = jnp.zeros_like(levels)
            for level in range(LEVELS):
                here = levels == float(level)
                first = jnp.where(here, 0.5 * table_ref[0, level], first)
                second = jnp.where(here, 0.5 * table_ref[1, level], second)
            out_ref[0, rows, cols] = first
            out_ref[1, rows, cols] = second


def pack_kernel(spectra_ref, *refs, first_slot):
    outs, (stage, in_sems, out_sems) = refs[:-3], refs[-3:]
    rank = lax.axis_index("rcv")
    loads = [
        pltpu.make_async_copy(spectra_ref.at[first_slot + (rank ^ (n + 1))], stage.at[n], in_sems.at[n])
        for n in range(len(outs))
    ]
    stores = [pltpu.make_async_copy(stage.at[n], out, out_sems.at[n]) for n, out in enumerate(outs)]
    for load in loads:
        load.start()
    for load, store in zip(loads, stores):
        load.wait()
        store.start()
    for store in stores:
        store.wait()


def multiples_kernel(counts_ref, column_ref, row_ref, spectra_ref, gains_hbm, *refs, first_slot):
    tiles, (out, result, data, gains, u, w, y1, y2, tile_sems, gain_sem, out_sems) = refs[:-11], refs[-11:]
    source_tiles, receiver_tiles, _, receiver_tile, source_tile = result.shape
    side = data.shape[3]
    pick = min(PICK, side)
    rank = lax.axis_index("rcv")
    plane = lax.axis_index("freq")
    live = first_slot + rank < counts_ref[plane]

    def send(first, count):
        tiles_of = pl.ds(first, count)
        return [
            pltpu.make_async_copy(result.at[a, tiles_of], out.at[a, tiles_of], out_sems.at[a, first // count])
            for a in range(source_tiles)
        ]

    at_once = pick // receiver_tile
    copies = [copy for first in range(0, receiver_tiles, at_once) for copy in send(first, at_once)]

    @pl.when(jnp.logical_not(live))
    def _():
        result[...] = jnp.zeros_like(result)
        for copy in copies:
            copy.start()

    @pl.when(live)
    def _():
        sources = [spectra_ref.at[first_slot + rank]] + list(tiles)
        copies = [pltpu.make_async_copy(source, data.at[n], tile_sems.at[n]) for n, source in enumerate(sources)]
        for copy in copies:
            copy.start()
        gain_copy = pltpu.make_async_copy(gains_hbm, gains, gain_sem)
        gain_copy.start()
        for n, copy in enumerate(copies):
            copy.wait()
            first_row = (rank ^ n) * receiver_tile
            real, imag = split(data[n, 0]), split(data[n, 1])
            for place, part in ((0, 0), (1, 1), (2, 0)):
                top = pl.ds(pl.multiple_of(first_row + place * 2 * side, receiver_tile), receiver_tile)
                low = pl.ds(pl.multiple_of(first_row + (place * 2 + 1) * side, receiver_tile), receiver_tile)
                w[top, :side] = real[part]
                w[top, side:] = imag[part]
                w[low, :side] = -imag[part]
                w[low, side:] = real[part]
        high, again, low = (slice(n * 2 * side, (n + 1) * 2 * side) for n in range(3))
        for start in range(0, side, pick):
            rows = slice(start, start + pick)
            table = gather_table(column_ref[rows, :], start, pick)
            u[rows, high] = mm(table, w[rows, :]).astype(jnp.bfloat16)
            u[rows, again] = u[rows, high]
            u[rows, low] = mm(table, w[2 * side + start : 2 * side + start + pick, :]).astype(jnp.bfloat16)

        def product(result, beside=()):
            columns = range(0, 2 * side, PICK)
            each = -(-len(beside) // len(columns))
            for n, start in enumerate(columns):
                cols = slice(start, start + PICK)
                result[:, cols] = mm(u[...], w[:, cols])
                for work in beside[n * each : (n + 1) * each]:
                    work()

        block = 128

        def weigh(y, order, q, s):
            qs, ss = slice(q, q + block), slice(s, s + block)
            for c in range(2):
                qc, sc = slice(c * side + q, c * side + q + block), slice(c * side + s, c * side + s + block)
                total = y[qs, sc] + y[ss, qc].T
                if q != s:
                    y[ss, qc] = gains[order, ss, qs] * total.T
                y[qs, sc] = gains[order, qs, ss] * total

        pairs = [(q, s) for q in range(0, side, block) for s in range(q, side, block)]
        product(y1)
        for start in range(0, side, 64):
            rows = slice(start, start + 64)
            u[rows, high], u[rows, low] = split(y1[rows, :])
            u[rows, again] = u[rows, high]
        gain_copy.wait()
        product(y2, [functools.partial(weigh, y1, 0, q, s) for q, s in pairs])
        for q, s in pairs:
            weigh(y2, 1, q, s)
        for start in range(0, side, pick):
            rows = slice(start, start + pick)
            table = scatter_table(row_ref[:, rows], start, pick)
            for c in range(2):
                cols = slice(c * side, (c + 1) * side)
                value_high, value_low = split(y1[rows, cols] + y2[rows, cols])
                natural = mm(table, value_high) + mm(table, value_low)
                for i in range(pick // receiver_tile):
                    tile = start // receiver_tile + i
                    for a in range(source_tiles):
                        result[a, tile, c] = natural[
                            i * receiver_tile : (i + 1) * receiver_tile, a * source_tile : (a + 1) * source_tile
                        ]
            for copy in send(start // receiver_tile, at_once):
                copy.start()

    for copy in copies:
        copy.wait()


def synthesis_kernel(table_ref, base_ref, *refs, receiver_tile):
    coefs, (out_ref, coef_ref, lines, tables, sems) = refs[:-5], refs[-5:]
    depth = table_ref.shape[0]
    source_tile = coef_ref.shape[1]
    first = pl.multiple_of(pl.program_id(0) * ROWS, ROWS)

    @pl.when(pl.program_id(0) == 0)
    def _():
        size = coef_ref.shape[0] // len(coefs)
        copies = [
            pltpu.make_async_copy(coef, coef_ref.at[pl.ds(n * size, size)], sems.at[n]) for n, coef in enumerate(coefs)
        ]
        for copy in copies:
            copy.start()
        high, low = split(table_ref[...])
        tables[:depth, :] = high
        tables[depth : 2 * depth, :] = high
        tables[2 * depth :, :] = low
        for copy in copies:
            copy.wait()

    for r in range(ROWS):
        column = coef_ref[pl.ds(first + r, depth, stride=receiver_tile), :]
        high = column.astype(jnp.bfloat16).astype(jnp.float32)
        both = jnp.concatenate([high, column - high], axis=0)
        for g in range(lines.shape[0]):
            lines[g, pl.ds(r, source_tile, stride=ROWS), :] = both[g * LANES : (g + 1) * LANES].T

    size = 32
    for start in range(0, source_tile, size):
        rows = slice(start * ROWS, (start + size) * ROWS)
        both = jnp.concatenate([lines[g, rows, :] for g in range(lines.shape[0])], axis=1).astype(jnp.bfloat16)
        total = mm(jnp.concatenate([both, both[:, :depth]], axis=1), tables[...])
        out_ref[start : start + size] = base_ref[start : start + size] - total.reshape(size, ROWS, -1)


def params(mebibytes):
    return pltpu.CompilerParams(vmem_limit_bytes=mebibytes * 1024 * 1024)


def whole_in(space=pltpu.VMEM):
    return pl.BlockSpec(memory_space=space)


def exchange(array, axis, distance):
    return lax.ppermute(array, axis, [(i, i ^ distance) for i in range(lax.axis_size(axis))])


def on_device(spectra, counts, partner, recorded, gain_index, gain_table):
    freq_count = lax.axis_size("freq")
    rcv_count = lax.axis_size("rcv")
    capacity, _, receiver_tile, side = spectra.shape
    source_tile, _, samples = recorded.shape
    parts = capacity // rcv_count
    senders = freq_count * rcv_count
    column = partner[:, None]
    row = partner[None, :]
    hbm = whole_in(pltpu.HBM)
    smem = whole_in(pltpu.SMEM)

    def gather(part, slots):
        tile = pltpu.HBM(spectra.shape[1:], spectra.dtype)
        packed = pl.pallas_call(
            functools.partial(pack_kernel, first_slot=part * rcv_count),
            out_shape=[tile] * (rcv_count - 1),
            in_specs=[hbm],
            out_specs=[hbm] * (rcv_count - 1),
            scratch_shapes=[
                pltpu.VMEM((rcv_count - 1,) + spectra.shape[1:], spectra.dtype),
                pltpu.SemaphoreType.DMA((rcv_count - 1,)),
                pltpu.SemaphoreType.DMA((rcv_count - 1,)),
            ],
            name="pack",
        )(slots)
        return packed, [exchange(tile, "rcv", n + 1) for n, tile in enumerate(packed)]

    def synthesis(coefs, table, base):
        depth = table.shape[0]
        block = pl.BlockSpec((source_tile, ROWS, samples), lambda n: (0, n, 0))
        return pl.pallas_call(
            functools.partial(synthesis_kernel, receiver_tile=receiver_tile),
            out_shape=jax.ShapeDtypeStruct(recorded.shape, jnp.float32),
            grid=(receiver_tile // ROWS,),
            in_specs=[whole_in(), block] + [hbm] * len(coefs),
            out_specs=block,
            scratch_shapes=[
                pltpu.VMEM((depth * receiver_tile, source_tile), jnp.float32),
                pltpu.VMEM((2 * depth // LANES, source_tile * ROWS, LANES), jnp.float32),
                pltpu.VMEM((3 * depth, samples), jnp.bfloat16),
                pltpu.SemaphoreType.DMA((len(coefs),)),
            ],
            compiler_params=params(24),
            name="synthesis",
        )(table, base, *coefs)

    def doubled(array, axis, distance):
        return jnp.concatenate([array, exchange(array, axis, distance)])

    _, first_tiles = gather(0, spectra)
    line = gain_index.T[None]
    distance = 1
    while distance < freq_count:
        line = doubled(line, "freq", distance)
        distance *= 2
    near = line[None]
    distance = 2
    while distance < rcv_count:
        near = doubled(near, "rcv", distance)
        distance *= 2
    far = exchange(near, "rcv", 1)
    gains = pl.pallas_call(
        functools.partial(gains_kernel, source_tiles=freq_count),
        out_shape=jax.ShapeDtypeStruct((2, side, side), jnp.float32),
        in_specs=[smem, whole_in(), whole_in(), whole_in()],
        out_specs=whole_in(),
        scratch_shapes=[pltpu.VMEM((senders, receiver_tile, source_tile), jnp.float32)],
        compiler_params=params(16),
        name="gains",
    )(gain_table, near, far, column)

    gathered = [first_tiles]
    slots = spectra
    for part in range(1, parts):
        slots, *gathered[-1] = lax.optimization_barrier((slots, *gathered[-1]))
        packed, tiles = gather(part, slots)
        gathered[-1][0], _ = lax.optimization_barrier((gathered[-1][0], packed[0]))
        gathered.append(tiles)

    results = []
    for part in range(parts):
        result = pl.pallas_call(
            functools.partial(multiples_kernel, first_slot=part * rcv_count),
            out_shape=pltpu.HBM((freq_count, rcv_count, 2, receiver_tile, source_tile), jnp.float32),
            in_specs=[smem, whole_in(), whole_in()] + [hbm] * (1 + rcv_count),
            out_specs=hbm,
            scratch_shapes=[
                pltpu.VMEM((freq_count, rcv_count, 2, receiver_tile, source_tile), jnp.float32),
                pltpu.VMEM((rcv_count, 2, receiver_tile, side), jnp.float32),
                pltpu.VMEM((2, side, side), jnp.float32),
                pltpu.VMEM((side, 6 * side), jnp.bfloat16),
                pltpu.VMEM((6 * side, 2 * side), jnp.bfloat16),
                pltpu.VMEM((side, 2 * side), jnp.float32),
                pltpu.VMEM((side, 2 * side), jnp.float32),
                pltpu.SemaphoreType.DMA((rcv_count,)),
                pltpu.SemaphoreType.DMA,
                pltpu.SemaphoreType.DMA((freq_count, rcv_count)),
            ],
            compiler_params=params(48),
            name="multiples",
        )(counts, column, row, spectra, gains, *gathered[part])
        if part < parts - 1:
            gathered[part + 1][0], result = lax.optimization_barrier((gathered[part + 1][0], result))
        results.append(result.reshape((senders,) + result.shape[2:]))

    before = jnp.arange(freq_count)[None, :] < jnp.arange(freq_count)[:, None]
    offsets = jnp.sum(jnp.where(before, counts[None, :], 0), axis=1)
    ranks = jnp.arange(rcv_count, dtype=jnp.int32)
    base = recorded
    for part, result in enumerate(results):
        coefs = lax.all_to_all(result, ("freq", "rcv"), split_axis=0, concat_axis=0, tiled=True)
        bins = offsets[:, None] + part * rcv_count + ranks[None, :] + 1
        table = time_table(bins.reshape(-1), samples).reshape(-1, samples)
        if part < parts - 1:
            coefs, _ = lax.optimization_barrier((coefs, results[part + 1]))
        base = synthesis([coefs.reshape(-1, source_tile)], table, base)
    return base


def solution(mesh):
    placed = (P("freq", None, "rcv", None), P(), P(), P("freq", "rcv", None), P("freq", "rcv"), P())
    return jax.shard_map(
        on_device, mesh=mesh, in_specs=placed, out_specs=P("freq", "rcv", None), check_vma=False
    )
```

profile of v0, /device:TPU:0, one launch (start us, length us, event | category | flops | bytes accessed | tf_op | source)
XLA Modules:
  0.0 208.0 jit_solution(3941979563417020982)
XLA Ops:
  0.0 3.0 %collective-permute-start.8 = (s32[1,64,128]{2,1,0:T(8,128)}, s32[1,64,128]{2,1,0:T(8,128)S(1)}, u32[]{:S(2)}, u32[]{:S(2)}) collective-permute-start(s32[1,64,128]{2,1,0:T(8,128)} %bitcast.17), channel_id=1, source_target_pairs={{0,8},{8,0},{16,24},{24,16},{1,9},{9,1},{17,25},{25,17},{2,10},{10... | collective-permute-start | bytes 98312 | tf_op jit(solution)/shard_map/ppermute | solution.py:234
  5.9 3.0 %collective-permute-start.9 = (s32[2,64,128]{2,1,0:T(8,128)S(1)}, s32[2,64,128]{2,1,0:T(8,128)S(1)}, u32[]{:S(2)}, u32[]{:S(2)}) collective-permute-start(s32[2,64,128]{2,1,0:T(8,128)S(1)} %pad_add_fusion.2), channel_id=1, source_target_pairs={{0,16},{8,24},{16,0},{24,8},{1,17},{9,25},{17,1},{25,9},{2,18},{10... | collective-permute-start | bytes 196616 | tf_op jit(solution)/shard_map/ppermute | solution.py:234
  8.9 2.2 %collective-permute-done.9 = s32[2,64,128]{2,1,0:T(8,128)S(1)} collective-permute-done((s32[2,64,128]{2,1,0:T(8,128)S(1)}, s32[2,64,128]{2,1,0:T(8,128)S(1)}, u32[]{:S(2)}, u32[]{:S(2)}) %collective-permute-start.9) | collective-permute-done | bytes 65568 | tf_op jit(solution)/shard_map/ppermute | solution.py:234
  13.8 3.1 %collective-permute-done.10 = s32[1,4,64,128]{3,2,1,0:T(8,128)S(1)} collective-permute-done((s32[1,4,64,128]{3,2,1,0:T(8,128)S(1)}, s32[1,4,64,128]{3,2,1,0:T(8,128)S(1)}, u32[]{:S(2)}, u32[]{:S(2)}) %collective-permute-start.10) | collective-permute-done | bytes 131104 | tf_op jit(solution)/shard_map/ppermute | solution.py:234
  18.9 2.3 %pack.2 = (f32[2,64,512]{2,1,0:T(8,128)}, f32[2,64,512]{2,1,0:T(8,128)}, f32[2,64,512]{2,1,0:T(8,128)}, f32[2,64,512]{2,1,0:T(8,128)}, f32[2,64,512]{2,1,0:T(8,1...) custom-call(f32[16,2,64,512]{3,2,1,0:T(8,128)} %spectra_ref.6), custom_call_target="tpu_custom_call" | custom-call | tf_op jit(solution)/shard_map/pack/pallas_call | solution.py:251
  26.2 4.5 %collective-permute-done.1.refs_1_ = f32[2,64,512]{2,1,0:T(8,128)S(1)} collective-permute-done((f32[2,64,512]{2,1,0:T(8,128)}, f32[2,64,512]{2,1,0:T(8,128)S(1)}, u32[]{:S(2)}, u32[]{:S(2)}) %collective-permute-start.1) | collective-permute-done | bytes 262176 | tf_op jit(solution)/shard_map/ppermute | solution.py:234
  32.8 2.6 %collective-permute-done.2.refs_2_ = f32[2,64,512]{2,1,0:T(8,128)S(1)} collective-permute-done((f32[2,64,512]{2,1,0:T(8,128)}, f32[2,64,512]{2,1,0:T(8,128)S(1)}, u32[]{:S(2)}, u32[]{:S(2)}) %collective-permute-start.2) | collective-permute-done | bytes 262176 | tf_op jit(solution)/shard_map/ppermute | solution.py:234
  38.9 9.3 %collective-permute-done.4.refs_4_ = f32[2,64,512]{2,1,0:T(8,128)S(1)} collective-permute-done((f32[2,64,512]{2,1,0:T(8,128)}, f32[2,64,512]{2,1,0:T(8,128)S(1)}, u32[]{:S(2)}, u32[]{:S(2)}) %collective-permute-start.4) | collective-permute-done | bytes 262176 | tf_op jit(solution)/shard_map/ppermute | solution.py:234
  50.4 2.3 %pack.3 = (f32[2,64,512]{2,1,0:T(8,128)}, f32[2,64,512]{2,1,0:T(8,128)}, f32[2,64,512]{2,1,0:T(8,128)}, f32[2,64,512]{2,1,0:T(8,128)}, f32[2,64,512]{2,1,0:T(8,1...) custom-call(f32[16,2,64,512]{3,2,1,0:T(8,128)} %spectra_ref.6), custom_call_target="tpu_custom_call" | custom-call | tf_op jit(solution)/shard_map/pack/pallas_call | solution.py:251
  53.3 2.5 %gains.1.gains_hbm = f32[2,512,512]{2,1,0:T(8,128)S(1)} custom-call(f32[2,16]{1,0:T(2,128)S(1)} %copy-done.18, s32[4,4,64,128]{3,2,1,0:T(8,128)S(1)} %pad_add_fusion.near_ref, s32[4,4,64,128]{3,2,1,0:T(8,128)S(1)} %collective-permute-done.12.far_ref, s32[512,1]{1,0:T(8,128)S(1)} %copy.16.column_ref), custom_call_target="tpu_custom_call" | custom-call | tf_op jit(solution)/shard_map/gains/pallas_call | solution.py:299
  61.6 11.7 %multiples.2 = f32[4,8,2,64,128]{4,3,2,1,0:T(8,128)} custom-call(s32[4]{0:T(128)S(1)} %copy-done.17, s32[512,1]{1,0:T(8,128)S(1)} %copy.16.column_ref, s32[1,512]{1,0:T(1,128)S(1)} %bitcast.13, f32[16,2,64,512]{3,2,1,0:T(8,128)} %spectra_ref.6, f32[2,512,512]{2,1,0:T(8,128)S(1)} %gains.1.gains_hbm, f32[2,64,512]{2,1,0:T(8,128)S(1)} %copy-done.3, ...), custom_call_target="tpu_custom_call" | custom-call | tf_op jit(solution)/shard_map/multiples/pallas_call | solution.py:319
  73.4 5.6 %all-to-all-start = ((f32[32,2,64,128]{3,2,1,0:T(8,128)}), f32[32,2,64,128]{3,2,1,0:T(8,128)}, u32[]{:S(2)}, u32[]{:S(2)}) async-start(f32[32,2,64,128]{3,2,1,0:T(8,128)} %bitcast.15), calls=%async_computation | async-start | bytes 4194304 | tf_op jit(solution)/shard_map/all_to_all | solution.py:348
  82.6 2.6 %collective-permute-start.17 = (f32[2,64,512]{2,1,0:T(8,128)S(1)}, f32[2,64,512]{2,1,0:T(8,128)S(1)}, u32[]{:S(2)}, u32[]{:S(2)}) collective-permute-start(f32[2,64,512]{2,1,0:T(8,128)S(1)} %copy-done.20), channel_id=1, source_target_pairs={{0,6},{1,7},{2,4},{3,5},{4,2},{5,3},{6,0},{7,1},{8,14},{9,15},{10,... | collective-permute-start | bytes 786440 | tf_op jit(solution)/shard_map/ppermute | solution.py:234
  85.2 20.4 %collective-permute-done.13.refs_1_ = f32[2,64,512]{2,1,0:T(8,128)S(1)} collective-permute-done((f32[2,64,512]{2,1,0:T(8,128)}, f32[2,64,512]{2,1,0:T(8,128)S(1)}, u32[]{:S(2)}, u32[]{:S(2)}) %collective-permute-start.13) | collective-permute-done | bytes 262176 | tf_op jit(solution)/shard_map/ppermute | solution.py:234
  106.0 6.1 %collective-permute-done.14.refs_2_ = f32[2,64,512]{2,1,0:T(8,128)S(1)} collective-permute-done((f32[2,64,512]{2,1,0:T(8,128)}, f32[2,64,512]{2,1,0:T(8,128)S(1)}, u32[]{:S(2)}, u32[]{:S(2)}) %collective-permute-start.14) | collective-permute-done | bytes 262176 | tf_op jit(solution)/shard_map/ppermute | solution.py:234
  112.2 8.3 %collective-permute-done.17.refs_5_ = f32[2,64,512]{2,1,0:T(8,128)S(1)} collective-permute-done((f32[2,64,512]{2,1,0:T(8,128)S(1)}, f32[2,64,512]{2,1,0:T(8,128)S(1)}, u32[]{:S(2)}, u32[]{:S(2)}) %collective-permute-start.17) | collective-permute-done | bytes 262176 | tf_op jit(solution)/shard_map/ppermute | solution.py:234
  120.4 7.4 %collective-permute-done.18.refs_6_ = f32[2,64,512]{2,1,0:T(8,128)S(1)} collective-permute-done((f32[2,64,512]{2,1,0:T(8,128)S(1)}, f32[2,64,512]{2,1,0:T(8,128)S(1)}, u32[]{:S(2)}, u32[]{:S(2)}) %collective-permute-start.18) | collective-permute-done | bytes 262176 | tf_op jit(solution)/shard_map/ppermute | solution.py:234
  127.9 2.6 %multiples.3 = f32[4,8,2,64,128]{4,3,2,1,0:T(8,128)} custom-call(s32[4]{0:T(128)S(1)} %copy-done.17, s32[512,1]{1,0:T(8,128)S(1)} %copy.16.column_ref, s32[1,512]{1,0:T(1,128)S(1)} %bitcast.14, f32[16,2,64,512]{3,2,1,0:T(8,128)} %spectra_ref.6, f32[2,512,512]{2,1,0:T(8,128)S(1)} %gains.1.gains_hbm, f32[2,64,512]{2,1,0:T(8,128)} %collective-permute-done.7.refs_0_, ...), custom_call_target="tpu_custom_call" | custom-call | tf_op jit(solution)/shard_map/multiples/pallas_call | solution.py:319
  130.5 13.3 %all-to-all-start.1 = ((f32[32,2,64,128]{3,2,1,0:T(8,128)}), f32[32,2,64,128]{3,2,1,0:T(8,128)S(1)}, u32[]{:S(2)}, u32[]{:S(2)}) async-start(f32[32,2,64,128]{3,2,1,0:T(8,128)} %bitcast.16), calls=%async_computation.1 | async-start | bytes 4194304 | tf_op jit(solution)/shard_map/all_to_all | solution.py:348
  145.4 12.5 %synthesis.2.base_ref = f32[128,64,512]{2,1,0:T(8,128)S(1)} custom-call(f32[64,512]{1,0:T(8,128)S(1)} %reshape.251.table_ref, f32[128,64,512]{2,1,0:T(8,128)} %base_ref.1, f32[4096,128]{1,0:T(8,128)} %bitcast.8.refs_0_), custom_call_target="tpu_custom_call" | custom-call | tf_op jit(solution)/shard_map/synthesis/pallas_call | solution.py:268
  157.9 6.2 %copy-done = f32[128,64,512]{2,1,0:T(8,128)} copy-done((f32[128,64,512]{2,1,0:T(8,128)}, f32[128,64,512]{2,1,0:T(8,128)S(1)}, u32[]{:S(2)}) %copy-start) | copy-done | bytes 16777240
  164.1 28.7 %all-to-all-done.1 = f32[32,2,64,128]{3,2,1,0:T(8,128)S(1)} async-done(((f32[32,2,64,128]{3,2,1,0:T(8,128)}), f32[32,2,64,128]{3,2,1,0:T(8,128)S(1)}, u32[]{:S(2)}, u32[]{:S(2)}) %all-to-all-start.1) | async-done | bytes 2097184 | tf_op jit(solution)/shard_map/all_to_all | solution.py:348
  192.7 5.8 %copy-done.1 = f32[128,64,512]{2,1,0:T(8,128)S(1)} copy-done((f32[128,64,512]{2,1,0:T(8,128)S(1)}, f32[128,64,512]{2,1,0:T(8,128)}, u32[]{:S(2)}) %copy-start.1) | copy-done | bytes 16777240
  198.5 9.3 %synthesis.3 = f32[128,64,512]{2,1,0:T(8,128)} custom-call(f32[64,512]{1,0:T(8,128)S(1)} %reshape.250.table_ref, f32[128,64,512]{2,1,0:T(8,128)S(1)} %copy-done.1, f32[4096,128]{1,0:T(8,128)S(1)} %bitcast.11), custom_call_target="tpu_custom_call" | custom-call | tf_op jit(solution)/shard_map/synthesis/pallas_call | solution.py:268
  (90 shorter events, 32.1 us)
Async XLA Ops:
  0.0 5.1 %collective-permute-start.8 = (s32[1,64,128]{2,1,0:T(8,128)}, s32[1,64,128]{2,1,0:T(8,128)S(1)}, u32[]{:S(2)}, u32[]{:S(2)}) collective-permute-start(s32[1,64,128]{2,1,0:T(8,128)} %bitcast.17), channel_id=1, source_target_pairs={{0,8},{8,0},{16,24},{24,16},{1,9},{9,1},{17,25},{25,17},{2,10},{10... | collective-permute-start | bytes 98312 | tf_op jit(solution)/shard_map/ppermute | solution.py:234
  5.9 5.3 %collective-permute-start.9 = (s32[2,64,128]{2,1,0:T(8,128)S(1)}, s32[2,64,128]{2,1,0:T(8,128)S(1)}, u32[]{:S(2)}, u32[]{:S(2)}) collective-permute-start(s32[2,64,128]{2,1,0:T(8,128)S(1)} %pad_add_fusion.2), channel_id=1, source_target_pairs={{0,16},{8,24},{16,0},{24,8},{1,17},{9,25},{17,1},{25,9},{2,18},{10... | collective-permute-start | bytes 196616 | tf_op jit(solution)/shard_map/ppermute | solution.py:234
  11.9 5.0 %collective-permute-start.10 = (s32[1,4,64,128]{3,2,1,0:T(8,128)S(1)}, s32[1,4,64,128]{3,2,1,0:T(8,128)S(1)}, u32[]{:S(2)}, u32[]{:S(2)}) collective-permute-start(s32[1,4,64,128]{3,2,1,0:T(8,128)S(1)} %add_bitcast_fusion), channel_id=1, source_target_pairs={{0,2},{1,3},{2,0},{3,1},{4,6},{5,7},{6,4},{7,5},{8,10},{9,11},{10,... | collective-permute-start | bytes 393224 | tf_op jit(solution)/shard_map/ppermute | solution.py:234
  17.0 6.5 %collective-permute-start.11 = (s32[2,4,64,128]{3,2,1,0:T(8,128)S(1)}, s32[2,4,64,128]{3,2,1,0:T(8,128)S(1)}, u32[]{:S(2)}, u32[]{:S(2)}) collective-permute-start(s32[2,4,64,128]{3,2,1,0:T(8,128)S(1)} %pad_add_fusion.1), channel_id=1, source_target_pairs={{0,4},{1,5},{2,6},{3,7},{4,0},{5,1},{6,2},{7,3},{8,12},{9,13},{10,... | collective-permute-start | bytes 786440 | tf_op jit(solution)/shard_map/ppermute | solution.py:234
  21.2 2.4 %collective-permute-start = (f32[2,64,512]{2,1,0:T(8,128)}, f32[2,64,512]{2,1,0:T(8,128)S(1)}, u32[]{:S(2)}, u32[]{:S(2)}) collective-permute-start(f32[2,64,512]{2,1,0:T(8,128)} %get-tuple-element.31), channel_id=1, source_target_pairs={{0,1},{1,0},{2,3},{3,2},{4,5},{5,4},{6,7},{7,6},{8,9},{9,8},{10,11... | collective-permute-start | bytes 786440 | tf_op jit(solution)/shard_map/ppermute | solution.py:234
  21.3 9.4 %collective-permute-start.1 = (f32[2,64,512]{2,1,0:T(8,128)}, f32[2,64,512]{2,1,0:T(8,128)S(1)}, u32[]{:S(2)}, u32[]{:S(2)}) collective-permute-start(f32[2,64,512]{2,1,0:T(8,128)} %get-tuple-element.32), channel_id=1, source_target_pairs={{0,2},{1,3},{2,0},{3,1},{4,6},{5,7},{6,4},{7,5},{8,10},{9,11},{10,... | collective-permute-start | bytes 786440 | tf_op jit(solution)/shard_map/ppermute | solution.py:234
  22.9 12.6 %collective-permute-start.2 = (f32[2,64,512]{2,1,0:T(8,128)}, f32[2,64,512]{2,1,0:T(8,128)S(1)}, u32[]{:S(2)}, u32[]{:S(2)}) collective-permute-start(f32[2,64,512]{2,1,0:T(8,128)} %get-tuple-element.33), channel_id=1, source_target_pairs={{0,3},{1,2},{2,1},{3,0},{4,7},{5,6},{6,5},{7,4},{8,11},{9,10},{10,... | collective-permute-start | bytes 786440 | tf_op jit(solution)/shard_map/ppermute | solution.py:234
  23.2 15.0 %collective-permute-start.3 = (f32[2,64,512]{2,1,0:T(8,128)}, f32[2,64,512]{2,1,0:T(8,128)S(1)}, u32[]{:S(2)}, u32[]{:S(2)}) collective-permute-start(f32[2,64,512]{2,1,0:T(8,128)} %get-tuple-element.34), channel_id=1, source_target_pairs={{0,4},{1,5},{2,6},{3,7},{4,0},{5,1},{6,2},{7,3},{8,12},{9,13},{10,... | collective-permute-start | bytes 786440 | tf_op jit(solution)/shard_map/ppermute | solution.py:234
  23.5 29.8 %collective-permute-start.12 = (s32[4,4,64,128]{3,2,1,0:T(8,128)S(1)}, s32[4,4,64,128]{3,2,1,0:T(8,128)S(1)}, u32[]{:S(2)}, u32[]{:S(2)}) collective-permute-start(s32[4,4,64,128]{3,2,1,0:T(8,128)S(1)} %pad_add_fusion.near_ref), channel_id=1, source_target_pairs={{0,1},{1,0},{2,3},{3,2},{4,5},{5,4},{6,7},{7,6},{8,9},{9,8},{10,11... | collective-permute-start | bytes 1572872 | tf_op jit(solution)/shard_map/ppermute | solution.py:234
  24.3 23.9 %collective-permute-start.4 = (f32[2,64,512]{2,1,0:T(8,128)}, f32[2,64,512]{2,1,0:T(8,128)S(1)}, u32[]{:S(2)}, u32[]{:S(2)}) collective-permute-start(f32[2,64,512]{2,1,0:T(8,128)} %get-tuple-element.35), channel_id=1, source_target_pairs={{0,5},{1,4},{2,7},{3,6},{4,1},{5,0},{6,3},{7,2},{8,13},{9,12},{10,... | collective-permute-start | bytes 786440 | tf_op jit(solution)/shard_map/ppermute | solution.py:234
  31.4 17.5 %collective-permute-start.5 = (f32[2,64,512]{2,1,0:T(8,128)}, f32[2,64,512]{2,1,0:T(8,128)S(1)}, u32[]{:S(2)}, u32[]{:S(2)}) collective-permute-start(f32[2,64,512]{2,1,0:T(8,128)} %get-tuple-element.36), channel_id=1, source_target_pairs={{0,6},{1,7},{2,4},{3,5},{4,2},{5,3},{6,0},{7,1},{8,14},{9,15},{10,... | collective-permute-start | bytes 786440 | tf_op jit(solution)/shard_map/ppermute | solution.py:234
  36.1 17.0 %copy-start.16 = (s32[512]{0:T(512)S(1)}, s32[512]{0:T(512)}, u32[]{:S(2)}) copy-start(s32[512]{0:T(512)} %param.8) | copy-start | bytes 6148
  36.2 17.2 %copy-start.18 = (f32[2,16]{1,0:T(2,128)S(1)}, f32[2,16]{1,0:T(2,128)}, u32[]{:S(2)}) copy-start(f32[2,16]{1,0:T(2,128)} %table_ref.1) | copy-start | bytes 388
  36.2 13.5 %collective-permute-start.6 = (f32[2,64,512]{2,1,0:T(8,128)}, f32[2,64,512]{2,1,0:T(8,128)S(1)}, u32[]{:S(2)}, u32[]{:S(2)}) collective-permute-start(f32[2,64,512]{2,1,0:T(8,128)} %get-tuple-element.37), channel_id=1, source_target_pairs={{0,7},{1,6},{2,5},{3,4},{4,3},{5,2},{6,1},{7,0},{8,15},{9,14},{10,... | collective-permute-start | bytes 786440 | tf_op jit(solution)/shard_map/ppermute | solution.py:234
  52.7 20.6 %collective-permute-start.7 = (f32[2,64,512]{2,1,0:T(8,128)}, f32[2,64,512]{2,1,0:T(8,128)}, u32[]{:S(2)}, u32[]{:S(2)}) collective-permute-start(f32[2,64,512]{2,1,0:T(8,128)} %get-tuple-element.39), channel_id=1, source_target_pairs={{0,1},{1,0},{2,3},{3,2},{4,5},{5,4},{6,7},{7,6},{8,9},{9,8},{10,11... | collective-permute-start | bytes 786440 | tf_op jit(solution)/shard_map/ppermute | solution.py:234
  73.4 32.2 %copy-start.19 = (f32[2,64,512]{2,1,0:T(8,128)S(1)}, f32[2,64,512]{2,1,0:T(8,128)}, u32[]{:S(2)}) copy-start(f32[2,64,512]{2,1,0:T(8,128)} %get-tuple-element.55) | copy-start | bytes 786436
  73.4 57.1 %all-to-all-start = ((f32[32,2,64,128]{3,2,1,0:T(8,128)}), f32[32,2,64,128]{3,2,1,0:T(8,128)}, u32[]{:S(2)}, u32[]{:S(2)}) async-start(f32[32,2,64,128]{3,2,1,0:T(8,128)} %bitcast.15), calls=%async_computation | async-start | bytes 4194304 | tf_op jit(solution)/shard_map/all_to_all | solution.py:348
  79.0 26.5 %collective-permute-start.13 = (f32[2,64,512]{2,1,0:T(8,128)}, f32[2,64,512]{2,1,0:T(8,128)S(1)}, u32[]{:S(2)}, u32[]{:S(2)}) collective-permute-start(f32[2,64,512]{2,1,0:T(8,128)} %get-tuple-element.50), channel_id=1, source_target_pairs={{0,2},{1,3},{2,0},{3,1},{4,6},{5,7},{6,4},{7,5},{8,10},{9,11},{10,... | collective-permute-start | bytes 786440 | tf_op jit(solution)/shard_map/ppermute | solution.py:234
  80.8 31.4 %collective-permute-start.14 = (f32[2,64,512]{2,1,0:T(8,128)}, f32[2,64,512]{2,1,0:T(8,128)S(1)}, u32[]{:S(2)}, u32[]{:S(2)}) collective-permute-start(f32[2,64,512]{2,1,0:T(8,128)} %get-tuple-element.51), channel_id=1, source_target_pairs={{0,3},{1,2},{2,1},{3,0},{4,7},{5,6},{6,5},{7,4},{8,11},{9,10},{10,... | collective-permute-start | bytes 786440 | tf_op jit(solution)/shard_map/ppermute | solution.py:234
  80.8 31.4 %collective-permute-start.15 = (f32[2,64,512]{2,1,0:T(8,128)S(1)}, f32[2,64,512]{2,1,0:T(8,128)S(1)}, u32[]{:S(2)}, u32[]{:S(2)}) collective-permute-start(f32[2,64,512]{2,1,0:T(8,128)S(1)} %copy-done.22), channel_id=1, source_target_pairs={{0,4},{1,5},{2,6},{3,7},{4,0},{5,1},{6,2},{7,3},{8,12},{9,13},{10,... | collective-permute-start | bytes 786440 | tf_op jit(solution)/shard_map/ppermute | solution.py:234
  82.3 29.9 %collective-permute-start.16 = (f32[2,64,512]{2,1,0:T(8,128)S(1)}, f32[2,64,512]{2,1,0:T(8,128)S(1)}, u32[]{:S(2)}, u32[]{:S(2)}) collective-permute-start(f32[2,64,512]{2,1,0:T(8,128)S(1)} %copy-done.21), channel_id=1, source_target_pairs={{0,5},{1,4},{2,7},{3,6},{4,1},{5,0},{6,3},{7,2},{8,13},{9,12},{10,... | collective-permute-start | bytes 786440 | tf_op jit(solution)/shard_map/ppermute | solution.py:234
  82.6 37.8 %collective-permute-start.17 = (f32[2,64,512]{2,1,0:T(8,128)S(1)}, f32[2,64,512]{2,1,0:T(8,128)S(1)}, u32[]{:S(2)}, u32[]{:S(2)}) collective-permute-start(f32[2,64,512]{2,1,0:T(8,128)S(1)} %copy-done.20), channel_id=1, source_target_pairs={{0,6},{1,7},{2,4},{3,5},{4,2},{5,3},{6,0},{7,1},{8,14},{9,15},{10,... | collective-permute-start | bytes 786440 | tf_op jit(solution)/shard_map/ppermute | solution.py:234
  105.5 22.3 %collective-permute-start.18 = (f32[2,64,512]{2,1,0:T(8,128)S(1)}, f32[2,64,512]{2,1,0:T(8,128)S(1)}, u32[]{:S(2)}, u32[]{:S(2)}) collective-permute-start(f32[2,64,512]{2,1,0:T(8,128)S(1)} %copy-done.19), channel_id=1, source_target_pairs={{0,7},{1,6},{2,5},{3,4},{4,3},{5,2},{6,1},{7,0},{8,15},{9,14},{10,... | collective-permute-start | bytes 786440 | tf_op jit(solution)/shard_map/ppermute | solution.py:234
  130.5 62.2 %all-to-all-start.1 = ((f32[32,2,64,128]{3,2,1,0:T(8,128)}), f32[32,2,64,128]{3,2,1,0:T(8,128)S(1)}, u32[]{:S(2)}, u32[]{:S(2)}) async-start(f32[32,2,64,128]{3,2,1,0:T(8,128)} %bitcast.16), calls=%async_computation.1 | async-start | bytes 4194304 | tf_op jit(solution)/shard_map/all_to_all | solution.py:348
  (20 other events, 54.0 us)
where the time goes:
time: 208 us
  waiting for transfers between devices  94.8 us (46%)
  starting transfers between devices  43.6 us (21%)
  Pallas kernels  43.2 us (21%)
  local copies, waits for them, and re-layouts  23.3 us (11%)
  other arithmetic  2.57 us (1%)
    ppermute x19, waiting for transfers between devices, exchange(): lax.ppermute(array, axis, [(i, i ^ distance) for i in range(lax.axis_size...  66.1 us
    all_to_all x2, waiting for transfers between devices, on_device(): lax.all_to_all(result, ('freq', 'rcv'), split_axis=0, concat_axis=0, tile...  28.7 us
    ppermute x19, starting transfers between devices, exchange(): lax.ppermute(array, axis, [(i, i ^ distance) for i in range(lax.axis_size...  24.6 us
    unnamed x46, local copies, waits for them, and re-layouts  22.6 us
    pallas_call x2, Pallas kernels, synthesis(): pl.pallas_call(functools.partial(synthesis_kernel, receiver_tile=receiver...  21.8 us
    all_to_all x2, starting transfers between devices, on_device(): lax.all_to_all(result, ('freq', 'rcv'), split_axis=0, concat_axis=0, tile...  19 us
    pallas_call x2, Pallas kernels, on_device(): pl.pallas_call(functools.partial(multiples_kernel, first_slot=part * rcv_...  14.3 us
    pallas_call x2, Pallas kernels, gather(): pl.pallas_call(functools.partial(pack_kernel, first_slot=part * rcv_count...  4.62 us
  transfers between devices with their start and end apart: 21, of which 11 were waited for; matrix products, arithmetic and copies ran while one was open for 1% of the time, Pallas kernels for 16%

commit v1 on v0

--- a/solution.py
+++ b/solution.py
@@ -70,11 +70,12 @@
 def pack_kernel(spectra_ref, *refs, first_slot):
     outs, (stage, in_sems, out_sems) = refs[:-3], refs[-3:]
     rank = lax.axis_index("rcv")
-    loads = [
-        pltpu.make_async_copy(spectra_ref.at[first_slot + (rank ^ (n + 1))], stage.at[n], in_sems.at[n])
-        for n in range(len(outs))
-    ]
-    stores = [pltpu.make_async_copy(stage.at[n], out, out_sems.at[n]) for n, out in enumerate(outs)]
+    loads, stores = [], []
+    for n in range(stage.shape[0]):
+        slot = n if len(outs) == 1 else rank ^ (n + 1)
+        out = outs[0].at[n] if len(outs) == 1 else outs[n]
+        loads.append(pltpu.make_async_copy(spectra_ref.at[first_slot + slot], stage.at[n], in_sems.at[n]))
+        stores.append(pltpu.make_async_copy(stage.at[n], out, out_sems.at[n]))
     for load in loads:
         load.start()
     for load, store in zip(loads, stores):
@@ -111,7 +112,11 @@
 
     @pl.when(live)
     def _():
-        sources = [spectra_ref.at[first_slot + rank]] + list(tiles)
+        if len(tiles) == 1:
+            sources, origins = [tiles[0].at[n] for n in range(receiver_tiles)], range(receiver_tiles)
+        else:
+            sources = [spectra_ref.at[first_slot + rank]] + list(tiles)
+            origins = [rank ^ n for n in range(receiver_tiles)]
         copies = [pltpu.make_async_copy(source, data.at[n], tile_sems.at[n]) for n, source in enumerate(sources)]
         for copy in copies:
             copy.start()
@@ -119,11 +124,13 @@
         gain_copy.start()
         for n, copy in enumerate(copies):
             copy.wait()
-            first_row = (rank ^ n) * receiver_tile
+            first_row = origins[n] * receiver_tile
             real, imag = split(data[n, 0]), split(data[n, 1])
             for place, part in ((0, 0), (1, 1), (2, 0)):
-                top = pl.ds(pl.multiple_of(first_row + place * 2 * side, receiver_tile), receiver_tile)
-                low = pl.ds(pl.multiple_of(first_row + (place * 2 + 1) * side, receiver_tile), receiver_tile)
+                top, low = (
+                    pl.ds(pl.multiple_of(first_row + at * side, receiver_tile), receiver_tile)
+                    for at in (2 * place, 2 * place + 1)
+                )
                 w[top, :side] = real[part]
                 w[top, side:] = imag[part]
                 w[low, :side] = -imag[part]
@@ -246,28 +253,30 @@
     hbm = whole_in(pltpu.HBM)
     smem = whole_in(pltpu.SMEM)
 
-    def gather(part, slots):
-        tile = pltpu.HBM(spectra.shape[1:], spectra.dtype)
-        packed = pl.pallas_call(
+    def in_hbm(array):
+        return pltpu.with_memory_space_constraint(array, pltpu.HBM)
+
+    def pack(part, slots, count, shape):
+        return pl.pallas_call(
             functools.partial(pack_kernel, first_slot=part * rcv_count),
-            out_shape=[tile] * (rcv_count - 1),
+            out_shape=[pltpu.HBM(shape, spectra.dtype)] * count,
             in_specs=[hbm],
-            out_specs=[hbm] * (rcv_count - 1),
+            out_specs=[hbm] * count,
             scratch_shapes=[
-                pltpu.VMEM((rcv_count - 1,) + spectra.shape[1:], spectra.dtype),
-                pltpu.SemaphoreType.DMA((rcv_count - 1,)),
-                pltpu.SemaphoreType.DMA((rcv_count - 1,)),
+                pltpu.VMEM((rcv_count if count == 1 else count,) + spectra.shape[1:], spectra.dtype),
+                pltpu.SemaphoreType.DMA((rcv_count,)),
+                pltpu.SemaphoreType.DMA((rcv_count,)),
             ],
+            compiler_params=params(8),
             name="pack",
-        )(slots)
-        return packed, [exchange(tile, "rcv", n + 1) for n, tile in enumerate(packed)]
+        )(in_hbm(slots))
 
     def synthesis(coefs, table, base):
         depth = table.shape[0]
         block = pl.BlockSpec((source_tile, ROWS, samples), lambda n: (0, n, 0))
         return pl.pallas_call(
             functools.partial(synthesis_kernel, receiver_tile=receiver_tile),
-            out_shape=jax.ShapeDtypeStruct(recorded.shape, jnp.float32),
+            out_shape=pltpu.HBM(recorded.shape, jnp.float32),
             grid=(receiver_tile // ROWS,),
             in_specs=[whole_in(), block] + [hbm] * len(coefs),
             out_specs=block,
@@ -279,12 +288,13 @@
             ],
             compiler_params=params(24),
             name="synthesis",
-        )(table, base, *coefs)
+        )(table, in_hbm(base), *coefs)
 
     def doubled(array, axis, distance):
         return jnp.concatenate([array, exchange(array, axis, distance)])
 
-    _, first_tiles = gather(0, spectra)
+    packed = pack(0, spectra, 1, (rcv_count,) + spectra.shape[1:])[0]
+    gathered = [[lax.all_to_all(packed, "rcv", split_axis=0, concat_axis=0, tiled=True)]]
     line = gain_index.T[None]
     distance = 1
     while distance < freq_count:
@@ -306,20 +316,19 @@
         name="gains",
     )(gain_table, near, far, column)
 
-    gathered = [first_tiles]
     slots = spectra
     for part in range(1, parts):
-        slots, *gathered[-1] = lax.optimization_barrier((slots, *gathered[-1]))
-        packed, tiles = gather(part, slots)
-        gathered[-1][0], _ = lax.optimization_barrier((gathered[-1][0], packed[0]))
-        gathered.append(tiles)
+        slots, gathered[-1][0] = lax.optimization_barrier((slots, gathered[-1][0]))
+        packed = pack(part, slots, rcv_count - 1, spectra.shape[1:])
+        gathered[-1][0], *packed = lax.optimization_barrier((gathered[-1][0], *packed))
+        gathered.append([exchange(tile, "rcv", n + 1) for n, tile in enumerate(packed)])
 
     results = []
     for part in range(parts):
         result = pl.pallas_call(
             functools.partial(multiples_kernel, first_slot=part * rcv_count),
             out_shape=pltpu.HBM((freq_count, rcv_count, 2, receiver_tile, source_tile), jnp.float32),
-            in_specs=[smem, whole_in(), whole_in()] + [hbm] * (1 + rcv_count),
+            in_specs=[smem, whole_in(), whole_in()] + [hbm] * (2 + len(gathered[part])),
             out_specs=hbm,
             scratch_shapes=[
                 pltpu.VMEM((freq_count, rcv_count, 2, receiver_tile, source_tile), jnp.float32),
@@ -333,11 +342,12 @@
                 pltpu.SemaphoreType.DMA,
                 pltpu.SemaphoreType.DMA((freq_count, rcv_count)),
             ],
-            compiler_params=params(48),
+            compiler_params=params(32),
             name="multiples",
-        )(counts, column, row, spectra, gains, *gathered[part])
+        )(counts, column, row, in_hbm(spectra), gains, *gathered[part])
         if part < parts - 1:
-            gathered[part + 1][0], result = lax.optimization_barrier((gathered[part + 1][0], result))
+            nearest = slice(1, 5)
+            result, *gathered[part + 1][nearest] = lax.optimization_barrier((result, *gathered[part + 1][nearest]))
         results.append(result.reshape((senders,) + result.shape[2:]))
 
     before = jnp.arange(freq_count)[None, :] < jnp.arange(freq_count)[:, None]

time: 208 us -> 187 us (0.90)
  local copies, waits for them, and re-layouts: 23.3 us -> 0.75 us
  starting transfers between devices: 43.6 us -> 27.2 us
  Pallas kernels: 43.2 us -> 54.1 us
  waiting for transfers between devices: 94.8 us -> 103 us
    unnamed x46 -> x16, local copies, waits for them, and re-layouts: 22.6 us -> 0.05 us
    all_to_all x2, waiting for transfers between devices: 28.7 us -> 41.4 us  [on_device(): lax.all_to_all(result, ('freq', 'rcv'), split_axis=0, concat_axis=0, tile...]
    pallas_call x2, Pallas kernels: 21.8 us -> 32.8 us  [synthesis(): pl.pallas_call(functools.partial(synthesis_kernel, receiver_tile=receiver...]
    all_to_all x2, starting transfers between devices: 19 us -> 8.01 us  [on_device(): lax.all_to_all(result, ('freq', 'rcv'), split_axis=0, concat_axis=0, tile...]
    ppermute x19 -> x12, starting transfers between devices: 24.6 us -> 14 us  [exchange(): lax.ppermute(array, axis, [(i, i ^ distance) for i in range(lax.axis_size...]
    all_to_all x0 -> x1, starting transfers between devices: none -> 5.18 us  [on_device(): lax.all_to_all(packed, 'rcv', split_axis=0, concat_axis=0, tiled=True)]
    ppermute x19 -> x12, waiting for transfers between devices: 66.1 us -> 61.5 us  [exchange(): lax.ppermute(array, axis, [(i, i ^ distance) for i in range(lax.axis_size...]
  transfers between devices with their start and end apart: 21 -> 15, of which waited for: 11 -> 8; matrix products, arithmetic and copies ran while one was open for 1% -> 1% of each run, Pallas kernels for 16% -> 19%
where the time goes in v1:
time: 187 us; the launch traced here: 186 us
  waiting for transfers between devices  103 us (55%)
  Pallas kernels  54.1 us (29%)
  starting transfers between devices  27.2 us (15%)
    ppermute x12, waiting for transfers between devices, exchange(): lax.ppermute(array, axis, [(i, i ^ distance) for i in range(lax.axis_size...  61.5 us
    all_to_all x2, waiting for transfers between devices, on_device(): lax.all_to_all(result, ('freq', 'rcv'), split_axis=0, concat_axis=0, tile...  41.4 us
    pallas_call x2, Pallas kernels, synthesis(): pl.pallas_call(functools.partial(synthesis_kernel, receiver_tile=receiver...  32.8 us
    ppermute x12, starting transfers between devices, exchange(): lax.ppermute(array, axis, [(i, i ^ distance) for i in range(lax.axis_size...  14 us
    pallas_call x2, Pallas kernels, on_device(): pl.pallas_call(functools.partial(multiples_kernel, first_slot=part * rcv_...  13.3 us
    all_to_all x2, starting transfers between devices, on_device(): lax.all_to_all(result, ('freq', 'rcv'), split_axis=0, concat_axis=0, tile...  8.01 us
    pallas_call x2, Pallas kernels, pack(): pl.pallas_call(functools.partial(pack_kernel, first_slot=part * rcv_count...  5.54 us
    all_to_all x1, starting transfers between devices, on_device(): lax.all_to_all(packed, 'rcv', split_axis=0, concat_axis=0, tiled=True)  5.18 us
  transfers between devices with their start and end apart: 15, of which 8 were waited for; matrix products, arithmetic and copies ran while one was open for 1% of the time, Pallas kernels for 19%

profile of v1, /device:TPU:0, one launch (start us, length us, event | category | flops | bytes accessed | tf_op | source)
XLA Modules:
  0.0 186.4 jit_solution(3269779121095116294)
XLA Ops:
  0.0 2.4 %pack.2 = f32[8,2,64,512]{3,2,1,0:T(8,128)} custom-call(f32[16,2,64,512]{3,2,1,0:T(8,128)} %spectra_ref.6), custom_call_target="tpu_custom_call" | custom-call | tf_op jit(solution)/shard_map/pack/pallas_call | solution.py:260
  2.4 5.2 %all-to-all-start = ((f32[8,2,64,512]{3,2,1,0:T(8,128)}), f32[8,2,64,512]{3,2,1,0:T(8,128)S(1)}, u32[]{:S(2)}, u32[]{:S(2)}) async-start(f32[8,2,64,512]{3,2,1,0:T(8,128)} %pack.2), calls=%async_computation | async-start | bytes 4194304 | tf_op jit(solution)/shard_map/all_to_all | solution.py:297
  7.6 1.6 collective-permute-start
  9.2 2.3 %collective-permute-done = s32[1,64,128]{2,1,0:T(8,128)S(1)} collective-permute-done((s32[1,64,128]{2,1,0:T(8,128)S(1)}, s32[1,64,128]{2,1,0:T(8,128)S(1)}, u32[]{:S(2)}, u32[]{:S(2)}) %collective-permute-start) | collective-permute-done | bytes 32800 | tf_op jit(solution)/shard_map/ppermute | solution.py:241
  11.6 2.6 %collective-permute-start.1 = (s32[2,64,128]{2,1,0:T(8,128)S(1)}, s32[2,64,128]{2,1,0:T(8,128)S(1)}, u32[]{:S(2)}, u32[]{:S(2)}) collective-permute-start(s32[2,64,128]{2,1,0:T(8,128)S(1)} %pad_add_fusion.2), channel_id=1, source_target_pairs={{0,16},{8,24},{16,0},{24,8},{1,17},{9,25},{17,1},{25,9},{2,18},{10... | collective-permute-start | bytes 196616 | tf_op jit(solution)/shard_map/ppermute | solution.py:241
  14.2 2.9 %collective-permute-done.1 = s32[2,64,128]{2,1,0:T(8,128)S(1)} collective-permute-done((s32[2,64,128]{2,1,0:T(8,128)S(1)}, s32[2,64,128]{2,1,0:T(8,128)S(1)}, u32[]{:S(2)}, u32[]{:S(2)}) %collective-permute-start.1) | collective-permute-done | bytes 65568 | tf_op jit(solution)/shard_map/ppermute | solution.py:241
  17.1 1.7 collective-permute-start.2
  18.8 17.3 %collective-permute-done.2 = s32[1,4,64,128]{3,2,1,0:T(8,128)S(1)} collective-permute-done((s32[1,4,64,128]{3,2,1,0:T(8,128)S(1)}, s32[1,4,64,128]{3,2,1,0:T(8,128)S(1)}, u32[]{:S(2)}, u32[]{:S(2)}) %collective-permute-start.2) | collective-permute-done | bytes 131104 | tf_op jit(solution)/shard_map/ppermute | solution.py:241
  36.2 1.5 collective-permute-start.3
  37.7 6.4 %collective-permute-done.3 = s32[2,4,64,128]{3,2,1,0:T(8,128)S(1)} collective-permute-done((s32[2,4,64,128]{3,2,1,0:T(8,128)S(1)}, s32[2,4,64,128]{3,2,1,0:T(8,128)S(1)}, u32[]{:S(2)}, u32[]{:S(2)}) %collective-permute-start.3) | collective-permute-done | bytes 262176 | tf_op jit(solution)/shard_map/ppermute | solution.py:241
  44.3 3.2 %pack.3 = (f32[2,64,512]{2,1,0:T(8,128)}, f32[2,64,512]{2,1,0:T(8,128)}, f32[2,64,512]{2,1,0:T(8,128)}, f32[2,64,512]{2,1,0:T(8,128)}, f32[2,64,512]{2,1,0:T(8,1...) custom-call(f32[16,2,64,512]{3,2,1,0:T(8,128)} %spectra_ref.6), custom_call_target="tpu_custom_call" | custom-call | tf_op jit(solution)/shard_map/pack/pallas_call | solution.py:260
  49.3 1.5 collective-permute-start.7
  51.2 2.5 %gains.1.gains_hbm = f32[2,512,512]{2,1,0:T(8,128)S(1)} custom-call(f32[2,16]{1,0:T(2,128)S(1)} %copy-done.4, s32[4,4,64,128]{3,2,1,0:T(8,128)S(1)} %pad_add_fusion.near_ref, s32[4,4,64,128]{3,2,1,0:T(8,128)S(1)} %collective-permute-done.4.far_ref, s32[512,1]{1,0:T(8,128)S(1)} %copy.16.column_ref), custom_call_target="tpu_custom_call" | custom-call | tf_op jit(solution)/shard_map/gains/pallas_call | solution.py:309
  53.7 10.8 %multiples.2 = f32[4,8,2,64,128]{4,3,2,1,0:T(8,128)} custom-call(s32[4]{0:T(128)S(1)} %copy-done.3, s32[512,1]{1,0:T(8,128)S(1)} %copy.16.column_ref, s32[1,512]{1,0:T(1,128)S(1)} %bitcast.13, f32[16,2,64,512]{3,2,1,0:T(8,128)} %spectra_ref.6, f32[2,512,512]{2,1,0:T(8,128)S(1)} %gains.1.gains_hbm, f32[8,2,64,512]{3,2,1,0:T(8,128)S(1)} %copy-done.1), custom_call_target="tpu_custom_call" | custom-call | tf_op jit(solution)/shard_map/multiples/pallas_call | solution.py:328
  64.6 4.3 %all-to-all-start.1 = ((f32[32,2,64,128]{3,2,1,0:T(8,128)}), f32[32,2,64,128]{3,2,1,0:T(8,128)}, u32[]{:S(2)}, u32[]{:S(2)}) async-start(f32[32,2,64,128]{3,2,1,0:T(8,128)} %bitcast.15), calls=%async_computation.1 | async-start | bytes 4194304 | tf_op jit(solution)/shard_map/all_to_all | solution.py:358
  69.1 2.6 %collective-permute-start.10 = (f32[2,64,512]{2,1,0:T(8,128)S(1)}, f32[2,64,512]{2,1,0:T(8,128)S(1)}, u32[]{:S(2)}, u32[]{:S(2)}) collective-permute-start(f32[2,64,512]{2,1,0:T(8,128)S(1)} %copy-done.7), channel_id=1, source_target_pairs={{0,6},{1,7},{2,4},{3,5},{4,2},{5,3},{6,0},{7,1},{8,14},{9,15},{10,... | collective-permute-start | bytes 786440 | tf_op jit(solution)/shard_map/ppermute | solution.py:241
  71.7 26.5 %collective-permute-done.10.refs_5_ = f32[2,64,512]{2,1,0:T(8,128)S(1)} collective-permute-done((f32[2,64,512]{2,1,0:T(8,128)S(1)}, f32[2,64,512]{2,1,0:T(8,128)S(1)}, u32[]{:S(2)}, u32[]{:S(2)}) %collective-permute-start.10) | collective-permute-done | bytes 262176 | tf_op jit(solution)/shard_map/ppermute | solution.py:241
  98.2 6.0 %collective-permute-done.11.refs_6_ = f32[2,64,512]{2,1,0:T(8,128)S(1)} collective-permute-done((f32[2,64,512]{2,1,0:T(8,128)S(1)}, f32[2,64,512]{2,1,0:T(8,128)S(1)}, u32[]{:S(2)}, u32[]{:S(2)}) %collective-permute-start.11) | collective-permute-done | bytes 262176 | tf_op jit(solution)/shard_map/ppermute | solution.py:241
  104.2 2.5 %multiples.3 = f32[4,8,2,64,128]{4,3,2,1,0:T(8,128)} custom-call(s32[4]{0:T(128)S(1)} %copy-done.3, s32[512,1]{1,0:T(8,128)S(1)} %copy.16.column_ref, s32[1,512]{1,0:T(1,128)S(1)} %bitcast.14, f32[16,2,64,512]{3,2,1,0:T(8,128)} %spectra_ref.6, f32[2,512,512]{2,1,0:T(8,128)S(1)} %gains.1.gains_hbm, f32[2,64,512]{2,1,0:T(8,128)S(1)} %collective-permute-done.9.refs_0_, ...), custom_call_target="tpu_custom_call" | custom-call | tf_op jit(solution)/shard_map/multiples/pallas_call | solution.py:328
  106.8 11.3 %all-to-all-done.1 = f32[32,2,64,128]{3,2,1,0:T(8,128)} async-done(((f32[32,2,64,128]{3,2,1,0:T(8,128)}), f32[32,2,64,128]{3,2,1,0:T(8,128)}, u32[]{:S(2)}, u32[]{:S(2)}) %all-to-all-start.1) | async-done | bytes 2097184 | tf_op jit(solution)/shard_map/all_to_all | solution.py:358
  118.1 3.7 %all-to-all-start.2 = ((f32[32,2,64,128]{3,2,1,0:T(8,128)}), f32[32,2,64,128]{3,2,1,0:T(8,128)S(1)}, u32[]{:S(2)}, u32[]{:S(2)}) async-start(f32[32,2,64,128]{3,2,1,0:T(8,128)} %bitcast.16), calls=%async_computation.2 | async-start | bytes 4194304 | tf_op jit(solution)/shard_map/all_to_all | solution.py:358
  123.4 17.2 %synthesis.2.base_ref = f32[128,64,512]{2,1,0:T(8,128)} custom-call(f32[64,512]{1,0:T(8,128)S(1)} %reshape.251.table_ref, f32[128,64,512]{2,1,0:T(8,128)} %base_ref.1, f32[4096,128]{1,0:T(8,128)} %bitcast.8.refs_0_), custom_call_target="tpu_custom_call" | custom-call | tf_op jit(solution)/shard_map/synthesis/pallas_call | solution.py:277
  140.5 30.1 %all-to-all-done.2 = f32[32,2,64,128]{3,2,1,0:T(8,128)S(1)} async-done(((f32[32,2,64,128]{3,2,1,0:T(8,128)}), f32[32,2,64,128]{3,2,1,0:T(8,128)S(1)}, u32[]{:S(2)}, u32[]{:S(2)}) %all-to-all-start.2) | async-done | bytes 2097184 | tf_op jit(solution)/shard_map/all_to_all | solution.py:358
  170.7 15.6 %synthesis.3 = f32[128,64,512]{2,1,0:T(8,128)} custom-call(f32[64,512]{1,0:T(8,128)S(1)} %reshape.250.table_ref, f32[128,64,512]{2,1,0:T(8,128)} %synthesis.2.base_ref, f32[4096,128]{1,0:T(8,128)S(1)} %bitcast.11), custom_call_target="tpu_custom_call" | custom-call | tf_op jit(solution)/shard_map/synthesis/pallas_call | solution.py:277
  (48 shorter events, 4.2 us)
Async XLA Ops:
  2.4 5.2 %copy-start.5 = (s32[128,64]{0,1:T(8,128)S(1)}, s32[128,64]{0,1:T(8,128)}, u32[]{:S(2)}) copy-start(s32[128,64]{0,1:T(8,128)} %param.10) | copy-start | bytes 98308
  2.4 41.8 %all-to-all-start = ((f32[8,2,64,512]{3,2,1,0:T(8,128)}), f32[8,2,64,512]{3,2,1,0:T(8,128)S(1)}, u32[]{:S(2)}, u32[]{:S(2)}) async-start(f32[8,2,64,512]{3,2,1,0:T(8,128)} %pack.2), calls=%async_computation | async-start | bytes 4194304 | tf_op jit(solution)/shard_map/all_to_all | solution.py:297
  7.6 4.0 %collective-permute-start = (s32[1,64,128]{2,1,0:T(8,128)S(1)}, s32[1,64,128]{2,1,0:T(8,128)S(1)}, u32[]{:S(2)}, u32[]{:S(2)}) collective-permute-start(s32[1,64,128]{2,1,0:T(8,128)S(1)} %bitcast.17), channel_id=1, source_target_pairs={{0,8},{8,0},{16,24},{24,16},{1,9},{9,1},{17,25},{25,17},{2,10},{10... | collective-permute-start | bytes 98312 | tf_op jit(solution)/shard_map/ppermute | solution.py:241
  11.6 5.5 %collective-permute-start.1 = (s32[2,64,128]{2,1,0:T(8,128)S(1)}, s32[2,64,128]{2,1,0:T(8,128)S(1)}, u32[]{:S(2)}, u32[]{:S(2)}) collective-permute-start(s32[2,64,128]{2,1,0:T(8,128)S(1)} %pad_add_fusion.2), channel_id=1, source_target_pairs={{0,16},{8,24},{16,0},{24,8},{1,17},{9,25},{17,1},{25,9},{2,18},{10... | collective-permute-start | bytes 196616 | tf_op jit(solution)/shard_map/ppermute | solution.py:241
  17.1 19.0 %collective-permute-start.2 = (s32[1,4,64,128]{3,2,1,0:T(8,128)S(1)}, s32[1,4,64,128]{3,2,1,0:T(8,128)S(1)}, u32[]{:S(2)}, u32[]{:S(2)}) collective-permute-start(s32[1,4,64,128]{3,2,1,0:T(8,128)S(1)} %add_bitcast_fusion), channel_id=1, source_target_pairs={{0,2},{1,3},{2,0},{3,1},{4,6},{5,7},{6,4},{7,5},{8,10},{9,11},{10,... | collective-permute-start | bytes 393224 | tf_op jit(solution)/shard_map/ppermute | solution.py:241
  36.2 7.9 %collective-permute-start.3 = (s32[2,4,64,128]{3,2,1,0:T(8,128)S(1)}, s32[2,4,64,128]{3,2,1,0:T(8,128)S(1)}, u32[]{:S(2)}, u32[]{:S(2)}) collective-permute-start(s32[2,4,64,128]{3,2,1,0:T(8,128)S(1)} %pad_add_fusion.1), channel_id=1, source_target_pairs={{0,4},{1,5},{2,6},{3,7},{4,0},{5,1},{6,2},{7,3},{8,12},{9,13},{10,... | collective-permute-start | bytes 786440 | tf_op jit(solution)/shard_map/ppermute | solution.py:241
  44.1 6.9 %copy-start.2 = (s32[512]{0:T(512)S(1)}, s32[512]{0:T(512)}, u32[]{:S(2)}) copy-start(s32[512]{0:T(512)} %param.8) | copy-start | bytes 6148
  44.1 7.0 %copy-start.4 = (f32[2,16]{1,0:T(2,128)S(1)}, f32[2,16]{1,0:T(2,128)}, u32[]{:S(2)}) copy-start(f32[2,16]{1,0:T(2,128)} %table_ref.1) | copy-start | bytes 388
  44.2 7.0 %collective-permute-start.4 = (s32[4,4,64,128]{3,2,1,0:T(8,128)S(1)}, s32[4,4,64,128]{3,2,1,0:T(8,128)S(1)}, u32[]{:S(2)}, u32[]{:S(2)}) collective-permute-start(s32[4,4,64,128]{3,2,1,0:T(8,128)S(1)} %pad_add_fusion.near_ref), channel_id=1, source_target_pairs={{0,1},{1,0},{2,3},{3,2},{4,5},{5,4},{6,7},{7,6},{8,9},{9,8},{10,11... | collective-permute-start | bytes 1572872 | tf_op jit(solution)/shard_map/ppermute | solution.py:241
  44.2 3.2 %copy-start = (f32[8,2,64,512]{3,2,1,0:T(8,128)}, f32[8,2,64,512]{3,2,1,0:T(8,128)S(1)}, u32[]{:S(2)}) copy-start(f32[8,2,64,512]{3,2,1,0:T(8,128)S(1)} %all-to-all-done.refs_0_) | copy-start | bytes 6291460
  47.4 6.3 %copy-start.3 = (s32[4]{0:T(128)S(1)}, s32[4]{0:T(128)}, u32[]{:S(2)}) copy-start(s32[4]{0:T(128)} %counts_ref.3) | copy-start | bytes 52
  47.4 17.1 %collective-permute-start.5 = (f32[2,64,512]{2,1,0:T(8,128)}, f32[2,64,512]{2,1,0:T(8,128)}, u32[]{:S(2)}, u32[]{:S(2)}) collective-permute-start(f32[2,64,512]{2,1,0:T(8,128)} %get-tuple-element.38), channel_id=1, source_target_pairs={{0,2},{1,3},{2,0},{3,1},{4,6},{5,7},{6,4},{7,5},{8,10},{9,11},{10,... | collective-permute-start | bytes 786440 | tf_op jit(solution)/shard_map/ppermute | solution.py:241
  48.2 16.3 %collective-permute-start.6 = (f32[2,64,512]{2,1,0:T(8,128)}, f32[2,64,512]{2,1,0:T(8,128)}, u32[]{:S(2)}, u32[]{:S(2)}) collective-permute-start(f32[2,64,512]{2,1,0:T(8,128)} %get-tuple-element.39), channel_id=1, source_target_pairs={{0,3},{1,2},{2,1},{3,0},{4,7},{5,6},{6,5},{7,4},{8,11},{9,10},{10,... | collective-permute-start | bytes 786440 | tf_op jit(solution)/shard_map/ppermute | solution.py:241
  49.3 15.2 %collective-permute-start.7 = (f32[2,64,512]{2,1,0:T(8,128)}, f32[2,64,512]{2,1,0:T(8,128)}, u32[]{:S(2)}, u32[]{:S(2)}) collective-permute-start(f32[2,64,512]{2,1,0:T(8,128)} %get-tuple-element.40), channel_id=1, source_target_pairs={{0,4},{1,5},{2,6},{3,7},{4,0},{5,1},{6,2},{7,3},{8,12},{9,13},{10,... | collective-permute-start | bytes 786440 | tf_op jit(solution)/shard_map/ppermute | solution.py:241
  50.8 13.7 %collective-permute-start.8 = (f32[2,64,512]{2,1,0:T(8,128)}, f32[2,64,512]{2,1,0:T(8,128)}, u32[]{:S(2)}, u32[]{:S(2)}) collective-permute-start(f32[2,64,512]{2,1,0:T(8,128)} %get-tuple-element.41), channel_id=1, source_target_pairs={{0,5},{1,4},{2,7},{3,6},{4,1},{5,0},{6,3},{7,2},{8,13},{9,12},{10,... | collective-permute-start | bytes 786440 | tf_op jit(solution)/shard_map/ppermute | solution.py:241
  51.1 2.6 %copy-start.1 = (f32[8,2,64,512]{3,2,1,0:T(8,128)S(1)}, f32[8,2,64,512]{3,2,1,0:T(8,128)}, u32[]{:S(2)}) copy-start(f32[8,2,64,512]{3,2,1,0:T(8,128)} %copy-done) | copy-start | bytes 6291460
  64.5 4.6 %copy-start.7 = (f32[2,64,512]{2,1,0:T(8,128)S(1)}, f32[2,64,512]{2,1,0:T(8,128)}, u32[]{:S(2)}) copy-start(f32[2,64,512]{2,1,0:T(8,128)} %get-tuple-element.48) | copy-start | bytes 786436
  64.5 7.2 %copy-start.6 = (f32[2,64,512]{2,1,0:T(8,128)S(1)}, f32[2,64,512]{2,1,0:T(8,128)}, u32[]{:S(2)}) copy-start(f32[2,64,512]{2,1,0:T(8,128)} %get-tuple-element.49) | copy-start | bytes 786436
  64.6 53.5 %all-to-all-start.1 = ((f32[32,2,64,128]{3,2,1,0:T(8,128)}), f32[32,2,64,128]{3,2,1,0:T(8,128)}, u32[]{:S(2)}, u32[]{:S(2)}) async-start(f32[32,2,64,128]{3,2,1,0:T(8,128)} %bitcast.15), calls=%async_computation.1 | async-start | bytes 4194304 | tf_op jit(solution)/shard_map/all_to_all | solution.py:358
  68.9 2.9 %collective-permute-start.9 = (f32[2,64,512]{2,1,0:T(8,128)}, f32[2,64,512]{2,1,0:T(8,128)S(1)}, u32[]{:S(2)}, u32[]{:S(2)}) collective-permute-start(f32[2,64,512]{2,1,0:T(8,128)} %get-tuple-element.43), channel_id=1, source_target_pairs={{0,1},{1,0},{2,3},{3,2},{4,5},{5,4},{6,7},{7,6},{8,9},{9,8},{10,11... | collective-permute-start | bytes 786440 | tf_op jit(solution)/shard_map/ppermute | solution.py:241
  69.1 29.1 %collective-permute-start.10 = (f32[2,64,512]{2,1,0:T(8,128)S(1)}, f32[2,64,512]{2,1,0:T(8,128)S(1)}, u32[]{:S(2)}, u32[]{:S(2)}) collective-permute-start(f32[2,64,512]{2,1,0:T(8,128)S(1)} %copy-done.7), channel_id=1, source_target_pairs={{0,6},{1,7},{2,4},{3,5},{4,2},{5,3},{6,0},{7,1},{8,14},{9,15},{10,... | collective-permute-start | bytes 786440 | tf_op jit(solution)/shard_map/ppermute | solution.py:241
  71.7 32.5 %collective-permute-start.11 = (f32[2,64,512]{2,1,0:T(8,128)S(1)}, f32[2,64,512]{2,1,0:T(8,128)S(1)}, u32[]{:S(2)}, u32[]{:S(2)}) collective-permute-start(f32[2,64,512]{2,1,0:T(8,128)S(1)} %copy-done.6), channel_id=1, source_target_pairs={{0,7},{1,6},{2,5},{3,4},{4,3},{5,2},{6,1},{7,0},{8,15},{9,14},{10,... | collective-permute-start | bytes 786440 | tf_op jit(solution)/shard_map/ppermute | solution.py:241
  118.1 52.6 %all-to-all-start.2 = ((f32[32,2,64,128]{3,2,1,0:T(8,128)}), f32[32,2,64,128]{3,2,1,0:T(8,128)S(1)}, u32[]{:S(2)}, u32[]{:S(2)}) async-start(f32[32,2,64,128]{3,2,1,0:T(8,128)} %bitcast.16), calls=%async_computation.2 | async-start | bytes 4194304 | tf_op jit(solution)/shard_map/all_to_all | solution.py:358

commit v2 on v1

--- a/solution.py
+++ b/solution.py
@@ -43,10 +43,10 @@
     side = source_tiles * source_tile
     receiver_tiles = side // receiver_tile
     for half, ref in enumerate((near_ref, far_ref)):
-        for h in range(ref.shape[0]):
+        for h in range(ref.shape[1]):
             for e in range(source_tiles):
                 tile = (lax.axis_index("freq") ^ e) * receiver_tiles + (lax.axis_index("rcv") ^ (2 * h + half))
-                tiles_ref[tile] = ref[h, e].astype(jnp.float32)
+                tiles_ref[tile] = ref[e, h].astype(jnp.float32)
     pick = min(PICK, side)
     for start in range(0, side, pick):
         rows = slice(start, start + pick)
@@ -290,21 +290,15 @@
             name="synthesis",
         )(table, in_hbm(base), *coefs)
 
-    def doubled(array, axis, distance):
-        return jnp.concatenate([array, exchange(array, axis, distance)])
-
+    tile = gain_index.T
+    near = jnp.stack([tile if n == 0 else exchange(tile, "rcv", 2 * n) for n in range(rcv_count // 2)])
     packed = pack(0, spectra, 1, (rcv_count,) + spectra.shape[1:])[0]
+    packed, near = lax.optimization_barrier((packed, near))
     gathered = [[lax.all_to_all(packed, "rcv", split_axis=0, concat_axis=0, tiled=True)]]
-    line = gain_index.T[None]
-    distance = 1
-    while distance < freq_count:
-        line = doubled(line, "freq", distance)
-        distance *= 2
-    near = line[None]
-    distance = 2
-    while distance < rcv_count:
-        near = doubled(near, "rcv", distance)
-        distance *= 2
+    later = [list(pack(part, spectra, rcv_count - 1, spectra.shape[1:])) for part in range(1, parts)]
+    for packed in later:
+        near, packed[0] = lax.optimization_barrier((near, packed[0]))
+    near = jnp.stack([near if e == 0 else exchange(near, "freq", e) for e in range(freq_count)])
     far = exchange(near, "rcv", 1)
     gains = pl.pallas_call(
         functools.partial(gains_kernel, source_tiles=freq_count),
@@ -316,10 +310,7 @@
         name="gains",
     )(gain_table, near, far, column)
 
-    slots = spectra
-    for part in range(1, parts):
-        slots, gathered[-1][0] = lax.optimization_barrier((slots, gathered[-1][0]))
-        packed = pack(part, slots, rcv_count - 1, spectra.shape[1:])
+    for packed in later:
         gathered[-1][0], *packed = lax.optimization_barrier((gathered[-1][0], *packed))
         gathered.append([exchange(tile, "rcv", n + 1) for n, tile in enumerate(packed)])
 

time: 187 us -> 180 us (0.963)
  waiting for transfers between devices: 103 us -> 86.8 us
  Pallas kernels: 54.1 us -> 62.7 us
    ppermute x12 -> x14, waiting for transfers between devices: 61.5 us -> 46 us  [exchange(): lax.ppermute(array, axis, [(i, i ^ distance) for i in range(lax.axis_size...]
    pallas_call x2, Pallas kernels: 13.3 us -> 22.7 us  [on_device(): pl.pallas_call(functools.partial(multiples_kernel, first_slot=part * rcv_...]
    all_to_all x2, waiting for transfers between devices: 41.4 us -> 32 us  [on_device(): lax.all_to_all(result, ('freq', 'rcv'), split_axis=0, concat_axis=0, tile...]
    all_to_all x1, waiting for transfers between devices: 0.01 us -> 8.75 us  [on_device(): lax.all_to_all(packed, 'rcv', split_axis=0, concat_axis=0, tiled=True)]
    ppermute x12 -> x14, starting transfers between devices: 14 us -> 15.4 us  [exchange(): lax.ppermute(array, axis, [(i, i ^ distance) for i in range(lax.axis_size...]
  transfers between devices with their start and end apart: 15 -> 17, of which waited for: 8 -> 9; matrix products, arithmetic and copies ran while one was open for 1% -> 1% of each run, Pallas kernels for 19% -> 26%
where the time goes in v2:
time: 180 us
  waiting for transfers between devices  86.8 us (48%)
  Pallas kernels  62.7 us (35%)
  starting transfers between devices  26.8 us (15%)
  local copies, waits for them, and re-layouts  2.06 us (1%)
    ppermute x14, waiting for transfers between devices, exchange(): lax.ppermute(array, axis, [(i, i ^ distance) for i in range(lax.axis_size...  46 us
    pallas_call x2, Pallas kernels, synthesis(): pl.pallas_call(functools.partial(synthesis_kernel, receiver_tile=receiver...  32.8 us
    all_to_all x2, waiting for transfers between devices, on_device(): lax.all_to_all(result, ('freq', 'rcv'), split_axis=0, concat_axis=0, tile...  32 us
    pallas_call x2, Pallas kernels, on_device(): pl.pallas_call(functools.partial(multiples_kernel, first_slot=part * rcv_...  22.7 us
    ppermute x14, starting transfers between devices, exchange(): lax.ppermute(array, axis, [(i, i ^ distance) for i in range(lax.axis_size...  15.4 us
    all_to_all x1, waiting for transfers between devices, on_device(): lax.all_to_all(packed, 'rcv', split_axis=0, concat_axis=0, tiled=True)  8.75 us
    all_to_all x2, starting transfers between devices, on_device(): lax.all_to_all(result, ('freq', 'rcv'), split_axis=0, concat_axis=0, tile...  7.8 us
    pallas_call x2, Pallas kernels, pack(): pl.pallas_call(functools.partial(pack_kernel, first_slot=part * rcv_count...  4.71 us
  transfers between devices with their start and end apart: 17, of which 9 were waited for; matrix products, arithmetic and copies ran while one was open for 1% of the time, Pallas kernels for 26%

profile of v2, /device:TPU:0, one launch (start us, length us, event | category | flops | bytes accessed | tf_op | source)
XLA Modules:
  0.0 179.8 jit_solution(17573838191036843023)
XLA Ops:
  0.0 3.0 %collective-permute-start.1 = (s32[64,128]{1,0:T(8,128)}, s32[64,128]{1,0:T(8,128)S(1)}, u32[]{:S(2)}, u32[]{:S(2)}) collective-permute-start(s32[64,128]{1,0:T(8,128)} %bitcast.26), channel_id=1, source_target_pairs={{0,4},{1,5},{2,6},{3,7},{4,0},{5,1},{6,2},{7,3},{8,12},{9,13},{10,... | collective-permute-start | bytes 98312 | tf_op jit(solution)/shard_map/ppermute | solution.py:241
  3.0 1.5 collective-permute-start
  4.5 2.4 %pack.2 = f32[8,2,64,512]{3,2,1,0:T(8,128)} custom-call(f32[16,2,64,512]{3,2,1,0:T(8,128)} %spectra_ref.7), custom_call_target="tpu_custom_call" | custom-call | tf_op jit(solution)/shard_map/pack/pallas_call | solution.py:260
  7.2 2.3 %collective-permute-done.2 = s32[64,128]{1,0:T(8,128)S(1)} collective-permute-done((s32[64,128]{1,0:T(8,128)}, s32[64,128]{1,0:T(8,128)S(1)}, u32[]{:S(2)}, u32[]{:S(2)}) %collective-permute-start.2) | collective-permute-done | bytes 32800 | tf_op jit(solution)/shard_map/ppermute | solution.py:241
  9.5 3.6 %all-to-all-start = ((f32[8,2,64,512]{3,2,1,0:T(8,128)}), f32[8,2,64,512]{3,2,1,0:T(8,128)S(1)}, u32[]{:S(2)}, u32[]{:S(2)}) async-start(f32[8,2,64,512]{3,2,1,0:T(8,128)} %pack.2), calls=%async_computation | async-start | bytes 4194304 | tf_op jit(solution)/shard_map/all_to_all | solution.py:297
  13.2 2.3 %pack.3 = (f32[2,64,512]{2,1,0:T(8,128)}, f32[2,64,512]{2,1,0:T(8,128)}, f32[2,64,512]{2,1,0:T(8,128)}, f32[2,64,512]{2,1,0:T(8,128)}, f32[2,64,512]{2,1,0:T(8,1...) custom-call(f32[16,2,64,512]{3,2,1,0:T(8,128)} %spectra_ref.7), custom_call_target="tpu_custom_call" | custom-call | tf_op jit(solution)/shard_map/pack/pallas_call | solution.py:260
  15.5 3.7 %collective-permute-start.5 = (s32[4,64,128]{2,1,0:T(8,128)S(1)}, s32[4,64,128]{2,1,0:T(8,128)S(1)}, u32[]{:S(2)}, u32[]{:S(2)}) collective-permute-start(s32[4,64,128]{2,1,0:T(8,128)S(1)} %pad_add_fusion.1), channel_id=1, source_target_pairs={{0,24},{8,16},{16,8},{24,0},{1,25},{9,17},{17,9},{25,1},{2,26},{10... | collective-permute-start | bytes 393224 | tf_op jit(solution)/shard_map/ppermute | solution.py:241
  19.9 3.8 %collective-permute-done.5 = s32[4,64,128]{2,1,0:T(8,128)S(1)} collective-permute-done((s32[4,64,128]{2,1,0:T(8,128)S(1)}, s32[4,64,128]{2,1,0:T(8,128)S(1)}, u32[]{:S(2)}, u32[]{:S(2)}) %collective-permute-start.5) | collective-permute-done | bytes 131104 | tf_op jit(solution)/shard_map/ppermute | solution.py:241
  23.7 7.1 %collective-permute-done.4 = s32[4,64,128]{2,1,0:T(8,128)S(1)} collective-permute-done((s32[4,64,128]{2,1,0:T(8,128)S(1)}, s32[4,64,128]{2,1,0:T(8,128)S(1)}, u32[]{:S(2)}, u32[]{:S(2)}) %collective-permute-start.4) | collective-permute-done | bytes 131104 | tf_op jit(solution)/shard_map/ppermute | solution.py:241
  31.0 8.7 %all-to-all-done.refs_0_ = f32[8,2,64,512]{3,2,1,0:T(8,128)S(1)} async-done(((f32[8,2,64,512]{3,2,1,0:T(8,128)}), f32[8,2,64,512]{3,2,1,0:T(8,128)S(1)}, u32[]{:S(2)}, u32[]{:S(2)}) %all-to-all-start) | async-done | bytes 2097184 | tf_op jit(solution)/shard_map/all_to_all | solution.py:297
  39.7 1.3 copy-done
  42.2 2.3 %collective-permute-start.10 = (f32[2,64,512]{2,1,0:T(8,128)}, f32[2,64,512]{2,1,0:T(8,128)}, u32[]{:S(2)}, u32[]{:S(2)}) collective-permute-start(f32[2,64,512]{2,1,0:T(8,128)} %get-tuple-element.45), channel_id=1, source_target_pairs={{0,5},{1,4},{2,7},{3,6},{4,1},{5,0},{6,3},{7,2},{8,13},{9,12},{10,... | collective-permute-start | bytes 786440 | tf_op jit(solution)/shard_map/ppermute | solution.py:241
  44.7 2.5 %gains.1.gains_hbm = f32[2,512,512]{2,1,0:T(8,128)S(1)} custom-call(f32[2,16]{1,0:T(2,128)S(1)} %copy-done.4, s32[4,4,64,128]{3,2,1,0:T(8,128)S(1)} %pad_add_fusion.near_ref, s32[4,4,64,128]{3,2,1,0:T(8,128)S(1)} %collective-permute-done.6.far_ref, s32[512,1]{1,0:T(8,128)S(1)} %copy.16.column_ref), custom_call_target="tpu_custom_call" | custom-call | tf_op jit(solution)/shard_map/gains/pallas_call | solution.py:303
  47.3 10.8 %multiples.2 = f32[4,8,2,64,128]{4,3,2,1,0:T(8,128)} custom-call(s32[4]{0:T(128)S(1)} %copy-done.3, s32[512,1]{1,0:T(8,128)S(1)} %copy.16.column_ref, s32[1,512]{1,0:T(1,128)S(1)} %bitcast.18, f32[16,2,64,512]{3,2,1,0:T(8,128)} %spectra_ref.7, f32[2,512,512]{2,1,0:T(8,128)S(1)} %gains.1.gains_hbm, f32[8,2,64,512]{3,2,1,0:T(8,128)S(1)} %copy-done.1), custom_call_target="tpu_custom_call" | custom-call | tf_op jit(solution)/shard_map/multiples/pallas_call | solution.py:319
  58.1 4.1 %all-to-all-start.1 = ((f32[32,2,64,128]{3,2,1,0:T(8,128)}), f32[32,2,64,128]{3,2,1,0:T(8,128)}, u32[]{:S(2)}, u32[]{:S(2)}) async-start(f32[32,2,64,128]{3,2,1,0:T(8,128)} %bitcast.20), calls=%async_computation.1 | async-start | bytes 4194304 | tf_op jit(solution)/shard_map/all_to_all | solution.py:349
  62.5 2.6 %collective-permute-start.12 = (f32[2,64,512]{2,1,0:T(8,128)S(1)}, f32[2,64,512]{2,1,0:T(8,128)S(1)}, u32[]{:S(2)}, u32[]{:S(2)}) collective-permute-start(f32[2,64,512]{2,1,0:T(8,128)S(1)} %copy-done.7), channel_id=1, source_target_pairs={{0,6},{1,7},{2,4},{3,5},{4,2},{5,3},{6,0},{7,1},{8,14},{9,15},{10,... | collective-permute-start | bytes 786440 | tf_op jit(solution)/shard_map/ppermute | solution.py:241
  65.1 26.5 %collective-permute-done.12.refs_5_ = f32[2,64,512]{2,1,0:T(8,128)S(1)} collective-permute-done((f32[2,64,512]{2,1,0:T(8,128)S(1)}, f32[2,64,512]{2,1,0:T(8,128)S(1)}, u32[]{:S(2)}, u32[]{:S(2)}) %collective-permute-start.12) | collective-permute-done | bytes 262176 | tf_op jit(solution)/shard_map/ppermute | solution.py:241
  91.5 6.0 %collective-permute-done.13.refs_6_ = f32[2,64,512]{2,1,0:T(8,128)S(1)} collective-permute-done((f32[2,64,512]{2,1,0:T(8,128)S(1)}, f32[2,64,512]{2,1,0:T(8,128)S(1)}, u32[]{:S(2)}, u32[]{:S(2)}) %collective-permute-start.13) | collective-permute-done | bytes 262176 | tf_op jit(solution)/shard_map/ppermute | solution.py:241
  97.6 11.9 %multiples.3 = f32[4,8,2,64,128]{4,3,2,1,0:T(8,128)} custom-call(s32[4]{0:T(128)S(1)} %copy-done.3, s32[512,1]{1,0:T(8,128)S(1)} %copy.16.column_ref, s32[1,512]{1,0:T(1,128)S(1)} %bitcast.19, f32[16,2,64,512]{3,2,1,0:T(8,128)} %spectra_ref.7, f32[2,512,512]{2,1,0:T(8,128)S(1)} %gains.1.gains_hbm, f32[2,64,512]{2,1,0:T(8,128)S(1)} %collective-permute-done.11.refs_0_, ...), custom_call_target="tpu_custom_call" | custom-call | tf_op jit(solution)/shard_map/multiples/pallas_call | solution.py:319
  109.5 1.9 %all-to-all-done.1 = f32[32,2,64,128]{3,2,1,0:T(8,128)} async-done(((f32[32,2,64,128]{3,2,1,0:T(8,128)}), f32[32,2,64,128]{3,2,1,0:T(8,128)}, u32[]{:S(2)}, u32[]{:S(2)}) %all-to-all-start.1) | async-done | bytes 2097184 | tf_op jit(solution)/shard_map/all_to_all | solution.py:349
  111.4 3.7 %all-to-all-start.2 = ((f32[32,2,64,128]{3,2,1,0:T(8,128)}), f32[32,2,64,128]{3,2,1,0:T(8,128)S(1)}, u32[]{:S(2)}, u32[]{:S(2)}) async-start(f32[32,2,64,128]{3,2,1,0:T(8,128)} %bitcast.21), calls=%async_computation.2 | async-start | bytes 4194304 | tf_op jit(solution)/shard_map/all_to_all | solution.py:349
  116.7 17.2 %synthesis.2.base_ref = f32[128,64,512]{2,1,0:T(8,128)} custom-call(f32[64,512]{1,0:T(8,128)S(1)} %reshape.251.table_ref, f32[128,64,512]{2,1,0:T(8,128)} %base_ref.1, f32[4096,128]{1,0:T(8,128)} %bitcast.13.refs_0_), custom_call_target="tpu_custom_call" | custom-call | tf_op jit(solution)/shard_map/synthesis/pallas_call | solution.py:277
  133.9 30.1 %all-to-all-done.2 = f32[32,2,64,128]{3,2,1,0:T(8,128)S(1)} async-done(((f32[32,2,64,128]{3,2,1,0:T(8,128)}), f32[32,2,64,128]{3,2,1,0:T(8,128)S(1)}, u32[]{:S(2)}, u32[]{:S(2)}) %all-to-all-start.2) | async-done | bytes 2097184 | tf_op jit(solution)/shard_map/all_to_all | solution.py:349
  164.0 15.6 %synthesis.3 = f32[128,64,512]{2,1,0:T(8,128)} custom-call(f32[64,512]{1,0:T(8,128)S(1)} %reshape.250.table_ref, f32[128,64,512]{2,1,0:T(8,128)} %synthesis.2.base_ref, f32[4096,128]{1,0:T(8,128)S(1)} %bitcast.16), custom_call_target="tpu_custom_call" | custom-call | tf_op jit(solution)/shard_map/synthesis/pallas_call | solution.py:277
  (52 shorter events, 4.4 us)
Async XLA Ops:
  0.0 9.5 %copy-start.5 = (s32[128,64]{0,1:T(8,128)S(1)}, s32[128,64]{0,1:T(8,128)}, u32[]{:S(2)}) copy-start(s32[128,64]{0,1:T(8,128)} %param.10) | copy-start | bytes 98308
  0.0 6.9 %collective-permute-start.1 = (s32[64,128]{1,0:T(8,128)}, s32[64,128]{1,0:T(8,128)S(1)}, u32[]{:S(2)}, u32[]{:S(2)}) collective-permute-start(s32[64,128]{1,0:T(8,128)} %bitcast.26), channel_id=1, source_target_pairs={{0,4},{1,5},{2,6},{3,7},{4,0},{5,1},{6,2},{7,3},{8,12},{9,13},{10,... | collective-permute-start | bytes 98312 | tf_op jit(solution)/shard_map/ppermute | solution.py:241
  3.0 4.2 %collective-permute-start = (s32[64,128]{1,0:T(8,128)}, s32[64,128]{1,0:T(8,128)S(1)}, u32[]{:S(2)}, u32[]{:S(2)}) collective-permute-start(s32[64,128]{1,0:T(8,128)} %bitcast.27), channel_id=1, source_target_pairs={{0,2},{1,3},{2,0},{3,1},{4,6},{5,7},{6,4},{7,5},{8,10},{9,11},{10,... | collective-permute-start | bytes 98312 | tf_op jit(solution)/shard_map/ppermute | solution.py:241
  4.5 5.0 %collective-permute-start.2 = (s32[64,128]{1,0:T(8,128)}, s32[64,128]{1,0:T(8,128)S(1)}, u32[]{:S(2)}, u32[]{:S(2)}) collective-permute-start(s32[64,128]{1,0:T(8,128)} %bitcast.28), channel_id=1, source_target_pairs={{0,6},{1,7},{2,4},{3,5},{4,2},{5,3},{6,0},{7,1},{8,14},{9,15},{10,... | collective-permute-start | bytes 98312 | tf_op jit(solution)/shard_map/ppermute | solution.py:241
  9.5 30.2 %all-to-all-start = ((f32[8,2,64,512]{3,2,1,0:T(8,128)}), f32[8,2,64,512]{3,2,1,0:T(8,128)S(1)}, u32[]{:S(2)}, u32[]{:S(2)}) async-start(f32[8,2,64,512]{3,2,1,0:T(8,128)} %pack.2), calls=%async_computation | async-start | bytes 4194304 | tf_op jit(solution)/shard_map/all_to_all | solution.py:297
  13.1 31.4 %copy-start.2 = (s32[512]{0:T(512)S(1)}, s32[512]{0:T(512)}, u32[]{:S(2)}) copy-start(s32[512]{0:T(512)} %param.8) | copy-start | bytes 6148
  13.1 31.6 %copy-start.4 = (f32[2,16]{1,0:T(2,128)S(1)}, f32[2,16]{1,0:T(2,128)}, u32[]{:S(2)}) copy-start(f32[2,16]{1,0:T(2,128)} %table_ref.1) | copy-start | bytes 388
  15.5 8.3 %collective-permute-start.5 = (s32[4,64,128]{2,1,0:T(8,128)S(1)}, s32[4,64,128]{2,1,0:T(8,128)S(1)}, u32[]{:S(2)}, u32[]{:S(2)}) collective-permute-start(s32[4,64,128]{2,1,0:T(8,128)S(1)} %pad_add_fusion.1), channel_id=1, source_target_pairs={{0,24},{8,16},{16,8},{24,0},{1,25},{9,17},{17,9},{25,1},{2,26},{10... | collective-permute-start | bytes 393224 | tf_op jit(solution)/shard_map/ppermute | solution.py:241
  19.1 11.7 %collective-permute-start.4 = (s32[4,64,128]{2,1,0:T(8,128)S(1)}, s32[4,64,128]{2,1,0:T(8,128)S(1)}, u32[]{:S(2)}, u32[]{:S(2)}) collective-permute-start(s32[4,64,128]{2,1,0:T(8,128)S(1)} %pad_add_fusion.1), channel_id=1, source_target_pairs={{0,16},{8,24},{16,0},{24,8},{1,17},{9,25},{17,1},{25,9},{2,18},{10... | collective-permute-start | bytes 393224 | tf_op jit(solution)/shard_map/ppermute | solution.py:241
  19.2 11.7 %collective-permute-start.3 = (s32[4,64,128]{2,1,0:T(8,128)S(1)}, s32[4,64,128]{2,1,0:T(8,128)S(1)}, u32[]{:S(2)}, u32[]{:S(2)}) collective-permute-start(s32[4,64,128]{2,1,0:T(8,128)S(1)} %pad_add_fusion.1), channel_id=1, source_target_pairs={{0,8},{8,0},{16,24},{24,16},{1,9},{9,1},{17,25},{25,17},{2,10},{10... | collective-permute-start | bytes 393224 | tf_op jit(solution)/shard_map/ppermute | solution.py:241
  30.9 16.4 %copy-start.3 = (s32[4]{0:T(128)S(1)}, s32[4]{0:T(128)}, u32[]{:S(2)}) copy-start(s32[4]{0:T(128)} %counts_ref.3) | copy-start | bytes 52
  30.9 13.8 %collective-permute-start.6 = (s32[4,4,64,128]{3,2,1,0:T(8,128)S(1)}, s32[4,4,64,128]{3,2,1,0:T(8,128)S(1)}, u32[]{:S(2)}, u32[]{:S(2)}) collective-permute-start(s32[4,4,64,128]{3,2,1,0:T(8,128)S(1)} %pad_add_fusion.near_ref), channel_id=1, source_target_pairs={{0,1},{1,0},{2,3},{3,2},{4,5},{5,4},{6,7},{7,6},{8,9},{9,8},{10,11... | collective-permute-start | bytes 1572872 | tf_op jit(solution)/shard_map/ppermute | solution.py:241
  41.0 17.0 %collective-permute-start.7 = (f32[2,64,512]{2,1,0:T(8,128)}, f32[2,64,512]{2,1,0:T(8,128)}, u32[]{:S(2)}, u32[]{:S(2)}) collective-permute-start(f32[2,64,512]{2,1,0:T(8,128)} %get-tuple-element.42), channel_id=1, source_target_pairs={{0,2},{1,3},{2,0},{3,1},{4,6},{5,7},{6,4},{7,5},{8,10},{9,11},{10,... | collective-permute-start | bytes 786440 | tf_op jit(solution)/shard_map/ppermute | solution.py:241
  41.5 16.5 %collective-permute-start.8 = (f32[2,64,512]{2,1,0:T(8,128)}, f32[2,64,512]{2,1,0:T(8,128)}, u32[]{:S(2)}, u32[]{:S(2)}) collective-permute-start(f32[2,64,512]{2,1,0:T(8,128)} %get-tuple-element.43), channel_id=1, source_target_pairs={{0,3},{1,2},{2,1},{3,0},{4,7},{5,6},{6,5},{7,4},{8,11},{9,10},{10,... | collective-permute-start | bytes 786440 | tf_op jit(solution)/shard_map/ppermute | solution.py:241
  41.5 16.5 %collective-permute-start.9 = (f32[2,64,512]{2,1,0:T(8,128)}, f32[2,64,512]{2,1,0:T(8,128)}, u32[]{:S(2)}, u32[]{:S(2)}) collective-permute-start(f32[2,64,512]{2,1,0:T(8,128)} %get-tuple-element.44), channel_id=1, source_target_pairs={{0,4},{1,5},{2,6},{3,7},{4,0},{5,1},{6,2},{7,3},{8,12},{9,13},{10,... | collective-permute-start | bytes 786440 | tf_op jit(solution)/shard_map/ppermute | solution.py:241
  42.2 15.9 %collective-permute-start.10 = (f32[2,64,512]{2,1,0:T(8,128)}, f32[2,64,512]{2,1,0:T(8,128)}, u32[]{:S(2)}, u32[]{:S(2)}) collective-permute-start(f32[2,64,512]{2,1,0:T(8,128)} %get-tuple-element.45), channel_id=1, source_target_pairs={{0,5},{1,4},{2,7},{3,6},{4,1},{5,0},{6,3},{7,2},{8,13},{9,12},{10,... | collective-permute-start | bytes 786440 | tf_op jit(solution)/shard_map/ppermute | solution.py:241
  58.1 4.1 %copy-start.8 = (f32[2,64,512]{2,1,0:T(8,128)S(1)}, f32[2,64,512]{2,1,0:T(8,128)}, u32[]{:S(2)}) copy-start(f32[2,64,512]{2,1,0:T(8,128)} %get-tuple-element.47) | copy-start | bytes 786436
  58.1 4.4 %copy-start.7 = (f32[2,64,512]{2,1,0:T(8,128)S(1)}, f32[2,64,512]{2,1,0:T(8,128)}, u32[]{:S(2)}) copy-start(f32[2,64,512]{2,1,0:T(8,128)} %get-tuple-element.52) | copy-start | bytes 786436
  58.1 7.0 %copy-start.6 = (f32[2,64,512]{2,1,0:T(8,128)S(1)}, f32[2,64,512]{2,1,0:T(8,128)}, u32[]{:S(2)}) copy-start(f32[2,64,512]{2,1,0:T(8,128)} %get-tuple-element.53) | copy-start | bytes 786436
  58.1 53.3 %all-to-all-start.1 = ((f32[32,2,64,128]{3,2,1,0:T(8,128)}), f32[32,2,64,128]{3,2,1,0:T(8,128)}, u32[]{:S(2)}, u32[]{:S(2)}) async-start(f32[32,2,64,128]{3,2,1,0:T(8,128)} %bitcast.20), calls=%async_computation.1 | async-start | bytes 4194304 | tf_op jit(solution)/shard_map/all_to_all | solution.py:349
  62.2 2.9 %collective-permute-start.11 = (f32[2,64,512]{2,1,0:T(8,128)S(1)}, f32[2,64,512]{2,1,0:T(8,128)S(1)}, u32[]{:S(2)}, u32[]{:S(2)}) collective-permute-start(f32[2,64,512]{2,1,0:T(8,128)S(1)} %copy-done.8), channel_id=1, source_target_pairs={{0,1},{1,0},{2,3},{3,2},{4,5},{5,4},{6,7},{7,6},{8,9},{9,8},{10,11... | collective-permute-start | bytes 786440 | tf_op jit(solution)/shard_map/ppermute | solution.py:241
  62.5 29.1 %collective-permute-start.12 = (f32[2,64,512]{2,1,0:T(8,128)S(1)}, f32[2,64,512]{2,1,0:T(8,128)S(1)}, u32[]{:S(2)}, u32[]{:S(2)}) collective-permute-start(f32[2,64,512]{2,1,0:T(8,128)S(1)} %copy-done.7), channel_id=1, source_target_pairs={{0,6},{1,7},{2,4},{3,5},{4,2},{5,3},{6,0},{7,1},{8,14},{9,15},{10,... | collective-permute-start | bytes 786440 | tf_op jit(solution)/shard_map/ppermute | solution.py:241
  65.1 32.5 %collective-permute-start.13 = (f32[2,64,512]{2,1,0:T(8,128)S(1)}, f32[2,64,512]{2,1,0:T(8,128)S(1)}, u32[]{:S(2)}, u32[]{:S(2)}) collective-permute-start(f32[2,64,512]{2,1,0:T(8,128)S(1)} %copy-done.6), channel_id=1, source_target_pairs={{0,7},{1,6},{2,5},{3,4},{4,3},{5,2},{6,1},{7,0},{8,15},{9,14},{10,... | collective-permute-start | bytes 786440 | tf_op jit(solution)/shard_map/ppermute | solution.py:241
  111.4 52.6 %all-to-all-start.2 = ((f32[32,2,64,128]{3,2,1,0:T(8,128)}), f32[32,2,64,128]{3,2,1,0:T(8,128)S(1)}, u32[]{:S(2)}, u32[]{:S(2)}) async-start(f32[32,2,64,128]{3,2,1,0:T(8,128)} %bitcast.21), calls=%async_computation.2 | async-start | bytes 4194304 | tf_op jit(solution)/shard_map/all_to_all | solution.py:349
  (2 other events, 3.9 us)

commit v3 on v2

--- a/solution.py
+++ b/solution.py
@@ -86,7 +86,7 @@
 
 
 def multiples_kernel(counts_ref, column_ref, row_ref, spectra_ref, gains_hbm, *refs, first_slot):
-    tiles, (out, result, data, gains, u, w, y1, y2, tile_sems, gain_sem, out_sems) = refs[:-11], refs[-11:]
+    tiles, (out, result, data, gains, u, u2, w, y1, y2, tile_sems, gain_sem, out_sems) = refs[:-12], refs[-12:]
     source_tiles, receiver_tiles, _, receiver_tile, source_tile = result.shape
     side = data.shape[3]
     pick = min(PICK, side)
@@ -143,36 +143,48 @@
             u[rows, again] = u[rows, high]
             u[rows, low] = mm(table, w[2 * side + start : 2 * side + start + pick, :]).astype(jnp.bfloat16)
 
-        def product(result, beside=()):
-            columns = range(0, 2 * side, PICK)
-            each = -(-len(beside) // len(columns))
-            for n, start in enumerate(columns):
+        def product(left, result, beside):
+            for n, start in enumerate(range(0, 2 * side, PICK)):
                 cols = slice(start, start + PICK)
-                result[:, cols] = mm(u[...], w[:, cols])
-                for work in beside[n * each : (n + 1) * each]:
+                result[:, cols] = mm(left[...], w[:, cols])
+                for work in beside[n]:
                     work()
 
+        blocks = 2 * side // PICK
+
+        def split_block(n):
+            cols = slice(n * PICK, (n + 1) * PICK)
+            for start in range(0, side, 64):
+                rows = slice(start, start + 64)
+                value_high, value_low = split(y1[rows, cols])
+                u2[rows, n * PICK : (n + 1) * PICK] = value_high
+                u2[rows, 2 * side + n * PICK : 2 * side + (n + 1) * PICK] = value_high
+                u2[rows, 4 * side + n * PICK : 4 * side + (n + 1) * PICK] = value_low
+
         block = 128
 
-        def weigh(y, order, q, s):
+        def weigh(y, order, c, q, s):
             qs, ss = slice(q, q + block), slice(s, s + block)
-            for c in range(2):
-                qc, sc = slice(c * side + q, c * side + q + block), slice(c * side + s, c * side + s + block)
-                total = y[qs, sc] + y[ss, qc].T
-                if q != s:
-                    y[ss, qc] = gains[order, ss, qs] * total.T
-                y[qs, sc] = gains[order, qs, ss] * total
+            qc, sc = slice(c * side + q, c * side + q + block), slice(c * side + s, c * side + s + block)
+            total = y[qs, sc] + y[ss, qc].T
+            if q != s:
+                y[ss, qc] = gains[order, ss, qs] * total.T
+            y[qs, sc] = gains[order, qs, ss] * total
 
         pairs = [(q, s) for q in range(0, side, block) for s in range(q, side, block)]
-        product(y1)
-        for start in range(0, side, 64):
-            rows = slice(start, start + 64)
-            u[rows, high], u[rows, low] = split(y1[rows, :])
-            u[rows, again] = u[rows, high]
+        product(u, y1, [[]] + [[functools.partial(split_block, n)] for n in range(blocks - 1)])
+        split_block(blocks - 1)
         gain_copy.wait()
-        product(y2, [functools.partial(weigh, y1, 0, q, s) for q, s in pairs])
+        half = blocks // 2
+        beside = [[] for _ in range(blocks)]
+        for c in range(2):
+            for n, (q, s) in enumerate(pairs):
+                beside[c * half + n % half].append(functools.partial(weigh, y1, 0, c, q, s))
+        for n, (q, s) in enumerate(pairs):
+            beside[half + n % half].append(functools.partial(weigh, y2, 1, 0, q, s))
+        product(u2, y2, beside)
         for q, s in pairs:
-            weigh(y2, 1, q, s)
+            weigh(y2, 1, 1, q, s)
         for start in range(0, side, pick):
             rows = slice(start, start + pick)
             table = scatter_table(row_ref[:, rows], start, pick)
@@ -193,8 +205,8 @@
         copy.wait()
 
 
-def synthesis_kernel(table_ref, base_ref, *refs, receiver_tile):
-    coefs, (out_ref, coef_ref, lines, tables, sems) = refs[:-5], refs[-5:]
+def synthesis_kernel(table_ref, *refs, receiver_tile, pieces):
+    bases, coefs, (out_ref, stage, out_sems, coef_ref, lines, tables, sems) = refs[:pieces], refs[pieces:-7], refs[-7:]
     depth = table_ref.shape[0]
     source_tile = coef_ref.shape[1]
     first = pl.multiple_of(pl.program_id(0) * ROWS, ROWS)
@@ -221,12 +233,39 @@
         for g in range(lines.shape[0]):
             lines[g, pl.ds(r, source_tile, stride=ROWS), :] = both[g * LANES : (g + 1) * LANES].T
 
-    size = 32
-    for start in range(0, source_tile, size):
-        rows = slice(start * ROWS, (start + size) * ROWS)
-        both = jnp.concatenate([lines[g, rows, :] for g in range(lines.shape[0])], axis=1).astype(jnp.bfloat16)
-        total = mm(jnp.concatenate([both, both[:, :depth]], axis=1), tables[...])
-        out_ref[start : start + size] = base_ref[start : start + size] - total.reshape(size, ROWS, -1)
+    step = pl.program_id(0)
+    slot = step % 2
+    piece = source_tile // pieces
+
+    def leave(at, k):
+        rows = pl.ds(pl.multiple_of(at * ROWS, ROWS), ROWS)
+        return pltpu.make_async_copy(
+            stage.at[at % 2, k], out_ref.at[pl.ds(k * piece, piece), rows], out_sems.at[at % 2, k]
+        )
+
+    @pl.when(step >= 2)
+    def _():
+        for k in range(pieces):
+            leave(step - 2, k).wait()
+
+    size = min(32, piece)
+    for k in range(pieces):
+        for start in range(0, piece, size):
+            rows = slice((k * piece + start) * ROWS, (k * piece + start + size) * ROWS)
+            both = jnp.concatenate([lines[g, rows, :] for g in range(lines.shape[0])], axis=1).astype(jnp.bfloat16)
+            total = mm(jnp.concatenate([both, both[:, :depth]], axis=1), tables[...])
+            span = slice(start, start + size)
+            stage[slot, k, span] = bases[k][span] - total.reshape(size, ROWS, -1)
+        leave(step, k).start()
+
+    @pl.when(step == pl.num_programs(0) - 1)
+    def _():
+        for k in range(pieces):
+            leave(step, k).wait()
+
+            @pl.when(step >= 1)
+            def _():
+                leave(step - 1, k).wait()
 
 
 def params(mebibytes):
@@ -273,22 +312,26 @@
 
     def synthesis(coefs, table, base):
         depth = table.shape[0]
-        block = pl.BlockSpec((source_tile, ROWS, samples), lambda n: (0, n, 0))
+        pieces = 4
+        piece = (source_tile // pieces, ROWS, samples)
+        blocks = [pl.BlockSpec(piece, lambda n, k=k: (k, n, 0)) for k in range(pieces)]
         return pl.pallas_call(
-            functools.partial(synthesis_kernel, receiver_tile=receiver_tile),
+            functools.partial(synthesis_kernel, receiver_tile=receiver_tile, pieces=pieces),
             out_shape=pltpu.HBM(recorded.shape, jnp.float32),
             grid=(receiver_tile // ROWS,),
-            in_specs=[whole_in(), block] + [hbm] * len(coefs),
-            out_specs=block,
+            in_specs=[whole_in()] + blocks + [hbm] * len(coefs),
+            out_specs=hbm,
             scratch_shapes=[
+                pltpu.VMEM((2, pieces) + piece, jnp.float32),
+                pltpu.SemaphoreType.DMA((2, pieces)),
                 pltpu.VMEM((depth * receiver_tile, source_tile), jnp.float32),
                 pltpu.VMEM((2 * depth // LANES, source_tile * ROWS, LANES), jnp.float32),
                 pltpu.VMEM((3 * depth, samples), jnp.bfloat16),
                 pltpu.SemaphoreType.DMA((len(coefs),)),
             ],
-            compiler_params=params(24),
+            compiler_params=params(40),
             name="synthesis",
-        )(table, in_hbm(base), *coefs)
+        )(table, *[in_hbm(base)] * pieces, *coefs)
 
     tile = gain_index.T
     near = jnp.stack([tile if n == 0 else exchange(tile, "rcv", 2 * n) for n in range(rcv_count // 2)])
@@ -311,7 +354,7 @@
     )(gain_table, near, far, column)
 
     for packed in later:
-        gathered[-1][0], *packed = lax.optimization_barrier((gathered[-1][0], *packed))
+        gathered[-1][0], gains, *packed = lax.optimization_barrier((gathered[-1][0], gains, *packed))
         gathered.append([exchange(tile, "rcv", n + 1) for n, tile in enumerate(packed)])
 
     results = []
@@ -325,6 +368,7 @@
                 pltpu.VMEM((freq_count, rcv_count, 2, receiver_tile, source_tile), jnp.float32),
                 pltpu.VMEM((rcv_count, 2, receiver_tile, side), jnp.float32),
                 pltpu.VMEM((2, side, side), jnp.float32),
+                pltpu.VMEM((side, 6 * side), jnp.bfloat16),
                 pltpu.VMEM((side, 6 * side), jnp.bfloat16),
                 pltpu.VMEM((6 * side, 2 * side), jnp.bfloat16),
                 pltpu.VMEM((side, 2 * side), jnp.float32),

time: 180 us -> 178 us (0.989)
  waiting for transfers between devices: 86.8 us -> 84.9 us
    all_to_all x1, waiting for transfers between devices: 8.75 us -> 4.46 us  [on_device(): lax.all_to_all(packed, 'rcv', split_axis=0, concat_axis=0, tiled=True)]
    ppermute x14, waiting for transfers between devices: 46 us -> 47.9 us  [exchange(): lax.ppermute(array, axis, [(i, i ^ distance) for i in range(lax.axis_size...]
  transfers between devices with their start and end apart: 17 -> 17, of which waited for: 9 -> 11; matrix products, arithmetic and copies ran while one was open for 1% -> 1% of each run, Pallas kernels for 26% -> 27%
where the time goes in v3:
time: 178 us; the launch traced here: 177 us
  waiting for transfers between devices  84.9 us (48%)
  Pallas kernels  62.3 us (35%)
  starting transfers between devices  28 us (16%)
    ppermute x14, waiting for transfers between devices, exchange(): lax.ppermute(array, axis, [(i, i ^ distance) for i in range(lax.axis_size...  47.9 us
    all_to_all x2, waiting for transfers between devices, on_device(): lax.all_to_all(result, ('freq', 'rcv'), split_axis=0, concat_axis=0, tile...  32.6 us
    pallas_call x2, Pallas kernels, synthesis(): pl.pallas_call(functools.partial(synthesis_kernel, receiver_tile=receiver...  31.3 us
    pallas_call x2, Pallas kernels, on_device(): pl.pallas_call(functools.partial(multiples_kernel, first_slot=part * rcv_...  23.8 us
    ppermute x14, starting transfers between devices, exchange(): lax.ppermute(array, axis, [(i, i ^ distance) for i in range(lax.axis_size...  15.4 us
    all_to_all x2, starting transfers between devices, on_device(): lax.all_to_all(result, ('freq', 'rcv'), split_axis=0, concat_axis=0, tile...  8.23 us
    pallas_call x2, Pallas kernels, pack(): pl.pallas_call(functools.partial(pack_kernel, first_slot=part * rcv_count...  4.7 us
    all_to_all x1, waiting for transfers between devices, on_device(): lax.all_to_all(packed, 'rcv', split_axis=0, concat_axis=0, tiled=True)  4.46 us
  transfers between devices with their start and end apart: 17, of which 11 were waited for; matrix products, arithmetic and copies ran while one was open for 1% of the time, Pallas kernels for 27%

profile of v3, /device:TPU:0, one launch (start us, length us, event | category | flops | bytes accessed | tf_op | source)
XLA Modules:
  0.0 177.3 jit_solution(6907788082980338994)
XLA Ops:
  0.0 3.0 %collective-permute-start.1 = (s32[64,128]{1,0:T(8,128)}, s32[64,128]{1,0:T(8,128)S(1)}, u32[]{:S(2)}, u32[]{:S(2)}) collective-permute-start(s32[64,128]{1,0:T(8,128)} %bitcast.26), channel_id=1, source_target_pairs={{0,4},{1,5},{2,6},{3,7},{4,0},{5,1},{6,2},{7,3},{8,12},{9,13},{10,... | collective-permute-start | bytes 98312 | tf_op jit(solution)/shard_map/ppermute | solution.py:280
  3.0 1.5 collective-permute-start
  4.5 2.4 %pack.2 = f32[8,2,64,512]{3,2,1,0:T(8,128)} custom-call(f32[16,2,64,512]{3,2,1,0:T(8,128)} %spectra_ref.7), custom_call_target="tpu_custom_call" | custom-call | tf_op jit(solution)/shard_map/pack/pallas_call | solution.py:299
  7.2 2.3 %collective-permute-done.2 = s32[64,128]{1,0:T(8,128)S(1)} collective-permute-done((s32[64,128]{1,0:T(8,128)}, s32[64,128]{1,0:T(8,128)S(1)}, u32[]{:S(2)}, u32[]{:S(2)}) %collective-permute-start.2) | collective-permute-done | bytes 32800 | tf_op jit(solution)/shard_map/ppermute | solution.py:280
  9.5 4.4 %all-to-all-start = ((f32[8,2,64,512]{3,2,1,0:T(8,128)}), f32[8,2,64,512]{3,2,1,0:T(8,128)}, u32[]{:S(2)}, u32[]{:S(2)}) async-start(f32[8,2,64,512]{3,2,1,0:T(8,128)} %pack.2), calls=%async_computation | async-start | bytes 4194304 | tf_op jit(solution)/shard_map/all_to_all | solution.py:340
  13.9 2.3 %pack.3 = (f32[2,64,512]{2,1,0:T(8,128)}, f32[2,64,512]{2,1,0:T(8,128)}, f32[2,64,512]{2,1,0:T(8,128)}, f32[2,64,512]{2,1,0:T(8,128)}, f32[2,64,512]{2,1,0:T(8,1...) custom-call(f32[16,2,64,512]{3,2,1,0:T(8,128)} %spectra_ref.7), custom_call_target="tpu_custom_call" | custom-call | tf_op jit(solution)/shard_map/pack/pallas_call | solution.py:299
  16.2 3.7 %collective-permute-start.5 = (s32[4,64,128]{2,1,0:T(8,128)S(1)}, s32[4,64,128]{2,1,0:T(8,128)S(1)}, u32[]{:S(2)}, u32[]{:S(2)}) collective-permute-start(s32[4,64,128]{2,1,0:T(8,128)S(1)} %pad_add_fusion.1), channel_id=1, source_target_pairs={{0,24},{8,16},{16,8},{24,0},{1,25},{9,17},{17,9},{25,1},{2,26},{10... | collective-permute-start | bytes 393224 | tf_op jit(solution)/shard_map/ppermute | solution.py:280
  20.7 3.8 %collective-permute-done.5 = s32[4,64,128]{2,1,0:T(8,128)S(1)} collective-permute-done((s32[4,64,128]{2,1,0:T(8,128)S(1)}, s32[4,64,128]{2,1,0:T(8,128)S(1)}, u32[]{:S(2)}, u32[]{:S(2)}) %collective-permute-start.5) | collective-permute-done | bytes 131104 | tf_op jit(solution)/shard_map/ppermute | solution.py:280
  24.5 7.0 %collective-permute-done.4 = s32[4,64,128]{2,1,0:T(8,128)S(1)} collective-permute-done((s32[4,64,128]{2,1,0:T(8,128)S(1)}, s32[4,64,128]{2,1,0:T(8,128)S(1)}, u32[]{:S(2)}, u32[]{:S(2)}) %collective-permute-start.4) | collective-permute-done | bytes 131104 | tf_op jit(solution)/shard_map/ppermute | solution.py:280
  31.8 1.7 collective-permute-done.6.far_ref
  33.5 2.5 %gains.1.gains_hbm = f32[2,512,512]{2,1,0:T(8,128)S(1)} custom-call(f32[2,16]{1,0:T(2,128)S(1)} %copy-done.2, s32[4,4,64,128]{3,2,1,0:T(8,128)S(1)} %pad_add_fusion.near_ref, s32[4,4,64,128]{3,2,1,0:T(8,128)S(1)} %collective-permute-done.6.far_ref, s32[512,1]{1,0:T(8,128)S(1)} %copy.16.column_ref), custom_call_target="tpu_custom_call" | custom-call | tf_op jit(solution)/shard_map/gains/pallas_call | solution.py:346
  36.1 4.5 %all-to-all-done.refs_0_ = f32[8,2,64,512]{3,2,1,0:T(8,128)} async-done(((f32[8,2,64,512]{3,2,1,0:T(8,128)}), f32[8,2,64,512]{3,2,1,0:T(8,128)}, u32[]{:S(2)}, u32[]{:S(2)}) %all-to-all-start) | async-done | bytes 2097184 | tf_op jit(solution)/shard_map/all_to_all | solution.py:340
  41.7 2.3 %collective-permute-start.10 = (f32[2,64,512]{2,1,0:T(8,128)}, f32[2,64,512]{2,1,0:T(8,128)S(1)}, u32[]{:S(2)}, u32[]{:S(2)}) collective-permute-start(f32[2,64,512]{2,1,0:T(8,128)} %get-tuple-element.47), channel_id=1, source_target_pairs={{0,5},{1,4},{2,7},{3,6},{4,1},{5,0},{6,3},{7,2},{8,13},{9,12},{10,... | collective-permute-start | bytes 786440 | tf_op jit(solution)/shard_map/ppermute | solution.py:280
  44.0 11.7 %multiples.2 = f32[4,8,2,64,128]{4,3,2,1,0:T(8,128)} custom-call(s32[4]{0:T(128)S(1)} %copy-done.1, s32[512,1]{1,0:T(8,128)S(1)} %copy.16.column_ref, s32[1,512]{1,0:T(1,128)S(1)} %bitcast.18, f32[16,2,64,512]{3,2,1,0:T(8,128)} %spectra_ref.7, f32[2,512,512]{2,1,0:T(8,128)S(1)} %gains.1.gains_hbm, f32[8,2,64,512]{3,2,1,0:T(8,128)} %all-to-all-done.refs_0_), custom_call_target="tpu_custom_call" | custom-call | tf_op jit(solution)/shard_map/multiples/pallas_call | solution.py:362
  56.1 4.5 %all-to-all-start.1 = ((f32[32,2,64,128]{3,2,1,0:T(8,128)}), f32[32,2,64,128]{3,2,1,0:T(8,128)}, u32[]{:S(2)}, u32[]{:S(2)}) async-start(f32[32,2,64,128]{3,2,1,0:T(8,128)} %bitcast.20), calls=%async_computation.1 | async-start | bytes 4194304 | tf_op jit(solution)/shard_map/all_to_all | solution.py:393
  60.8 2.6 %collective-permute-start.12 = (f32[2,64,512]{2,1,0:T(8,128)}, f32[2,64,512]{2,1,0:T(8,128)S(1)}, u32[]{:S(2)}, u32[]{:S(2)}) collective-permute-start(f32[2,64,512]{2,1,0:T(8,128)} %get-tuple-element.54), channel_id=1, source_target_pairs={{0,6},{1,7},{2,4},{3,5},{4,2},{5,3},{6,0},{7,1},{8,14},{9,15},{10,... | collective-permute-start | bytes 786440 | tf_op jit(solution)/shard_map/ppermute | solution.py:280
  63.4 26.5 %collective-permute-done.12.refs_5_ = f32[2,64,512]{2,1,0:T(8,128)S(1)} collective-permute-done((f32[2,64,512]{2,1,0:T(8,128)}, f32[2,64,512]{2,1,0:T(8,128)S(1)}, u32[]{:S(2)}, u32[]{:S(2)}) %collective-permute-start.12) | collective-permute-done | bytes 262176 | tf_op jit(solution)/shard_map/ppermute | solution.py:280
  89.9 6.0 %collective-permute-done.13.refs_6_ = f32[2,64,512]{2,1,0:T(8,128)S(1)} collective-permute-done((f32[2,64,512]{2,1,0:T(8,128)}, f32[2,64,512]{2,1,0:T(8,128)S(1)}, u32[]{:S(2)}, u32[]{:S(2)}) %collective-permute-start.13) | collective-permute-done | bytes 262176 | tf_op jit(solution)/shard_map/ppermute | solution.py:280
  96.0 12.1 %multiples.3 = f32[4,8,2,64,128]{4,3,2,1,0:T(8,128)} custom-call(s32[4]{0:T(128)S(1)} %copy-done.1, s32[512,1]{1,0:T(8,128)S(1)} %copy.16.column_ref, s32[1,512]{1,0:T(1,128)S(1)} %bitcast.19, f32[16,2,64,512]{3,2,1,0:T(8,128)} %spectra_ref.7, f32[2,512,512]{2,1,0:T(8,128)S(1)} %gains.1.gains_hbm, f32[2,64,512]{2,1,0:T(8,128)S(1)} %collective-permute-done.11.refs_0_, ...), custom_call_target="tpu_custom_call" | custom-call | tf_op jit(solution)/shard_map/multiples/pallas_call | solution.py:362
  108.0 1.8 %all-to-all-done.1 = f32[32,2,64,128]{3,2,1,0:T(8,128)} async-done(((f32[32,2,64,128]{3,2,1,0:T(8,128)}), f32[32,2,64,128]{3,2,1,0:T(8,128)}, u32[]{:S(2)}, u32[]{:S(2)}) %all-to-all-start.1) | async-done | bytes 2097184 | tf_op jit(solution)/shard_map/all_to_all | solution.py:393
  109.8 3.7 %all-to-all-start.2 = ((f32[32,2,64,128]{3,2,1,0:T(8,128)}), f32[32,2,64,128]{3,2,1,0:T(8,128)S(1)}, u32[]{:S(2)}, u32[]{:S(2)}) async-start(f32[32,2,64,128]{3,2,1,0:T(8,128)} %bitcast.21), calls=%async_computation.2 | async-start | bytes 4194304 | tf_op jit(solution)/shard_map/all_to_all | solution.py:393
  115.1 16.5 %synthesis.2.refs_0_.refs_1_.refs_2_.refs_3_ = f32[128,64,512]{2,1,0:T(8,128)} custom-call(f32[64,512]{1,0:T(8,128)S(1)} %reshape.251.table_ref, f32[128,64,512]{2,1,0:T(8,128)} %refs_3_.1, f32[128,64,512]{2,1,0:T(8,128)} %refs_3_.1, f32[128,64,512]{2,1,0:T(8,128)} %refs_3_.1, f32[128,64,512]{2,1,0:T(8,128)} %refs_3_.1, f32[4096,128]{1,0:T(8,128)} %bitcast.13.refs_4_), custom_call_target="tpu_custom_call" | custom-call | tf_op jit(solution)/shard_map/synthesis/pallas_call | solution.py:318
  131.6 30.8 %all-to-all-done.2 = f32[32,2,64,128]{3,2,1,0:T(8,128)S(1)} async-done(((f32[32,2,64,128]{3,2,1,0:T(8,128)}), f32[32,2,64,128]{3,2,1,0:T(8,128)S(1)}, u32[]{:S(2)}, u32[]{:S(2)}) %all-to-all-start.2) | async-done | bytes 2097184 | tf_op jit(solution)/shard_map/all_to_all | solution.py:393
  162.4 14.8 %synthesis.3 = f32[128,64,512]{2,1,0:T(8,128)} custom-call(f32[64,512]{1,0:T(8,128)S(1)} %reshape.250.table_ref, f32[128,64,512]{2,1,0:T(8,128)} %synthesis.2.refs_0_.refs_1_.refs_2_.refs_3_, f32[128,64,512]{2,1,0:T(8,128)} %synthesis.2.refs_0_.refs_1_.refs_2_.refs_3_, f32[128,64,512]{2,1,0:T(8,128)} %synthesis.2.refs_0_.refs_1_.refs_2_.refs_3_, ...), custom_call_target="tpu_custom_call" | custom-call | tf_op jit(solution)/shard_map/synthesis/pallas_call | solution.py:318
  (42 shorter events, 4.6 us)
Async XLA Ops:
  0.0 9.5 %copy-start.3 = (s32[128,64]{0,1:T(8,128)S(1)}, s32[128,64]{0,1:T(8,128)}, u32[]{:S(2)}) copy-start(s32[128,64]{0,1:T(8,128)} %param.10) | copy-start | bytes 98308
  0.0 6.9 %collective-permute-start.1 = (s32[64,128]{1,0:T(8,128)}, s32[64,128]{1,0:T(8,128)S(1)}, u32[]{:S(2)}, u32[]{:S(2)}) collective-permute-start(s32[64,128]{1,0:T(8,128)} %bitcast.26), channel_id=1, source_target_pairs={{0,4},{1,5},{2,6},{3,7},{4,0},{5,1},{6,2},{7,3},{8,12},{9,13},{10,... | collective-permute-start | bytes 98312 | tf_op jit(solution)/shard_map/ppermute | solution.py:280
  3.0 4.2 %collective-permute-start = (s32[64,128]{1,0:T(8,128)}, s32[64,128]{1,0:T(8,128)S(1)}, u32[]{:S(2)}, u32[]{:S(2)}) collective-permute-start(s32[64,128]{1,0:T(8,128)} %bitcast.27), channel_id=1, source_target_pairs={{0,2},{1,3},{2,0},{3,1},{4,6},{5,7},{6,4},{7,5},{8,10},{9,11},{10,... | collective-permute-start | bytes 98312 | tf_op jit(solution)/shard_map/ppermute | solution.py:280
  4.5 5.0 %collective-permute-start.2 = (s32[64,128]{1,0:T(8,128)}, s32[64,128]{1,0:T(8,128)S(1)}, u32[]{:S(2)}, u32[]{:S(2)}) collective-permute-start(s32[64,128]{1,0:T(8,128)} %bitcast.28), channel_id=1, source_target_pairs={{0,6},{1,7},{2,4},{3,5},{4,2},{5,3},{6,0},{7,1},{8,14},{9,15},{10,... | collective-permute-start | bytes 98312 | tf_op jit(solution)/shard_map/ppermute | solution.py:280
  9.5 31.0 %all-to-all-start = ((f32[8,2,64,512]{3,2,1,0:T(8,128)}), f32[8,2,64,512]{3,2,1,0:T(8,128)}, u32[]{:S(2)}, u32[]{:S(2)}) async-start(f32[8,2,64,512]{3,2,1,0:T(8,128)} %pack.2), calls=%async_computation | async-start | bytes 4194304 | tf_op jit(solution)/shard_map/all_to_all | solution.py:340
  13.9 17.8 %copy-start = (s32[512]{0:T(512)S(1)}, s32[512]{0:T(512)}, u32[]{:S(2)}) copy-start(s32[512]{0:T(512)} %param.8) | copy-start | bytes 6148
  13.9 19.6 %copy-start.2 = (f32[2,16]{1,0:T(2,128)S(1)}, f32[2,16]{1,0:T(2,128)}, u32[]{:S(2)}) copy-start(f32[2,16]{1,0:T(2,128)} %table_ref.1) | copy-start | bytes 388
  16.2 8.3 %collective-permute-start.5 = (s32[4,64,128]{2,1,0:T(8,128)S(1)}, s32[4,64,128]{2,1,0:T(8,128)S(1)}, u32[]{:S(2)}, u32[]{:S(2)}) collective-permute-start(s32[4,64,128]{2,1,0:T(8,128)S(1)} %pad_add_fusion.1), channel_id=1, source_target_pairs={{0,24},{8,16},{16,8},{24,0},{1,25},{9,17},{17,9},{25,1},{2,26},{10... | collective-permute-start | bytes 393224 | tf_op jit(solution)/shard_map/ppermute | solution.py:280
  19.9 11.6 %collective-permute-start.4 = (s32[4,64,128]{2,1,0:T(8,128)S(1)}, s32[4,64,128]{2,1,0:T(8,128)S(1)}, u32[]{:S(2)}, u32[]{:S(2)}) collective-permute-start(s32[4,64,128]{2,1,0:T(8,128)S(1)} %pad_add_fusion.1), channel_id=1, source_target_pairs={{0,16},{8,24},{16,0},{24,8},{1,17},{9,25},{17,1},{25,9},{2,18},{10... | collective-permute-start | bytes 393224 | tf_op jit(solution)/shard_map/ppermute | solution.py:280
  19.9 11.6 %collective-permute-start.3 = (s32[4,64,128]{2,1,0:T(8,128)S(1)}, s32[4,64,128]{2,1,0:T(8,128)S(1)}, u32[]{:S(2)}, u32[]{:S(2)}) collective-permute-start(s32[4,64,128]{2,1,0:T(8,128)S(1)} %pad_add_fusion.1), channel_id=1, source_target_pairs={{0,8},{8,0},{16,24},{24,16},{1,9},{9,1},{17,25},{25,17},{2,10},{10... | collective-permute-start | bytes 393224 | tf_op jit(solution)/shard_map/ppermute | solution.py:280
  31.5 12.5 %copy-start.1 = (s32[4]{0:T(128)S(1)}, s32[4]{0:T(128)}, u32[]{:S(2)}) copy-start(s32[4]{0:T(128)} %counts_ref.3) | copy-start | bytes 52
  31.6 2.0 %collective-permute-start.6 = (s32[4,4,64,128]{3,2,1,0:T(8,128)S(1)}, s32[4,4,64,128]{3,2,1,0:T(8,128)S(1)}, u32[]{:S(2)}, u32[]{:S(2)}) collective-permute-start(s32[4,4,64,128]{3,2,1,0:T(8,128)S(1)} %pad_add_fusion.near_ref), channel_id=1, source_target_pairs={{0,1},{1,0},{2,3},{3,2},{4,5},{5,4},{6,7},{7,6},{8,9},{9,8},{10,11... | collective-permute-start | bytes 1572872 | tf_op jit(solution)/shard_map/ppermute | solution.py:280
  40.5 15.2 %collective-permute-start.7 = (f32[2,64,512]{2,1,0:T(8,128)}, f32[2,64,512]{2,1,0:T(8,128)S(1)}, u32[]{:S(2)}, u32[]{:S(2)}) collective-permute-start(f32[2,64,512]{2,1,0:T(8,128)} %get-tuple-element.44), channel_id=1, source_target_pairs={{0,2},{1,3},{2,0},{3,1},{4,6},{5,7},{6,4},{7,5},{8,10},{9,11},{10,... | collective-permute-start | bytes 786440 | tf_op jit(solution)/shard_map/ppermute | solution.py:280
  41.0 14.7 %collective-permute-start.8 = (f32[2,64,512]{2,1,0:T(8,128)}, f32[2,64,512]{2,1,0:T(8,128)S(1)}, u32[]{:S(2)}, u32[]{:S(2)}) collective-permute-start(f32[2,64,512]{2,1,0:T(8,128)} %get-tuple-element.45), channel_id=1, source_target_pairs={{0,3},{1,2},{2,1},{3,0},{4,7},{5,6},{6,5},{7,4},{8,11},{9,10},{10,... | collective-permute-start | bytes 786440 | tf_op jit(solution)/shard_map/ppermute | solution.py:280
  41.0 14.7 %collective-permute-start.9 = (f32[2,64,512]{2,1,0:T(8,128)}, f32[2,64,512]{2,1,0:T(8,128)S(1)}, u32[]{:S(2)}, u32[]{:S(2)}) collective-permute-start(f32[2,64,512]{2,1,0:T(8,128)} %get-tuple-element.46), channel_id=1, source_target_pairs={{0,4},{1,5},{2,6},{3,7},{4,0},{5,1},{6,2},{7,3},{8,12},{9,13},{10,... | collective-permute-start | bytes 786440 | tf_op jit(solution)/shard_map/ppermute | solution.py:280
  41.7 14.4 %collective-permute-start.10 = (f32[2,64,512]{2,1,0:T(8,128)}, f32[2,64,512]{2,1,0:T(8,128)S(1)}, u32[]{:S(2)}, u32[]{:S(2)}) collective-permute-start(f32[2,64,512]{2,1,0:T(8,128)} %get-tuple-element.47), channel_id=1, source_target_pairs={{0,5},{1,4},{2,7},{3,6},{4,1},{5,0},{6,3},{7,2},{8,13},{9,12},{10,... | collective-permute-start | bytes 786440 | tf_op jit(solution)/shard_map/ppermute | solution.py:280
  56.1 53.7 %all-to-all-start.1 = ((f32[32,2,64,128]{3,2,1,0:T(8,128)}), f32[32,2,64,128]{3,2,1,0:T(8,128)}, u32[]{:S(2)}, u32[]{:S(2)}) async-start(f32[32,2,64,128]{3,2,1,0:T(8,128)} %bitcast.20), calls=%async_computation.1 | async-start | bytes 4194304 | tf_op jit(solution)/shard_map/all_to_all | solution.py:393
  60.6 2.8 %collective-permute-start.11 = (f32[2,64,512]{2,1,0:T(8,128)}, f32[2,64,512]{2,1,0:T(8,128)S(1)}, u32[]{:S(2)}, u32[]{:S(2)}) collective-permute-start(f32[2,64,512]{2,1,0:T(8,128)} %get-tuple-element.49), channel_id=1, source_target_pairs={{0,1},{1,0},{2,3},{3,2},{4,5},{5,4},{6,7},{7,6},{8,9},{9,8},{10,11... | collective-permute-start | bytes 786440 | tf_op jit(solution)/shard_map/ppermute | solution.py:280
  60.8 29.1 %collective-permute-start.12 = (f32[2,64,512]{2,1,0:T(8,128)}, f32[2,64,512]{2,1,0:T(8,128)S(1)}, u32[]{:S(2)}, u32[]{:S(2)}) collective-permute-start(f32[2,64,512]{2,1,0:T(8,128)} %get-tuple-element.54), channel_id=1, source_target_pairs={{0,6},{1,7},{2,4},{3,5},{4,2},{5,3},{6,0},{7,1},{8,14},{9,15},{10,... | collective-permute-start | bytes 786440 | tf_op jit(solution)/shard_map/ppermute | solution.py:280
  63.4 32.5 %collective-permute-start.13 = (f32[2,64,512]{2,1,0:T(8,128)}, f32[2,64,512]{2,1,0:T(8,128)S(1)}, u32[]{:S(2)}, u32[]{:S(2)}) collective-permute-start(f32[2,64,512]{2,1,0:T(8,128)} %get-tuple-element.55), channel_id=1, source_target_pairs={{0,7},{1,6},{2,5},{3,4},{4,3},{5,2},{6,1},{7,0},{8,15},{9,14},{10,... | collective-permute-start | bytes 786440 | tf_op jit(solution)/shard_map/ppermute | solution.py:280
  109.8 52.6 %all-to-all-start.2 = ((f32[32,2,64,128]{3,2,1,0:T(8,128)}), f32[32,2,64,128]{3,2,1,0:T(8,128)S(1)}, u32[]{:S(2)}, u32[]{:S(2)}) async-start(f32[32,2,64,128]{3,2,1,0:T(8,128)} %bitcast.21), calls=%async_computation.2 | async-start | bytes 4194304 | tf_op jit(solution)/shard_map/all_to_all | solution.py:393

commit v4 on v2

--- a/solution.py
+++ b/solution.py
@@ -86,8 +86,10 @@
 
 
 def multiples_kernel(counts_ref, column_ref, row_ref, spectra_ref, gains_hbm, *refs, first_slot):
-    tiles, (out, result, data, gains, u, w, y1, y2, tile_sems, gain_sem, out_sems) = refs[:-11], refs[-11:]
+    result, data, gains, u, w, y1, y2, tile_sems, gain_sem, out_sems = refs[-10:]
     source_tiles, receiver_tiles, _, receiver_tile, source_tile = result.shape
+    halves = out_sems.shape[0]
+    tiles, outs = refs[: -10 - halves], refs[-10 - halves : -10]
     side = data.shape[3]
     pick = min(PICK, side)
     rank = lax.axis_index("rcv")
@@ -95,9 +97,13 @@
     live = first_slot + rank < counts_ref[plane]
 
     def send(first, count):
-        tiles_of = pl.ds(first, count)
+        span = pl.ds(first, count)
+        size = receiver_tile // halves
         return [
-            pltpu.make_async_copy(result.at[a, tiles_of], out.at[a, tiles_of], out_sems.at[a, first // count])
+            pltpu.make_async_copy(
+                result.at[a, span, :, pl.ds(h * size, size)], outs[h].at[a, span], out_sems.at[h, a, first // count]
+            )
+            for h in range(halves)
             for a in range(source_tiles)
         ]
 
@@ -193,26 +199,22 @@
         copy.wait()
 
 
-def synthesis_kernel(table_ref, base_ref, *refs, receiver_tile):
-    coefs, (out_ref, coef_ref, lines, tables, sems) = refs[:-5], refs[-5:]
+def synthesis_kernel(table_ref, *refs, receiver_tile, pieces, first_block):
+    bases, coef_hbm = refs[:pieces], refs[pieces]
+    out_ref, stage, out_sems, coef_ref, lines, tables, sem = refs[-7:]
     depth = table_ref.shape[0]
     source_tile = coef_ref.shape[1]
     first = pl.multiple_of(pl.program_id(0) * ROWS, ROWS)
 
     @pl.when(pl.program_id(0) == 0)
     def _():
-        size = coef_ref.shape[0] // len(coefs)
-        copies = [
-            pltpu.make_async_copy(coef, coef_ref.at[pl.ds(n * size, size)], sems.at[n]) for n, coef in enumerate(coefs)
-        ]
-        for copy in copies:
-            copy.start()
+        copy = pltpu.make_async_copy(coef_hbm, coef_ref, sem)
+        copy.start()
         high, low = split(table_ref[...])
         tables[:depth, :] = high
         tables[depth : 2 * depth, :] = high
         tables[2 * depth :, :] = low
-        for copy in copies:
-            copy.wait()
+        copy.wait()
 
     for r in range(ROWS):
         column = coef_ref[pl.ds(first + r, depth, stride=receiver_tile), :]
@@ -221,12 +223,39 @@
         for g in range(lines.shape[0]):
             lines[g, pl.ds(r, source_tile, stride=ROWS), :] = both[g * LANES : (g + 1) * LANES].T
 
-    size = 32
-    for start in range(0, source_tile, size):
-        rows = slice(start * ROWS, (start + size) * ROWS)
-        both = jnp.concatenate([lines[g, rows, :] for g in range(lines.shape[0])], axis=1).astype(jnp.bfloat16)
-        total = mm(jnp.concatenate([both, both[:, :depth]], axis=1), tables[...])
-        out_ref[start : start + size] = base_ref[start : start + size] - total.reshape(size, ROWS, -1)
+    step = pl.program_id(0)
+    slot = step % 2
+    piece = source_tile // pieces
+
+    def leave(at, k):
+        rows = pl.ds(pl.multiple_of((at + first_block) * ROWS, ROWS), ROWS)
+        return pltpu.make_async_copy(
+            stage.at[at % 2, k], out_ref.at[pl.ds(k * piece, piece), rows], out_sems.at[at % 2, k]
+        )
+
+    @pl.when(step >= 2)
+    def _():
+        for k in range(pieces):
+            leave(step - 2, k).wait()
+
+    size = min(32, piece)
+    for k in range(pieces):
+        for start in range(0, piece, size):
+            rows = slice((k * piece + start) * ROWS, (k * piece + start + size) * ROWS)
+            both = jnp.concatenate([lines[g, rows, :] for g in range(lines.shape[0])], axis=1).astype(jnp.bfloat16)
+            total = mm(jnp.concatenate([both, both[:, :depth]], axis=1), tables[...])
+            span = slice(start, start + size)
+            stage[slot, k, span] = bases[k][span] - total.reshape(size, ROWS, -1)
+        leave(step, k).start()
+
+    @pl.when(step == pl.num_programs(0) - 1)
+    def _():
+        for k in range(pieces):
+            leave(step, k).wait()
+
+            @pl.when(step >= 1)
+            def _():
+                leave(step - 1, k).wait()
 
 
 def params(mebibytes):
@@ -271,24 +300,32 @@
             name="pack",
         )(in_hbm(slots))
 
-    def synthesis(coefs, table, base):
+    def synthesis(coef, table, base, half, halves, out):
         depth = table.shape[0]
-        block = pl.BlockSpec((source_tile, ROWS, samples), lambda n: (0, n, 0))
+        pieces = 4
+        piece = (source_tile // pieces, ROWS, samples)
+        rows = receiver_tile // halves
+        first = half * rows // ROWS
+        blocks = [pl.BlockSpec(piece, lambda n, k=k: (k, n + first, 0)) for k in range(pieces)]
+        others = [] if out is None else [in_hbm(out)]
         return pl.pallas_call(
-            functools.partial(synthesis_kernel, receiver_tile=receiver_tile),
+            functools.partial(synthesis_kernel, receiver_tile=rows, pieces=pieces, first_block=first),
             out_shape=pltpu.HBM(recorded.shape, jnp.float32),
-            grid=(receiver_tile // ROWS,),
-            in_specs=[whole_in(), block] + [hbm] * len(coefs),
-            out_specs=block,
+            grid=(rows // ROWS,),
+            in_specs=[whole_in()] + blocks + [hbm] * (1 + len(others)),
+            out_specs=hbm,
             scratch_shapes=[
-                pltpu.VMEM((depth * receiver_tile, source_tile), jnp.float32),
+                pltpu.VMEM((2, pieces) + piece, jnp.float32),
+                pltpu.SemaphoreType.DMA((2, pieces)),
+                pltpu.VMEM((depth * rows, source_tile), jnp.float32),
                 pltpu.VMEM((2 * depth // LANES, source_tile * ROWS, LANES), jnp.float32),
                 pltpu.VMEM((3 * depth, samples), jnp.bfloat16),
-                pltpu.SemaphoreType.DMA((len(coefs),)),
+                pltpu.SemaphoreType.DMA,
             ],
-            compiler_params=params(24),
+            input_output_aliases={2 + pieces: 0} if others else {},
+            compiler_params=params(40),
             name="synthesis",
-        )(table, in_hbm(base), *coefs)
+        )(table, *[in_hbm(base)] * pieces, coef, *others)
 
     tile = gain_index.T
     near = jnp.stack([tile if n == 0 else exchange(tile, "rcv", 2 * n) for n in range(rcv_count // 2)])
@@ -311,16 +348,18 @@
     )(gain_table, near, far, column)
 
     for packed in later:
-        gathered[-1][0], *packed = lax.optimization_barrier((gathered[-1][0], *packed))
+        gains, *packed = lax.optimization_barrier((gains, *packed))
         gathered.append([exchange(tile, "rcv", n + 1) for n, tile in enumerate(packed)])
 
     results = []
     for part in range(parts):
+        halves = 2 if part == parts - 1 else 1
+        rows = receiver_tile // halves
         result = pl.pallas_call(
             functools.partial(multiples_kernel, first_slot=part * rcv_count),
-            out_shape=pltpu.HBM((freq_count, rcv_count, 2, receiver_tile, source_tile), jnp.float32),
+            out_shape=[pltpu.HBM((freq_count, rcv_count, 2, rows, source_tile), jnp.float32)] * halves,
             in_specs=[smem, whole_in(), whole_in()] + [hbm] * (2 + len(gathered[part])),
-            out_specs=hbm,
+            out_specs=[hbm] * halves,
             scratch_shapes=[
                 pltpu.VMEM((freq_count, rcv_count, 2, receiver_tile, source_tile), jnp.float32),
                 pltpu.VMEM((rcv_count, 2, receiver_tile, side), jnp.float32),
@@ -331,27 +370,36 @@
                 pltpu.VMEM((side, 2 * side), jnp.float32),
                 pltpu.SemaphoreType.DMA((rcv_count,)),
                 pltpu.SemaphoreType.DMA,
-                pltpu.SemaphoreType.DMA((freq_count, rcv_count)),
+                pltpu.SemaphoreType.DMA((halves, freq_count, rcv_count)),
             ],
             compiler_params=params(32),
             name="multiples",
         )(counts, column, row, in_hbm(spectra), gains, *gathered[part])
+        result = list(result)
         if part < parts - 1:
             nearest = slice(1, 5)
-            result, *gathered[part + 1][nearest] = lax.optimization_barrier((result, *gathered[part + 1][nearest]))
-        results.append(result.reshape((senders,) + result.shape[2:]))
+            result[0], *gathered[part + 1][nearest] = lax.optimization_barrier(
+                (result[0], *gathered[part + 1][nearest])
+            )
+        results.append([half.reshape((senders,) + half.shape[2:]) for half in result])
 
     before = jnp.arange(freq_count)[None, :] < jnp.arange(freq_count)[:, None]
     offsets = jnp.sum(jnp.where(before, counts[None, :], 0), axis=1)
     ranks = jnp.arange(rcv_count, dtype=jnp.int32)
     base = recorded
-    for part, result in enumerate(results):
-        coefs = lax.all_to_all(result, ("freq", "rcv"), split_axis=0, concat_axis=0, tiled=True)
+    for part, halves in enumerate(results):
+        came = [
+            lax.all_to_all(half, ("freq", "rcv"), split_axis=0, concat_axis=0, tiled=True).reshape(-1, source_tile)
+            for half in halves
+        ]
         bins = offsets[:, None] + part * rcv_count + ranks[None, :] + 1
         table = time_table(bins.reshape(-1), samples).reshape(-1, samples)
         if part < parts - 1:
-            coefs, _ = lax.optimization_barrier((coefs, results[part + 1]))
-        base = synthesis([coefs.reshape(-1, source_tile)], table, base)
+            came[0], _ = lax.optimization_barrier((came[0], results[part + 1][0]))
+        out = None
+        for n, coef in enumerate(came):
+            out = synthesis(coef, table, base, n, len(came), out)
+        base = out
     return base
 
 

time: 180 us -> 198 us (1.10)
  blocking collectives: 0 us -> 91.7 us
  waiting for transfers between devices: 86.8 us -> 24.9 us
  Pallas kernels: 62.7 us -> 52.2 us
    all_to_all x0 -> x2, blocking collectives: none -> 91.7 us  [on_device(): lax.all_to_all(half, ('freq', 'rcv'), split_axis=0, concat_axis=0, tiled=...]
    all_to_all x2 -> x1, waiting for transfers between devices: 32 us -> 1.95 us  [on_device(): lax.all_to_all(half, ('freq', 'rcv'), split_axis=0, concat_axis=0, tiled=...]
    ppermute x14, waiting for transfers between devices: 46 us -> 23 us  [exchange(): lax.ppermute(array, axis, [(i, i ^ distance) for i in range(lax.axis_size...]
    all_to_all x1, waiting for transfers between devices: 8.75 us -> 0.01 us  [on_device(): lax.all_to_all(packed, 'rcv', split_axis=0, concat_axis=0, tiled=True)]
    pallas_call x2, Pallas kernels: 22.7 us -> 14.6 us  [on_device(): pl.pallas_call(functools.partial(multiples_kernel, first_slot=part * rcv_...]
    all_to_all x2 -> x1, starting transfers between devices: 7.8 us -> 3.67 us  [on_device(): lax.all_to_all(half, ('freq', 'rcv'), split_axis=0, concat_axis=0, tiled=...]
    ppermute x14, starting transfers between devices: 15.4 us -> 18.6 us  [exchange(): lax.ppermute(array, axis, [(i, i ^ distance) for i in range(lax.axis_size...]
    pallas_call x2 -> x3, Pallas kernels: 32.8 us -> 30.4 us  [synthesis(): pl.pallas_call(functools.partial(synthesis_kernel, receiver_tile=rows, pi...]
  transfers between devices with their start and end apart: 17 -> 16, of which waited for: 9 -> 8; matrix products, arithmetic and copies ran while one was open for 1% -> 1% of each run, Pallas kernels for 26% -> 21%
where the time goes in v4:
time: 198 us
  blocking collectives  91.7 us (46%)
  Pallas kernels  52.2 us (26%)
  starting transfers between devices  26.7 us (13%)
  waiting for transfers between devices  24.9 us (13%)
    all_to_all x2, blocking collectives, on_device(): lax.all_to_all(half, ('freq', 'rcv'), split_axis=0, concat_axis=0, tiled=...  91.7 us
    pallas_call x3, Pallas kernels, synthesis(): pl.pallas_call(functools.partial(synthesis_kernel, receiver_tile=rows, pi...  30.4 us
    ppermute x14, waiting for transfers between devices, exchange(): lax.ppermute(array, axis, [(i, i ^ distance) for i in range(lax.axis_size...  23 us
    ppermute x14, starting transfers between devices, exchange(): lax.ppermute(array, axis, [(i, i ^ distance) for i in range(lax.axis_size...  18.6 us
    pallas_call x2, Pallas kernels, on_device(): pl.pallas_call(functools.partial(multiples_kernel, first_slot=part * rcv_...  14.6 us
    pallas_call x2, Pallas kernels, pack(): pl.pallas_call(functools.partial(pack_kernel, first_slot=part * rcv_count...  4.72 us
    all_to_all x1, starting transfers between devices, on_device(): lax.all_to_all(packed, 'rcv', split_axis=0, concat_axis=0, tiled=True)  4.36 us
  transfers between devices with their start and end apart: 16, of which 8 were waited for; matrix products, arithmetic and copies ran while one was open for 1% of the time, Pallas kernels for 21%

profile of v4, /device:TPU:0, one launch (start us, length us, event | category | flops | bytes accessed | tf_op | source)
XLA Modules:
  0.0 197.8 jit_solution(10003300247642879319)
XLA Ops:
  0.0 3.0 %collective-permute-start.1 = (s32[64,128]{1,0:T(8,128)}, s32[64,128]{1,0:T(8,128)S(1)}, u32[]{:S(2)}, u32[]{:S(2)}) collective-permute-start(s32[64,128]{1,0:T(8,128)} %bitcast.31), channel_id=1, source_target_pairs={{0,4},{1,5},{2,6},{3,7},{4,0},{5,1},{6,2},{7,3},{8,12},{9,13},{10,... | collective-permute-start | bytes 98312 | tf_op jit(solution)/shard_map/ppermute | solution.py:270
  4.5 2.4 %pack.2 = f32[8,2,64,512]{3,2,1,0:T(8,128)} custom-call(f32[16,2,64,512]{3,2,1,0:T(8,128)} %spectra_ref.7), custom_call_target="tpu_custom_call" | custom-call | tf_op jit(solution)/shard_map/pack/pallas_call | solution.py:289
  7.2 2.3 %collective-permute-done.2 = s32[64,128]{1,0:T(8,128)S(1)} collective-permute-done((s32[64,128]{1,0:T(8,128)}, s32[64,128]{1,0:T(8,128)S(1)}, u32[]{:S(2)}, u32[]{:S(2)}) %collective-permute-start.2) | collective-permute-done | bytes 32800 | tf_op jit(solution)/shard_map/ppermute | solution.py:270
  9.5 4.4 %all-to-all-start = ((f32[8,2,64,512]{3,2,1,0:T(8,128)}), f32[8,2,64,512]{3,2,1,0:T(8,128)}, u32[]{:S(2)}, u32[]{:S(2)}) async-start(f32[8,2,64,512]{3,2,1,0:T(8,128)} %pack.2), calls=%async_computation | async-start | bytes 4194304 | tf_op jit(solution)/shard_map/all_to_all | solution.py:334
  13.9 2.3 %pack.3 = (f32[2,64,512]{2,1,0:T(8,128)}, f32[2,64,512]{2,1,0:T(8,128)}, f32[2,64,512]{2,1,0:T(8,128)}, f32[2,64,512]{2,1,0:T(8,128)}, f32[2,64,512]{2,1,0:T(8,1...) custom-call(f32[16,2,64,512]{3,2,1,0:T(8,128)} %spectra_ref.7), custom_call_target="tpu_custom_call" | custom-call | tf_op jit(solution)/shard_map/pack/pallas_call | solution.py:289
  16.2 3.7 %collective-permute-start.5 = (s32[4,64,128]{2,1,0:T(8,128)S(1)}, s32[4,64,128]{2,1,0:T(8,128)S(1)}, u32[]{:S(2)}, u32[]{:S(2)}) collective-permute-start(s32[4,64,128]{2,1,0:T(8,128)S(1)} %pad_add_fusion.1), channel_id=1, source_target_pairs={{0,24},{8,16},{16,8},{24,0},{1,25},{9,17},{17,9},{25,1},{2,26},{10... | collective-permute-start | bytes 393224 | tf_op jit(solution)/shard_map/ppermute | solution.py:270
  20.7 3.8 %collective-permute-done.5 = s32[4,64,128]{2,1,0:T(8,128)S(1)} collective-permute-done((s32[4,64,128]{2,1,0:T(8,128)S(1)}, s32[4,64,128]{2,1,0:T(8,128)S(1)}, u32[]{:S(2)}, u32[]{:S(2)}) %collective-permute-start.5) | collective-permute-done | bytes 131104 | tf_op jit(solution)/shard_map/ppermute | solution.py:270
  24.5 7.0 %collective-permute-done.4 = s32[4,64,128]{2,1,0:T(8,128)S(1)} collective-permute-done((s32[4,64,128]{2,1,0:T(8,128)S(1)}, s32[4,64,128]{2,1,0:T(8,128)S(1)}, u32[]{:S(2)}, u32[]{:S(2)}) %collective-permute-start.4) | collective-permute-done | bytes 131104 | tf_op jit(solution)/shard_map/ppermute | solution.py:270
  31.8 1.7 collective-permute-done.6.far_ref
  33.6 2.5 %gains.1.gains_hbm = f32[2,512,512]{2,1,0:T(8,128)S(1)} custom-call(f32[2,16]{1,0:T(2,128)S(1)} %copy-done.3, s32[4,4,64,128]{3,2,1,0:T(8,128)S(1)} %pad_add_fusion.near_ref, s32[4,4,64,128]{3,2,1,0:T(8,128)S(1)} %collective-permute-done.6.far_ref, s32[512,1]{1,0:T(8,128)S(1)} %copy.17.column_ref), custom_call_target="tpu_custom_call" | custom-call | tf_op jit(solution)/shard_map/gains/pallas_call | solution.py:340
  36.1 1.7 collective-permute-start.7
  40.0 5.5 %collective-permute-done.7.refs_1_ = f32[2,64,512]{2,1,0:T(8,128)S(1)} collective-permute-done((f32[2,64,512]{2,1,0:T(8,128)}, f32[2,64,512]{2,1,0:T(8,128)S(1)}, u32[]{:S(2)}, u32[]{:S(2)}) %collective-permute-start.7) | collective-permute-done | bytes 262176 | tf_op jit(solution)/shard_map/ppermute | solution.py:270
  45.5 2.6 %collective-permute-start.12 = (f32[2,64,512]{2,1,0:T(8,128)}, f32[2,64,512]{2,1,0:T(8,128)}, u32[]{:S(2)}, u32[]{:S(2)}) collective-permute-start(f32[2,64,512]{2,1,0:T(8,128)} %get-tuple-element.54), channel_id=1, source_target_pairs={{0,6},{1,7},{2,4},{3,5},{4,2},{5,3},{6,0},{7,1},{8,14},{9,15},{10,... | collective-permute-start | bytes 786440 | tf_op jit(solution)/shard_map/ppermute | solution.py:270
  48.1 2.3 %collective-permute-done.8.refs_2_ = f32[2,64,512]{2,1,0:T(8,128)S(1)} collective-permute-done((f32[2,64,512]{2,1,0:T(8,128)}, f32[2,64,512]{2,1,0:T(8,128)S(1)}, u32[]{:S(2)}, u32[]{:S(2)}) %collective-permute-start.8) | collective-permute-done | bytes 262176 | tf_op jit(solution)/shard_map/ppermute | solution.py:270
  50.4 3.1 %collective-permute-start.13 = (f32[2,64,512]{2,1,0:T(8,128)}, f32[2,64,512]{2,1,0:T(8,128)}, u32[]{:S(2)}, u32[]{:S(2)}) collective-permute-start(f32[2,64,512]{2,1,0:T(8,128)} %get-tuple-element.55), channel_id=1, source_target_pairs={{0,7},{1,6},{2,5},{3,4},{4,3},{5,2},{6,1},{7,0},{8,15},{9,14},{10,... | collective-permute-start | bytes 786440 | tf_op jit(solution)/shard_map/ppermute | solution.py:270
  53.6 11.7 %multiples.2 = f32[4,8,2,64,128]{4,3,2,1,0:T(8,128)} custom-call(s32[4]{0:T(128)S(1)} %copy-done.2, s32[512,1]{1,0:T(8,128)S(1)} %copy.17.column_ref, s32[1,512]{1,0:T(1,128)S(1)} %bitcast.22, f32[16,2,64,512]{3,2,1,0:T(8,128)} %spectra_ref.7, f32[2,512,512]{2,1,0:T(8,128)S(1)} %gains.1.gains_hbm, f32[8,2,64,512]{3,2,1,0:T(8,128)} %all-to-all-done.refs_0_), custom_call_target="tpu_custom_call" | custom-call | tf_op jit(solution)/shard_map/multiples/pallas_call | solution.py:358
  65.3 3.0 %multiples.3 = (f32[4,8,2,32,128]{4,3,2,1,0:T(8,128)}, f32[4,8,2,32,128]{4,3,2,1,0:T(8,128)}) custom-call(s32[4]{0:T(128)S(1)} %copy-done.2, s32[512,1]{1,0:T(8,128)S(1)} %copy.17.column_ref, s32[1,512]{1,0:T(1,128)S(1)} %bitcast.23, f32[16,2,64,512]{3,2,1,0:T(8,128)} %spectra_ref.7, f32[2,512,512]{2,1,0:T(8,128)S(1)} %gains.1.gains_hbm, ...), custom_call_target="tpu_custom_call" | custom-call | tf_op jit(solution)/shard_map/multiples/pallas_call | solution.py:358
  68.3 39.6 %all_to_all.20 = f32[32,2,32,128]{3,2,1,0:T(8,128)} all-to-all(f32[32,2,32,128]{3,2,1,0:T(8,128)} %bitcast.26), channel_id=1, replica_groups=mesh['freq'=4,'rcv'=8] {'freq','rcv'}, dimensions={0} | all-to-all | bytes 2097152 | tf_op jit(solution)/shard_map/all_to_all | solution.py:392
  107.9 52.1 %all_to_all.21 = f32[32,2,64,128]{3,2,1,0:T(8,128)S(1)} all-to-all(f32[32,2,64,128]{3,2,1,0:T(8,128)S(1)} %bitcast.24), channel_id=1, replica_groups=mesh['freq'=4,'rcv'=8] {'freq','rcv'}, dimensions={0} | all-to-all | bytes 4194304 | tf_op jit(solution)/shard_map/all_to_all | solution.py:392
  160.0 3.7 %all-to-all-start.2 = ((f32[32,2,32,128]{3,2,1,0:T(8,128)}), f32[32,2,32,128]{3,2,1,0:T(8,128)S(1)}, u32[]{:S(2)}, u32[]{:S(2)}) async-start(f32[32,2,32,128]{3,2,1,0:T(8,128)} %bitcast.25), calls=%async_computation.2 | async-start | bytes 2097152 | tf_op jit(solution)/shard_map/all_to_all | solution.py:392
  165.3 14.9 %synthesis.3.refs_0_.refs_1_.refs_2_.refs_3_ = f32[128,64,512]{2,1,0:T(8,128)} custom-call(f32[64,512]{1,0:T(8,128)S(1)} %reshape.257.table_ref, f32[128,64,512]{2,1,0:T(8,128)} %refs_3_.1, f32[128,64,512]{2,1,0:T(8,128)} %refs_3_.1, f32[128,64,512]{2,1,0:T(8,128)} %refs_3_.1, f32[128,64,512]{2,1,0:T(8,128)} %refs_3_.1, f32[4096,128]{1,0:T(8,128)S(1)} %bitcast.18), custom_call_target="tpu_custom_call" | custom-call | tf_op jit(solution)/shard_map/synthesis/pallas_call | solution.py:311
  180.2 7.7 %synthesis.4.refs_5_ = f32[128,64,512]{2,1,0:T(8,128)} custom-call(f32[64,512]{1,0:T(8,128)S(1)} %reshape.256.table_ref, f32[128,64,512]{2,1,0:T(8,128)} %synthesis.3.refs_0_.refs_1_.refs_2_.refs_3_, f32[128,64,512]{2,1,0:T(8,128)} %synthesis.3.refs_0_.refs_1_.refs_2_.refs_3_, f32[128,64,512]{2,1,0:T(8,128)} %synthesis.3.refs_0_.refs_1_.refs_2_.refs_3_, ...), custom_call_target="tpu_custom_call" | custom-call | tf_op jit(solution)/shard_map/synthesis/pallas_call | solution.py:311
  188.0 1.9 all-to-all-done.2
  189.9 7.7 %synthesis.5 = f32[128,64,512]{2,1,0:T(8,128)} custom-call(f32[64,512]{1,0:T(8,128)S(1)} %reshape.256.table_ref, f32[128,64,512]{2,1,0:T(8,128)} %synthesis.3.refs_0_.refs_1_.refs_2_.refs_3_, f32[128,64,512]{2,1,0:T(8,128)} %synthesis.3.refs_0_.refs_1_.refs_2_.refs_3_, ...), custom_call_target="tpu_custom_call", output_to_operand_aliasing={{}: (6, {})} | custom-call | tf_op jit(solution)/shard_map/synthesis/pallas_call | solution.py:311
  (47 shorter events, 6.6 us)
Async XLA Ops:
  0.0 9.5 %copy-start.5 = (s32[128,64]{0,1:T(8,128)S(1)}, s32[128,64]{0,1:T(8,128)}, u32[]{:S(2)}) copy-start(s32[128,64]{0,1:T(8,128)} %param.10) | copy-start | bytes 98308
  0.0 6.9 %collective-permute-start.1 = (s32[64,128]{1,0:T(8,128)}, s32[64,128]{1,0:T(8,128)S(1)}, u32[]{:S(2)}, u32[]{:S(2)}) collective-permute-start(s32[64,128]{1,0:T(8,128)} %bitcast.31), channel_id=1, source_target_pairs={{0,4},{1,5},{2,6},{3,7},{4,0},{5,1},{6,2},{7,3},{8,12},{9,13},{10,... | collective-permute-start | bytes 98312 | tf_op jit(solution)/shard_map/ppermute | solution.py:270
  3.0 4.2 %collective-permute-start = (s32[64,128]{1,0:T(8,128)}, s32[64,128]{1,0:T(8,128)S(1)}, u32[]{:S(2)}, u32[]{:S(2)}) collective-permute-start(s32[64,128]{1,0:T(8,128)} %bitcast.32), channel_id=1, source_target_pairs={{0,2},{1,3},{2,0},{3,1},{4,6},{5,7},{6,4},{7,5},{8,10},{9,11},{10,... | collective-permute-start | bytes 98312 | tf_op jit(solution)/shard_map/ppermute | solution.py:270
  4.5 5.0 %collective-permute-start.2 = (s32[64,128]{1,0:T(8,128)}, s32[64,128]{1,0:T(8,128)S(1)}, u32[]{:S(2)}, u32[]{:S(2)}) collective-permute-start(s32[64,128]{1,0:T(8,128)} %bitcast.33), channel_id=1, source_target_pairs={{0,6},{1,7},{2,4},{3,5},{4,2},{5,3},{6,0},{7,1},{8,14},{9,15},{10,... | collective-permute-start | bytes 98312 | tf_op jit(solution)/shard_map/ppermute | solution.py:270
  9.5 22.2 %copy-start.1 = (s32[512]{0:T(512)S(1)}, s32[512]{0:T(512)}, u32[]{:S(2)}) copy-start(s32[512]{0:T(512)} %param.8) | copy-start | bytes 6148
  9.5 24.0 %copy-start.3 = (f32[2,16]{1,0:T(2,128)S(1)}, f32[2,16]{1,0:T(2,128)}, u32[]{:S(2)}) copy-start(f32[2,16]{1,0:T(2,128)} %table_ref.1) | copy-start | bytes 388
  9.5 44.0 %all-to-all-start = ((f32[8,2,64,512]{3,2,1,0:T(8,128)}), f32[8,2,64,512]{3,2,1,0:T(8,128)}, u32[]{:S(2)}, u32[]{:S(2)}) async-start(f32[8,2,64,512]{3,2,1,0:T(8,128)} %pack.2), calls=%async_computation | async-start | bytes 4194304 | tf_op jit(solution)/shard_map/all_to_all | solution.py:334
  13.9 39.7 %copy-start.2 = (s32[4]{0:T(128)S(1)}, s32[4]{0:T(128)}, u32[]{:S(2)}) copy-start(s32[4]{0:T(128)} %counts_ref.3) | copy-start | bytes 52
  16.2 8.3 %collective-permute-start.5 = (s32[4,64,128]{2,1,0:T(8,128)S(1)}, s32[4,64,128]{2,1,0:T(8,128)S(1)}, u32[]{:S(2)}, u32[]{:S(2)}) collective-permute-start(s32[4,64,128]{2,1,0:T(8,128)S(1)} %pad_add_fusion.1), channel_id=1, source_target_pairs={{0,24},{8,16},{16,8},{24,0},{1,25},{9,17},{17,9},{25,1},{2,26},{10... | collective-permute-start | bytes 393224 | tf_op jit(solution)/shard_map/ppermute | solution.py:270
  19.9 11.6 %collective-permute-start.4 = (s32[4,64,128]{2,1,0:T(8,128)S(1)}, s32[4,64,128]{2,1,0:T(8,128)S(1)}, u32[]{:S(2)}, u32[]{:S(2)}) collective-permute-start(s32[4,64,128]{2,1,0:T(8,128)S(1)} %pad_add_fusion.1), channel_id=1, source_target_pairs={{0,16},{8,24},{16,0},{24,8},{1,17},{9,25},{17,1},{25,9},{2,18},{10... | collective-permute-start | bytes 393224 | tf_op jit(solution)/shard_map/ppermute | solution.py:270
  19.9 11.6 %collective-permute-start.3 = (s32[4,64,128]{2,1,0:T(8,128)S(1)}, s32[4,64,128]{2,1,0:T(8,128)S(1)}, u32[]{:S(2)}, u32[]{:S(2)}) collective-permute-start(s32[4,64,128]{2,1,0:T(8,128)S(1)} %pad_add_fusion.1), channel_id=1, source_target_pairs={{0,8},{8,0},{16,24},{24,16},{1,9},{9,1},{17,25},{25,17},{2,10},{10... | collective-permute-start | bytes 393224 | tf_op jit(solution)/shard_map/ppermute | solution.py:270
  31.6 2.0 collective-permute-start.6
  36.1 9.4 %collective-permute-start.7 = (f32[2,64,512]{2,1,0:T(8,128)}, f32[2,64,512]{2,1,0:T(8,128)S(1)}, u32[]{:S(2)}, u32[]{:S(2)}) collective-permute-start(f32[2,64,512]{2,1,0:T(8,128)} %get-tuple-element.44), channel_id=1, source_target_pairs={{0,2},{1,3},{2,0},{3,1},{4,6},{5,7},{6,4},{7,5},{8,10},{9,11},{10,... | collective-permute-start | bytes 786440 | tf_op jit(solution)/shard_map/ppermute | solution.py:270
  37.8 12.6 %collective-permute-start.8 = (f32[2,64,512]{2,1,0:T(8,128)}, f32[2,64,512]{2,1,0:T(8,128)S(1)}, u32[]{:S(2)}, u32[]{:S(2)}) collective-permute-start(f32[2,64,512]{2,1,0:T(8,128)} %get-tuple-element.45), channel_id=1, source_target_pairs={{0,3},{1,2},{2,1},{3,0},{4,7},{5,6},{6,5},{7,4},{8,11},{9,10},{10,... | collective-permute-start | bytes 786440 | tf_op jit(solution)/shard_map/ppermute | solution.py:270
  37.8 27.4 %collective-permute-start.9 = (f32[2,64,512]{2,1,0:T(8,128)}, f32[2,64,512]{2,1,0:T(8,128)S(1)}, u32[]{:S(2)}, u32[]{:S(2)}) collective-permute-start(f32[2,64,512]{2,1,0:T(8,128)} %get-tuple-element.46), channel_id=1, source_target_pairs={{0,4},{1,5},{2,6},{3,7},{4,0},{5,1},{6,2},{7,3},{8,12},{9,13},{10,... | collective-permute-start | bytes 786440 | tf_op jit(solution)/shard_map/ppermute | solution.py:270
  39.4 25.9 %collective-permute-start.10 = (f32[2,64,512]{2,1,0:T(8,128)}, f32[2,64,512]{2,1,0:T(8,128)S(1)}, u32[]{:S(2)}, u32[]{:S(2)}) collective-permute-start(f32[2,64,512]{2,1,0:T(8,128)} %get-tuple-element.47), channel_id=1, source_target_pairs={{0,5},{1,4},{2,7},{3,6},{4,1},{5,0},{6,3},{7,2},{8,13},{9,12},{10,... | collective-permute-start | bytes 786440 | tf_op jit(solution)/shard_map/ppermute | solution.py:270
  39.6 25.7 %collective-permute-start.11 = (f32[2,64,512]{2,1,0:T(8,128)}, f32[2,64,512]{2,1,0:T(8,128)}, u32[]{:S(2)}, u32[]{:S(2)}) collective-permute-start(f32[2,64,512]{2,1,0:T(8,128)} %get-tuple-element.49), channel_id=1, source_target_pairs={{0,1},{1,0},{2,3},{3,2},{4,5},{5,4},{6,7},{7,6},{8,9},{9,8},{10,11... | collective-permute-start | bytes 786440 | tf_op jit(solution)/shard_map/ppermute | solution.py:270
  45.5 19.8 %collective-permute-start.12 = (f32[2,64,512]{2,1,0:T(8,128)}, f32[2,64,512]{2,1,0:T(8,128)}, u32[]{:S(2)}, u32[]{:S(2)}) collective-permute-start(f32[2,64,512]{2,1,0:T(8,128)} %get-tuple-element.54), channel_id=1, source_target_pairs={{0,6},{1,7},{2,4},{3,5},{4,2},{5,3},{6,0},{7,1},{8,14},{9,15},{10,... | collective-permute-start | bytes 786440 | tf_op jit(solution)/shard_map/ppermute | solution.py:270
  50.4 14.9 %collective-permute-start.13 = (f32[2,64,512]{2,1,0:T(8,128)}, f32[2,64,512]{2,1,0:T(8,128)}, u32[]{:S(2)}, u32[]{:S(2)}) collective-permute-start(f32[2,64,512]{2,1,0:T(8,128)} %get-tuple-element.55), channel_id=1, source_target_pairs={{0,7},{1,6},{2,5},{3,4},{4,3},{5,2},{6,1},{7,0},{8,15},{9,14},{10,... | collective-permute-start | bytes 786440 | tf_op jit(solution)/shard_map/ppermute | solution.py:270
  65.3 42.6 %copy-start.4 = (f32[4,8,2,64,128]{4,3,2,1,0:T(8,128)S(1)}, f32[4,8,2,64,128]{4,3,2,1,0:T(8,128)}, u32[]{:S(2)}) copy-start(f32[4,8,2,64,128]{4,3,2,1,0:T(8,128)} %multiples.2) | copy-start | bytes 6291460
  160.0 29.9 %all-to-all-start.2 = ((f32[32,2,32,128]{3,2,1,0:T(8,128)}), f32[32,2,32,128]{3,2,1,0:T(8,128)S(1)}, u32[]{:S(2)}, u32[]{:S(2)}) async-start(f32[32,2,32,128]{3,2,1,0:T(8,128)} %bitcast.25), calls=%async_computation.2 | async-start | bytes 2097152 | tf_op jit(solution)/shard_map/all_to_all | solution.py:392
  165.3 15.0 %copy-start = (f32[32,2,32,128]{3,2,1,0:T(8,128)S(1)}, f32[32,2,32,128]{3,2,1,0:T(8,128)}, u32[]{:S(2)}) copy-start(f32[32,2,32,128]{3,2,1,0:T(8,128)} %all_to_all.20) | copy-start | bytes 3145732

commit v5 on v4

--- a/solution.py
+++ b/solution.py
@@ -347,13 +347,13 @@
         name="gains",
     )(gain_table, near, far, column)
 
+    nearest = slice(1, 5)
     for packed in later:
-        gains, *packed = lax.optimization_barrier((gains, *packed))
-        gathered.append([exchange(tile, "rcv", n + 1) for n, tile in enumerate(packed)])
+        gains, *packed[nearest] = lax.optimization_barrier((gains, *packed[nearest]))
 
     results = []
     for part in range(parts):
-        halves = 2 if part == parts - 1 else 1
+        halves = 1
         rows = receiver_tile // halves
         result = pl.pallas_call(
             functools.partial(multiples_kernel, first_slot=part * rcv_count),
@@ -377,10 +377,14 @@
         )(counts, column, row, in_hbm(spectra), gains, *gathered[part])
         result = list(result)
         if part < parts - 1:
-            nearest = slice(1, 5)
-            result[0], *gathered[part + 1][nearest] = lax.optimization_barrier(
-                (result[0], *gathered[part + 1][nearest])
-            )
+            packed = later[part]
+            near_tiles = [exchange(tile, "rcv", n + 2) for n, tile in enumerate(packed[nearest])]
+            far_tiles = [packed[0]] + packed[nearest.stop :]
+            result[0], *both = lax.optimization_barrier((result[0], *near_tiles, *far_tiles))
+            near_tiles, far_tiles = both[: len(near_tiles)], both[len(near_tiles) :]
+            distances = [1] + list(range(nearest.stop + 1, rcv_count))
+            far_tiles = [exchange(tile, "rcv", n) for n, tile in zip(distances, far_tiles)]
+            gathered.append(far_tiles[:1] + near_tiles + far_tiles[1:])
         results.append([half.reshape((senders,) + half.shape[2:]) for half in result])
 
     before = jnp.arange(freq_count)[None, :] < jnp.arange(freq_count)[:, None]
@@ -395,7 +399,7 @@
         bins = offsets[:, None] + part * rcv_count + ranks[None, :] + 1
         table = time_table(bins.reshape(-1), samples).reshape(-1, samples)
         if part < parts - 1:
-            came[0], _ = lax.optimization_barrier((came[0], results[part + 1][0]))
+            came[0], results[part + 1][0] = lax.optimization_barrier((came[0], results[part + 1][0]))
         out = None
         for n, coef in enumerate(came):
             out = synthesis(coef, table, base, n, len(came), out)

time: 198 us -> 175 us (0.88)
  blocking collectives: 91.7 us -> 0 us
  waiting for transfers between devices: 24.9 us -> 90.8 us
    all_to_all x2 -> x0, blocking collectives: 91.7 us -> none  [on_device(): lax.all_to_all(half, ('freq', 'rcv'), split_axis=0, concat_axis=0, tiled=...]
    all_to_all x1 -> x2, waiting for transfers between devices: 1.95 us -> 42.1 us  [on_device(): lax.all_to_all(half, ('freq', 'rcv'), split_axis=0, concat_axis=0, tiled=...]
    ppermute x14, waiting for transfers between devices: 23 us -> 47.6 us  [exchange(): lax.ppermute(array, axis, [(i, i ^ distance) for i in range(lax.axis_size...]
    all_to_all x1 -> x2, starting transfers between devices: 3.67 us -> 8.49 us  [on_device(): lax.all_to_all(half, ('freq', 'rcv'), split_axis=0, concat_axis=0, tiled=...]
    ppermute x14, starting transfers between devices: 18.6 us -> 15.4 us  [exchange(): lax.ppermute(array, axis, [(i, i ^ distance) for i in range(lax.axis_size...]
    pallas_call x3 -> x2, Pallas kernels: 30.4 us -> 31.3 us  [synthesis(): pl.pallas_call(functools.partial(synthesis_kernel, receiver_tile=rows, pi...]
  transfers between devices with their start and end apart: 16 -> 17, of which waited for: 8 -> 10; matrix products, arithmetic and copies ran while one was open for 1% -> 1% of each run, Pallas kernels for 21% -> 22%
where the time goes in v5:
time: 175 us; the launch traced here: 174 us
  waiting for transfers between devices  90.8 us (52%)
  Pallas kernels  52.8 us (30%)
  starting transfers between devices  28.3 us (16%)
    ppermute x14, waiting for transfers between devices, exchange(): lax.ppermute(array, axis, [(i, i ^ distance) for i in range(lax.axis_size...  47.6 us
    all_to_all x2, waiting for transfers between devices, on_device(): lax.all_to_all(half, ('freq', 'rcv'), split_axis=0, concat_axis=0, tiled=...  42.1 us
    pallas_call x2, Pallas kernels, synthesis(): pl.pallas_call(functools.partial(synthesis_kernel, receiver_tile=rows, pi...  31.3 us
    ppermute x14, starting transfers between devices, exchange(): lax.ppermute(array, axis, [(i, i ^ distance) for i in range(lax.axis_size...  15.4 us
    pallas_call x2, Pallas kernels, on_device(): pl.pallas_call(functools.partial(multiples_kernel, first_slot=part * rcv_...  14.3 us
    all_to_all x2, starting transfers between devices, on_device(): lax.all_to_all(half, ('freq', 'rcv'), split_axis=0, concat_axis=0, tiled=...  8.49 us
    pallas_call x2, Pallas kernels, pack(): pl.pallas_call(functools.partial(pack_kernel, first_slot=part * rcv_count...  4.7 us
    all_to_all x1, starting transfers between devices, on_device(): lax.all_to_all(packed, 'rcv', split_axis=0, concat_axis=0, tiled=True)  4.37 us
  transfers between devices with their start and end apart: 17, of which 10 were waited for; matrix products, arithmetic and copies ran while one was open for 1% of the time, Pallas kernels for 22%

profile of v5, /device:TPU:0, one launch (start us, length us, event | category | flops | bytes accessed | tf_op | source)
XLA Modules:
  0.0 174.0 jit_solution(6531527674146837730)
XLA Ops:
  0.0 3.0 %collective-permute-start.1 = (s32[64,128]{1,0:T(8,128)}, s32[64,128]{1,0:T(8,128)S(1)}, u32[]{:S(2)}, u32[]{:S(2)}) collective-permute-start(s32[64,128]{1,0:T(8,128)} %bitcast.26), channel_id=1, source_target_pairs={{0,4},{1,5},{2,6},{3,7},{4,0},{5,1},{6,2},{7,3},{8,12},{9,13},{10,... | collective-permute-start | bytes 98312 | tf_op jit(solution)/shard_map/ppermute | solution.py:270
  3.0 1.5 collective-permute-start
  4.5 2.4 %pack.2 = f32[8,2,64,512]{3,2,1,0:T(8,128)} custom-call(f32[16,2,64,512]{3,2,1,0:T(8,128)} %spectra_ref.7), custom_call_target="tpu_custom_call" | custom-call | tf_op jit(solution)/shard_map/pack/pallas_call | solution.py:289
  7.2 2.3 %collective-permute-done.2 = s32[64,128]{1,0:T(8,128)S(1)} collective-permute-done((s32[64,128]{1,0:T(8,128)}, s32[64,128]{1,0:T(8,128)S(1)}, u32[]{:S(2)}, u32[]{:S(2)}) %collective-permute-start.2) | collective-permute-done | bytes 32800 | tf_op jit(solution)/shard_map/ppermute | solution.py:270
  9.5 4.4 %all-to-all-start = ((f32[8,2,64,512]{3,2,1,0:T(8,128)}), f32[8,2,64,512]{3,2,1,0:T(8,128)}, u32[]{:S(2)}, u32[]{:S(2)}) async-start(f32[8,2,64,512]{3,2,1,0:T(8,128)} %pack.2), calls=%async_computation | async-start | bytes 4194304 | tf_op jit(solution)/shard_map/all_to_all | solution.py:334
  13.9 2.3 %pack.3 = (f32[2,64,512]{2,1,0:T(8,128)}, f32[2,64,512]{2,1,0:T(8,128)}, f32[2,64,512]{2,1,0:T(8,128)}, f32[2,64,512]{2,1,0:T(8,128)}, f32[2,64,512]{2,1,0:T(8,1...) custom-call(f32[16,2,64,512]{3,2,1,0:T(8,128)} %spectra_ref.7), custom_call_target="tpu_custom_call" | custom-call | tf_op jit(solution)/shard_map/pack/pallas_call | solution.py:289
  16.2 3.7 %collective-permute-start.5 = (s32[4,64,128]{2,1,0:T(8,128)S(1)}, s32[4,64,128]{2,1,0:T(8,128)S(1)}, u32[]{:S(2)}, u32[]{:S(2)}) collective-permute-start(s32[4,64,128]{2,1,0:T(8,128)S(1)} %pad_add_fusion.1), channel_id=1, source_target_pairs={{0,24},{8,16},{16,8},{24,0},{1,25},{9,17},{17,9},{25,1},{2,26},{10... | collective-permute-start | bytes 393224 | tf_op jit(solution)/shard_map/ppermute | solution.py:270
  20.7 3.8 %collective-permute-done.5 = s32[4,64,128]{2,1,0:T(8,128)S(1)} collective-permute-done((s32[4,64,128]{2,1,0:T(8,128)S(1)}, s32[4,64,128]{2,1,0:T(8,128)S(1)}, u32[]{:S(2)}, u32[]{:S(2)}) %collective-permute-start.5) | collective-permute-done | bytes 131104 | tf_op jit(solution)/shard_map/ppermute | solution.py:270
  24.5 7.0 %collective-permute-done.4 = s32[4,64,128]{2,1,0:T(8,128)S(1)} collective-permute-done((s32[4,64,128]{2,1,0:T(8,128)S(1)}, s32[4,64,128]{2,1,0:T(8,128)S(1)}, u32[]{:S(2)}, u32[]{:S(2)}) %collective-permute-start.4) | collective-permute-done | bytes 131104 | tf_op jit(solution)/shard_map/ppermute | solution.py:270
  31.8 1.7 collective-permute-done.6.far_ref
  33.5 2.5 %gains.1.gains_hbm = f32[2,512,512]{2,1,0:T(8,128)S(1)} custom-call(f32[2,16]{1,0:T(2,128)S(1)} %copy-done.2, s32[4,4,64,128]{3,2,1,0:T(8,128)S(1)} %pad_add_fusion.near_ref, s32[4,4,64,128]{3,2,1,0:T(8,128)S(1)} %collective-permute-done.6.far_ref, s32[512,1]{1,0:T(8,128)S(1)} %copy.16.column_ref), custom_call_target="tpu_custom_call" | custom-call | tf_op jit(solution)/shard_map/gains/pallas_call | solution.py:340
  36.1 1.7 collective-permute-start.7
  37.8 1.5 collective-permute-start.9
  40.7 11.7 %multiples.2 = f32[4,8,2,64,128]{4,3,2,1,0:T(8,128)} custom-call(s32[4]{0:T(128)S(1)} %copy-done.1, s32[512,1]{1,0:T(8,128)S(1)} %copy.16.column_ref, s32[1,512]{1,0:T(1,128)S(1)} %bitcast.18, f32[16,2,64,512]{3,2,1,0:T(8,128)} %spectra_ref.7, f32[2,512,512]{2,1,0:T(8,128)S(1)} %gains.1.gains_hbm, f32[8,2,64,512]{3,2,1,0:T(8,128)} %all-to-all-done.refs_0_), custom_call_target="tpu_custom_call" | custom-call | tf_op jit(solution)/shard_map/multiples/pallas_call | solution.py:358
  52.4 4.6 %all-to-all-start.1 = ((f32[32,2,64,128]{3,2,1,0:T(8,128)}), f32[32,2,64,128]{3,2,1,0:T(8,128)}, u32[]{:S(2)}, u32[]{:S(2)}) async-start(f32[32,2,64,128]{3,2,1,0:T(8,128)} %bitcast.20), calls=%async_computation.1 | async-start | bytes 4194304 | tf_op jit(solution)/shard_map/all_to_all | solution.py:396
  57.3 2.6 %collective-permute-start.12 = (f32[2,64,512]{2,1,0:T(8,128)}, f32[2,64,512]{2,1,0:T(8,128)S(1)}, u32[]{:S(2)}, u32[]{:S(2)}) collective-permute-start(f32[2,64,512]{2,1,0:T(8,128)} %get-tuple-element.53), channel_id=1, source_target_pairs={{0,6},{1,7},{2,4},{3,5},{4,2},{5,3},{6,0},{7,1},{8,14},{9,15},{10,... | collective-permute-start | bytes 786440 | tf_op jit(solution)/shard_map/ppermute | solution.py:270
  59.9 26.5 %collective-permute-done.12.refs_5_ = f32[2,64,512]{2,1,0:T(8,128)S(1)} collective-permute-done((f32[2,64,512]{2,1,0:T(8,128)}, f32[2,64,512]{2,1,0:T(8,128)S(1)}, u32[]{:S(2)}, u32[]{:S(2)}) %collective-permute-start.12) | collective-permute-done | bytes 262176 | tf_op jit(solution)/shard_map/ppermute | solution.py:270
  86.4 6.0 %collective-permute-done.13.refs_6_ = f32[2,64,512]{2,1,0:T(8,128)S(1)} collective-permute-done((f32[2,64,512]{2,1,0:T(8,128)}, f32[2,64,512]{2,1,0:T(8,128)S(1)}, u32[]{:S(2)}, u32[]{:S(2)}) %collective-permute-start.13) | collective-permute-done | bytes 262176 | tf_op jit(solution)/shard_map/ppermute | solution.py:270
  92.4 2.6 %multiples.3 = f32[4,8,2,64,128]{4,3,2,1,0:T(8,128)} custom-call(s32[4]{0:T(128)S(1)} %copy-done.1, s32[512,1]{1,0:T(8,128)S(1)} %copy.16.column_ref, s32[1,512]{1,0:T(1,128)S(1)} %bitcast.19, f32[16,2,64,512]{3,2,1,0:T(8,128)} %spectra_ref.7, f32[2,512,512]{2,1,0:T(8,128)S(1)} %gains.1.gains_hbm, f32[2,64,512]{2,1,0:T(8,128)S(1)} %collective-permute-done.11.refs_0_, ...), custom_call_target="tpu_custom_call" | custom-call | tf_op jit(solution)/shard_map/multiples/pallas_call | solution.py:358
  95.0 11.3 %all-to-all-done.1 = f32[32,2,64,128]{3,2,1,0:T(8,128)} async-done(((f32[32,2,64,128]{3,2,1,0:T(8,128)}), f32[32,2,64,128]{3,2,1,0:T(8,128)}, u32[]{:S(2)}, u32[]{:S(2)}) %all-to-all-start.1) | async-done | bytes 2097184 | tf_op jit(solution)/shard_map/all_to_all | solution.py:396
  106.2 3.9 %all-to-all-start.2 = ((f32[32,2,64,128]{3,2,1,0:T(8,128)}), f32[32,2,64,128]{3,2,1,0:T(8,128)S(1)}, u32[]{:S(2)}, u32[]{:S(2)}) async-start(f32[32,2,64,128]{3,2,1,0:T(8,128)} %bitcast.21), calls=%async_computation.2 | async-start | bytes 4194304 | tf_op jit(solution)/shard_map/all_to_all | solution.py:396
  111.7 16.5 %synthesis.2.refs_0_.refs_1_.refs_2_.refs_3_ = f32[128,64,512]{2,1,0:T(8,128)} custom-call(f32[64,512]{1,0:T(8,128)S(1)} %reshape.251.table_ref, f32[128,64,512]{2,1,0:T(8,128)} %refs_3_.1, f32[128,64,512]{2,1,0:T(8,128)} %refs_3_.1, f32[128,64,512]{2,1,0:T(8,128)} %refs_3_.1, f32[128,64,512]{2,1,0:T(8,128)} %refs_3_.1, f32[4096,128]{1,0:T(8,128)} %bitcast.12.refs_4_), custom_call_target="tpu_custom_call" | custom-call | tf_op jit(solution)/shard_map/synthesis/pallas_call | solution.py:311
  128.2 30.8 %all-to-all-done.2 = f32[32,2,64,128]{3,2,1,0:T(8,128)S(1)} async-done(((f32[32,2,64,128]{3,2,1,0:T(8,128)}), f32[32,2,64,128]{3,2,1,0:T(8,128)S(1)}, u32[]{:S(2)}, u32[]{:S(2)}) %all-to-all-start.2) | async-done | bytes 2097184 | tf_op jit(solution)/shard_map/all_to_all | solution.py:396
  159.0 14.8 %synthesis.3 = f32[128,64,512]{2,1,0:T(8,128)} custom-call(f32[64,512]{1,0:T(8,128)S(1)} %reshape.250.table_ref, f32[128,64,512]{2,1,0:T(8,128)} %synthesis.2.refs_0_.refs_1_.refs_2_.refs_3_, f32[128,64,512]{2,1,0:T(8,128)} %synthesis.2.refs_0_.refs_1_.refs_2_.refs_3_, f32[128,64,512]{2,1,0:T(8,128)} %synthesis.2.refs_0_.refs_1_.refs_2_.refs_3_, ...), custom_call_target="tpu_custom_call" | custom-call | tf_op jit(solution)/shard_map/synthesis/pallas_call | solution.py:311
  (42 shorter events, 4.6 us)
Async XLA Ops:
  0.0 9.5 %copy-start.3 = (s32[128,64]{0,1:T(8,128)S(1)}, s32[128,64]{0,1:T(8,128)}, u32[]{:S(2)}) copy-start(s32[128,64]{0,1:T(8,128)} %param.10) | copy-start | bytes 98308
  0.0 6.9 %collective-permute-start.1 = (s32[64,128]{1,0:T(8,128)}, s32[64,128]{1,0:T(8,128)S(1)}, u32[]{:S(2)}, u32[]{:S(2)}) collective-permute-start(s32[64,128]{1,0:T(8,128)} %bitcast.26), channel_id=1, source_target_pairs={{0,4},{1,5},{2,6},{3,7},{4,0},{5,1},{6,2},{7,3},{8,12},{9,13},{10,... | collective-permute-start | bytes 98312 | tf_op jit(solution)/shard_map/ppermute | solution.py:270
  3.0 4.2 %collective-permute-start = (s32[64,128]{1,0:T(8,128)}, s32[64,128]{1,0:T(8,128)S(1)}, u32[]{:S(2)}, u32[]{:S(2)}) collective-permute-start(s32[64,128]{1,0:T(8,128)} %bitcast.27), channel_id=1, source_target_pairs={{0,2},{1,3},{2,0},{3,1},{4,6},{5,7},{6,4},{7,5},{8,10},{9,11},{10,... | collective-permute-start | bytes 98312 | tf_op jit(solution)/shard_map/ppermute | solution.py:270
  4.5 5.0 %collective-permute-start.2 = (s32[64,128]{1,0:T(8,128)}, s32[64,128]{1,0:T(8,128)S(1)}, u32[]{:S(2)}, u32[]{:S(2)}) collective-permute-start(s32[64,128]{1,0:T(8,128)} %bitcast.28), channel_id=1, source_target_pairs={{0,6},{1,7},{2,4},{3,5},{4,2},{5,3},{6,0},{7,1},{8,14},{9,15},{10,... | collective-permute-start | bytes 98312 | tf_op jit(solution)/shard_map/ppermute | solution.py:270
  9.5 31.2 %all-to-all-start = ((f32[8,2,64,512]{3,2,1,0:T(8,128)}), f32[8,2,64,512]{3,2,1,0:T(8,128)}, u32[]{:S(2)}, u32[]{:S(2)}) async-start(f32[8,2,64,512]{3,2,1,0:T(8,128)} %pack.2), calls=%async_computation | async-start | bytes 4194304 | tf_op jit(solution)/shard_map/all_to_all | solution.py:334
  13.9 17.8 %copy-start = (s32[512]{0:T(512)S(1)}, s32[512]{0:T(512)}, u32[]{:S(2)}) copy-start(s32[512]{0:T(512)} %param.8) | copy-start | bytes 6148
  13.9 19.6 %copy-start.2 = (f32[2,16]{1,0:T(2,128)S(1)}, f32[2,16]{1,0:T(2,128)}, u32[]{:S(2)}) copy-start(f32[2,16]{1,0:T(2,128)} %table_ref.1) | copy-start | bytes 388
  16.2 8.3 %collective-permute-start.5 = (s32[4,64,128]{2,1,0:T(8,128)S(1)}, s32[4,64,128]{2,1,0:T(8,128)S(1)}, u32[]{:S(2)}, u32[]{:S(2)}) collective-permute-start(s32[4,64,128]{2,1,0:T(8,128)S(1)} %pad_add_fusion.1), channel_id=1, source_target_pairs={{0,24},{8,16},{16,8},{24,0},{1,25},{9,17},{17,9},{25,1},{2,26},{10... | collective-permute-start | bytes 393224 | tf_op jit(solution)/shard_map/ppermute | solution.py:270
  19.9 11.6 %collective-permute-start.4 = (s32[4,64,128]{2,1,0:T(8,128)S(1)}, s32[4,64,128]{2,1,0:T(8,128)S(1)}, u32[]{:S(2)}, u32[]{:S(2)}) collective-permute-start(s32[4,64,128]{2,1,0:T(8,128)S(1)} %pad_add_fusion.1), channel_id=1, source_target_pairs={{0,16},{8,24},{16,0},{24,8},{1,17},{9,25},{17,1},{25,9},{2,18},{10... | collective-permute-start | bytes 393224 | tf_op jit(solution)/shard_map/ppermute | solution.py:270
  19.9 11.6 %collective-permute-start.3 = (s32[4,64,128]{2,1,0:T(8,128)S(1)}, s32[4,64,128]{2,1,0:T(8,128)S(1)}, u32[]{:S(2)}, u32[]{:S(2)}) collective-permute-start(s32[4,64,128]{2,1,0:T(8,128)S(1)} %pad_add_fusion.1), channel_id=1, source_target_pairs={{0,8},{8,0},{16,24},{24,16},{1,9},{9,1},{17,25},{25,17},{2,10},{10... | collective-permute-start | bytes 393224 | tf_op jit(solution)/shard_map/ppermute | solution.py:270
  31.5 9.2 %copy-start.1 = (s32[4]{0:T(128)S(1)}, s32[4]{0:T(128)}, u32[]{:S(2)}) copy-start(s32[4]{0:T(128)} %counts_ref.3) | copy-start | bytes 52
  31.6 2.0 %collective-permute-start.6 = (s32[4,4,64,128]{3,2,1,0:T(8,128)S(1)}, s32[4,4,64,128]{3,2,1,0:T(8,128)S(1)}, u32[]{:S(2)}, u32[]{:S(2)}) collective-permute-start(s32[4,4,64,128]{3,2,1,0:T(8,128)S(1)} %pad_add_fusion.near_ref), channel_id=1, source_target_pairs={{0,1},{1,0},{2,3},{3,2},{4,5},{5,4},{6,7},{7,6},{8,9},{9,8},{10,11... | collective-permute-start | bytes 1572872 | tf_op jit(solution)/shard_map/ppermute | solution.py:270
  36.1 16.3 %collective-permute-start.7 = (f32[2,64,512]{2,1,0:T(8,128)}, f32[2,64,512]{2,1,0:T(8,128)S(1)}, u32[]{:S(2)}, u32[]{:S(2)}) collective-permute-start(f32[2,64,512]{2,1,0:T(8,128)} %get-tuple-element.40), channel_id=1, source_target_pairs={{0,2},{1,3},{2,0},{3,1},{4,6},{5,7},{6,4},{7,5},{8,10},{9,11},{10,... | collective-permute-start | bytes 786440 | tf_op jit(solution)/shard_map/ppermute | solution.py:270
  37.8 14.6 %collective-permute-start.8 = (f32[2,64,512]{2,1,0:T(8,128)}, f32[2,64,512]{2,1,0:T(8,128)S(1)}, u32[]{:S(2)}, u32[]{:S(2)}) collective-permute-start(f32[2,64,512]{2,1,0:T(8,128)} %get-tuple-element.41), channel_id=1, source_target_pairs={{0,3},{1,2},{2,1},{3,0},{4,7},{5,6},{6,5},{7,4},{8,11},{9,10},{10,... | collective-permute-start | bytes 786440 | tf_op jit(solution)/shard_map/ppermute | solution.py:270
  37.8 14.6 %collective-permute-start.9 = (f32[2,64,512]{2,1,0:T(8,128)}, f32[2,64,512]{2,1,0:T(8,128)S(1)}, u32[]{:S(2)}, u32[]{:S(2)}) collective-permute-start(f32[2,64,512]{2,1,0:T(8,128)} %get-tuple-element.42), channel_id=1, source_target_pairs={{0,4},{1,5},{2,6},{3,7},{4,0},{5,1},{6,2},{7,3},{8,12},{9,13},{10,... | collective-permute-start | bytes 786440 | tf_op jit(solution)/shard_map/ppermute | solution.py:270
  39.3 13.1 %collective-permute-start.10 = (f32[2,64,512]{2,1,0:T(8,128)}, f32[2,64,512]{2,1,0:T(8,128)S(1)}, u32[]{:S(2)}, u32[]{:S(2)}) collective-permute-start(f32[2,64,512]{2,1,0:T(8,128)} %get-tuple-element.43), channel_id=1, source_target_pairs={{0,5},{1,4},{2,7},{3,6},{4,1},{5,0},{6,3},{7,2},{8,13},{9,12},{10,... | collective-permute-start | bytes 786440 | tf_op jit(solution)/shard_map/ppermute | solution.py:270
  52.4 53.8 %all-to-all-start.1 = ((f32[32,2,64,128]{3,2,1,0:T(8,128)}), f32[32,2,64,128]{3,2,1,0:T(8,128)}, u32[]{:S(2)}, u32[]{:S(2)}) async-start(f32[32,2,64,128]{3,2,1,0:T(8,128)} %bitcast.20), calls=%async_computation.1 | async-start | bytes 4194304 | tf_op jit(solution)/shard_map/all_to_all | solution.py:396
  57.1 2.8 %collective-permute-start.11 = (f32[2,64,512]{2,1,0:T(8,128)}, f32[2,64,512]{2,1,0:T(8,128)S(1)}, u32[]{:S(2)}, u32[]{:S(2)}) collective-permute-start(f32[2,64,512]{2,1,0:T(8,128)} %get-tuple-element.48), channel_id=1, source_target_pairs={{0,1},{1,0},{2,3},{3,2},{4,5},{5,4},{6,7},{7,6},{8,9},{9,8},{10,11... | collective-permute-start | bytes 786440 | tf_op jit(solution)/shard_map/ppermute | solution.py:270
  57.3 29.1 %collective-permute-start.12 = (f32[2,64,512]{2,1,0:T(8,128)}, f32[2,64,512]{2,1,0:T(8,128)S(1)}, u32[]{:S(2)}, u32[]{:S(2)}) collective-permute-start(f32[2,64,512]{2,1,0:T(8,128)} %get-tuple-element.53), channel_id=1, source_target_pairs={{0,6},{1,7},{2,4},{3,5},{4,2},{5,3},{6,0},{7,1},{8,14},{9,15},{10,... | collective-permute-start | bytes 786440 | tf_op jit(solution)/shard_map/ppermute | solution.py:270
  59.9 32.5 %collective-permute-start.13 = (f32[2,64,512]{2,1,0:T(8,128)}, f32[2,64,512]{2,1,0:T(8,128)S(1)}, u32[]{:S(2)}, u32[]{:S(2)}) collective-permute-start(f32[2,64,512]{2,1,0:T(8,128)} %get-tuple-element.54), channel_id=1, source_target_pairs={{0,7},{1,6},{2,5},{3,4},{4,3},{5,2},{6,1},{7,0},{8,15},{9,14},{10,... | collective-permute-start | bytes 786440 | tf_op jit(solution)/shard_map/ppermute | solution.py:270
  106.2 52.8 %all-to-all-start.2 = ((f32[32,2,64,128]{3,2,1,0:T(8,128)}), f32[32,2,64,128]{3,2,1,0:T(8,128)S(1)}, u32[]{:S(2)}, u32[]{:S(2)}) async-start(f32[32,2,64,128]{3,2,1,0:T(8,128)} %bitcast.21), calls=%async_computation.2 | async-start | bytes 4194304 | tf_op jit(solution)/shard_map/all_to_all | solution.py:396

commit v6 on v5

--- a/solution.py
+++ b/solution.py
@@ -85,11 +85,10 @@
         store.wait()
 
 
-def multiples_kernel(counts_ref, column_ref, row_ref, spectra_ref, gains_hbm, *refs, first_slot):
+def multiples_kernel(counts_ref, column_ref, row_ref, spectra_ref, gains_hbm, *refs, first_slot, cuts):
     result, data, gains, u, w, y1, y2, tile_sems, gain_sem, out_sems = refs[-10:]
     source_tiles, receiver_tiles, _, receiver_tile, source_tile = result.shape
-    halves = out_sems.shape[0]
-    tiles, outs = refs[: -10 - halves], refs[-10 - halves : -10]
+    tiles, outs = refs[: -10 - len(cuts)], refs[-10 - len(cuts) : -10]
     side = data.shape[3]
     pick = min(PICK, side)
     rank = lax.axis_index("rcv")
@@ -98,12 +97,11 @@
 
     def send(first, count):
         span = pl.ds(first, count)
-        size = receiver_tile // halves
         return [
             pltpu.make_async_copy(
-                result.at[a, span, :, pl.ds(h * size, size)], outs[h].at[a, span], out_sems.at[h, a, first // count]
+                result.at[a, span, :, pl.ds(row, rows)], outs[n].at[a, span], out_sems.at[n, a, first // count]
             )
-            for h in range(halves)
+            for n, (row, rows) in enumerate(cuts)
             for a in range(source_tiles)
         ]
 
@@ -300,12 +298,12 @@
             name="pack",
         )(in_hbm(slots))
 
-    def synthesis(coef, table, base, half, halves, out):
+    def synthesis(coef, table, base, cut, out):
         depth = table.shape[0]
         pieces = 4
         piece = (source_tile // pieces, ROWS, samples)
-        rows = receiver_tile // halves
-        first = half * rows // ROWS
+        row, rows = cut
+        first = row // ROWS
         blocks = [pl.BlockSpec(piece, lambda n, k=k: (k, n + first, 0)) for k in range(pieces)]
         others = [] if out is None else [in_hbm(out)]
         return pl.pallas_call(
@@ -351,15 +349,20 @@
     for packed in later:
         gains, *packed[nearest] = lax.optimization_barrier((gains, *packed[nearest]))
 
+    def cuts_of(part):
+        if part < parts - 1:
+            return [(0, receiver_tile)]
+        end = max(receiver_tile // 4, ROWS)
+        return [(0, receiver_tile - end), (receiver_tile - end, end)]
+
     results = []
     for part in range(parts):
-        halves = 1
-        rows = receiver_tile // halves
+        cuts = cuts_of(part)
         result = pl.pallas_call(
-            functools.partial(multiples_kernel, first_slot=part * rcv_count),
-            out_shape=[pltpu.HBM((freq_count, rcv_count, 2, rows, source_tile), jnp.float32)] * halves,
+            functools.partial(multiples_kernel, first_slot=part * rcv_count, cuts=cuts),
+            out_shape=[pltpu.HBM((freq_count, rcv_count, 2, rows, source_tile), jnp.float32) for _, rows in cuts],
             in_specs=[smem, whole_in(), whole_in()] + [hbm] * (2 + len(gathered[part])),
-            out_specs=[hbm] * halves,
+            out_specs=[hbm] * len(cuts),
             scratch_shapes=[
                 pltpu.VMEM((freq_count, rcv_count, 2, receiver_tile, source_tile), jnp.float32),
                 pltpu.VMEM((rcv_count, 2, receiver_tile, side), jnp.float32),
@@ -370,7 +373,7 @@
                 pltpu.VMEM((side, 2 * side), jnp.float32),
                 pltpu.SemaphoreType.DMA((rcv_count,)),
                 pltpu.SemaphoreType.DMA,
-                pltpu.SemaphoreType.DMA((halves, freq_count, rcv_count)),
+                pltpu.SemaphoreType.DMA((len(cuts), freq_count, rcv_count)),
             ],
             compiler_params=params(32),
             name="multiples",
@@ -385,24 +388,23 @@
             distances = [1] + list(range(nearest.stop + 1, rcv_count))
             far_tiles = [exchange(tile, "rcv", n) for n, tile in zip(distances, far_tiles)]
             gathered.append(far_tiles[:1] + near_tiles + far_tiles[1:])
-        results.append([half.reshape((senders,) + half.shape[2:]) for half in result])
+        results.append([piece.reshape((senders,) + piece.shape[2:]) for piece in result])
 
     before = jnp.arange(freq_count)[None, :] < jnp.arange(freq_count)[:, None]
     offsets = jnp.sum(jnp.where(before, counts[None, :], 0), axis=1)
     ranks = jnp.arange(rcv_count, dtype=jnp.int32)
     base = recorded
-    for part, halves in enumerate(results):
-        came = [
-            lax.all_to_all(half, ("freq", "rcv"), split_axis=0, concat_axis=0, tiled=True).reshape(-1, source_tile)
-            for half in halves
-        ]
+    for part, pieces in enumerate(results):
         bins = offsets[:, None] + part * rcv_count + ranks[None, :] + 1
         table = time_table(bins.reshape(-1), samples).reshape(-1, samples)
-        if part < parts - 1:
-            came[0], results[part + 1][0] = lax.optimization_barrier((came[0], results[part + 1][0]))
         out = None
-        for n, coef in enumerate(came):
-            out = synthesis(coef, table, base, n, len(came), out)
+        for n, cut in enumerate(cuts_of(part)):
+            if part and n:
+                pieces[n], base = lax.optimization_barrier((pieces[n], base))
+            came = lax.all_to_all(pieces[n], ("freq", "rcv"), split_axis=0, concat_axis=0, tiled=True)
+            if part < parts - 1:
+                came, results[part + 1][0] = lax.optimization_barrier((came, results[part + 1][0]))
+            out = synthesis(came.reshape(-1, source_tile), table, base, cut, out)
         base = out
     return base
 

time: 175 us -> 172 us (0.983)
  waiting for transfers between devices: 90.8 us -> 74.5 us
  Pallas kernels: 52.8 us -> 62.7 us
  starting transfers between devices: 28.3 us -> 31.9 us
    all_to_all x2 -> x3, waiting for transfers between devices: 42.1 us -> 25.8 us  [on_device(): lax.all_to_all(pieces[n], ('freq', 'rcv'), split_axis=0, concat_axis=0, t...]
    pallas_call x2, Pallas kernels: 14.3 us -> 23.9 us  [on_device(): pl.pallas_call(functools.partial(multiples_kernel, first_slot=part * rcv_...]
    all_to_all x2 -> x3, starting transfers between devices: 8.49 us -> 12.1 us  [on_device(): lax.all_to_all(pieces[n], ('freq', 'rcv'), split_axis=0, concat_axis=0, t...]
    pallas_call x2 -> x3, Pallas kernels: 31.3 us -> 31.6 us  [synthesis(): pl.pallas_call(functools.partial(synthesis_kernel, receiver_tile=rows, pi...]
  transfers between devices with their start and end apart: 17 -> 18, of which waited for: 10 -> 11; matrix products, arithmetic and copies ran while one was open for 1% -> 1% of each run, Pallas kernels for 22% -> 34%
where the time goes in v6:
time: 172 us; the launch traced here: 171 us
  waiting for transfers between devices  74.5 us (43%)
  Pallas kernels  62.7 us (36%)
  starting transfers between devices  31.9 us (19%)
    ppermute x14, waiting for transfers between devices, exchange(): lax.ppermute(array, axis, [(i, i ^ distance) for i in range(lax.axis_size...  47.6 us
    pallas_call x3, Pallas kernels, synthesis(): pl.pallas_call(functools.partial(synthesis_kernel, receiver_tile=rows, pi...  31.6 us
    all_to_all x3, waiting for transfers between devices, on_device(): lax.all_to_all(pieces[n], ('freq', 'rcv'), split_axis=0, concat_axis=0, t...  25.8 us
    pallas_call x2, Pallas kernels, on_device(): pl.pallas_call(functools.partial(multiples_kernel, first_slot=part * rcv_...  23.9 us
    ppermute x14, starting transfers between devices, exchange(): lax.ppermute(array, axis, [(i, i ^ distance) for i in range(lax.axis_size...  15.4 us
    all_to_all x3, starting transfers between devices, on_device(): lax.all_to_all(pieces[n], ('freq', 'rcv'), split_axis=0, concat_axis=0, t...  12.1 us
    pallas_call x2, Pallas kernels, pack(): pl.pallas_call(functools.partial(pack_kernel, first_slot=part * rcv_count...  4.71 us
    all_to_all x1, starting transfers between devices, on_device(): lax.all_to_all(packed, 'rcv', split_axis=0, concat_axis=0, tiled=True)  4.36 us
  transfers between devices with their start and end apart: 18, of which 11 were waited for; matrix products, arithmetic and copies ran while one was open for 1% of the time, Pallas kernels for 34%

profile of v6, /device:TPU:0, one launch (start us, length us, event | category | flops | bytes accessed | tf_op | source)
XLA Modules:
  0.0 171.2 jit_solution(7428716164184001504)
XLA Ops:
  0.0 3.0 %collective-permute-start.1 = (s32[64,128]{1,0:T(8,128)}, s32[64,128]{1,0:T(8,128)S(1)}, u32[]{:S(2)}, u32[]{:S(2)}) collective-permute-start(s32[64,128]{1,0:T(8,128)} %bitcast.29), channel_id=1, source_target_pairs={{0,4},{1,5},{2,6},{3,7},{4,0},{5,1},{6,2},{7,3},{8,12},{9,13},{10,... | collective-permute-start | bytes 98312 | tf_op jit(solution)/shard_map/ppermute | solution.py:268
  4.5 2.4 %pack.2 = f32[8,2,64,512]{3,2,1,0:T(8,128)} custom-call(f32[16,2,64,512]{3,2,1,0:T(8,128)} %spectra_ref.7), custom_call_target="tpu_custom_call" | custom-call | tf_op jit(solution)/shard_map/pack/pallas_call | solution.py:287
  7.2 2.3 %collective-permute-done.2 = s32[64,128]{1,0:T(8,128)S(1)} collective-permute-done((s32[64,128]{1,0:T(8,128)}, s32[64,128]{1,0:T(8,128)S(1)}, u32[]{:S(2)}, u32[]{:S(2)}) %collective-permute-start.2) | collective-permute-done | bytes 32800 | tf_op jit(solution)/shard_map/ppermute | solution.py:268
  9.5 4.4 %all-to-all-start = ((f32[8,2,64,512]{3,2,1,0:T(8,128)}), f32[8,2,64,512]{3,2,1,0:T(8,128)}, u32[]{:S(2)}, u32[]{:S(2)}) async-start(f32[8,2,64,512]{3,2,1,0:T(8,128)} %pack.2), calls=%async_computation | async-start | bytes 4194304 | tf_op jit(solution)/shard_map/all_to_all | solution.py:332
  13.9 2.3 %pack.3 = (f32[2,64,512]{2,1,0:T(8,128)}, f32[2,64,512]{2,1,0:T(8,128)}, f32[2,64,512]{2,1,0:T(8,128)}, f32[2,64,512]{2,1,0:T(8,128)}, f32[2,64,512]{2,1,0:T(8,1...) custom-call(f32[16,2,64,512]{3,2,1,0:T(8,128)} %spectra_ref.7), custom_call_target="tpu_custom_call" | custom-call | tf_op jit(solution)/shard_map/pack/pallas_call | solution.py:287
  16.2 3.7 %collective-permute-start.5 = (s32[4,64,128]{2,1,0:T(8,128)S(1)}, s32[4,64,128]{2,1,0:T(8,128)S(1)}, u32[]{:S(2)}, u32[]{:S(2)}) collective-permute-start(s32[4,64,128]{2,1,0:T(8,128)S(1)} %pad_add_fusion.1), channel_id=1, source_target_pairs={{0,24},{8,16},{16,8},{24,0},{1,25},{9,17},{17,9},{25,1},{2,26},{10... | collective-permute-start | bytes 393224 | tf_op jit(solution)/shard_map/ppermute | solution.py:268
  20.7 3.8 %collective-permute-done.5 = s32[4,64,128]{2,1,0:T(8,128)S(1)} collective-permute-done((s32[4,64,128]{2,1,0:T(8,128)S(1)}, s32[4,64,128]{2,1,0:T(8,128)S(1)}, u32[]{:S(2)}, u32[]{:S(2)}) %collective-permute-start.5) | collective-permute-done | bytes 131104 | tf_op jit(solution)/shard_map/ppermute | solution.py:268
  24.5 7.0 %collective-permute-done.4 = s32[4,64,128]{2,1,0:T(8,128)S(1)} collective-permute-done((s32[4,64,128]{2,1,0:T(8,128)S(1)}, s32[4,64,128]{2,1,0:T(8,128)S(1)}, u32[]{:S(2)}, u32[]{:S(2)}) %collective-permute-start.4) | collective-permute-done | bytes 131104 | tf_op jit(solution)/shard_map/ppermute | solution.py:268
  31.8 1.7 %collective-permute-done.6.far_ref = s32[4,4,64,128]{3,2,1,0:T(8,128)S(1)} collective-permute-done((s32[4,4,64,128]{3,2,1,0:T(8,128)S(1)}, s32[4,4,64,128]{3,2,1,0:T(8,128)S(1)}, u32[]{:S(2)}, u32[]{:S(2)}) %collective-permute-start.6) | collective-permute-done | bytes 524320 | tf_op jit(solution)/shard_map/ppermute | solution.py:268
  33.5 2.5 %gains.1.gains_hbm = f32[2,512,512]{2,1,0:T(8,128)S(1)} custom-call(f32[2,16]{1,0:T(2,128)S(1)} %copy-done.2, s32[4,4,64,128]{3,2,1,0:T(8,128)S(1)} %pad_add_fusion.near_ref, s32[4,4,64,128]{3,2,1,0:T(8,128)S(1)} %collective-permute-done.6.far_ref, s32[512,1]{1,0:T(8,128)S(1)} %copy.17.column_ref), custom_call_target="tpu_custom_call" | custom-call | tf_op jit(solution)/shard_map/gains/pallas_call | solution.py:338
  36.1 1.7 %collective-permute-start.7 = (f32[2,64,512]{2,1,0:T(8,128)}, f32[2,64,512]{2,1,0:T(8,128)S(1)}, u32[]{:S(2)}, u32[]{:S(2)}) collective-permute-start(f32[2,64,512]{2,1,0:T(8,128)} %get-tuple-element.44), channel_id=1, source_target_pairs={{0,2},{1,3},{2,0},{3,1},{4,6},{5,7},{6,4},{7,5},{8,10},{9,11},{10,... | collective-permute-start | bytes 786440 | tf_op jit(solution)/shard_map/ppermute | solution.py:268
  40.7 11.7 %multiples.2 = f32[4,8,2,64,128]{4,3,2,1,0:T(8,128)} custom-call(s32[4]{0:T(128)S(1)} %copy-done.1, s32[512,1]{1,0:T(8,128)S(1)} %copy.17.column_ref, s32[1,512]{1,0:T(1,128)S(1)} %bitcast.21, f32[16,2,64,512]{3,2,1,0:T(8,128)} %spectra_ref.7, f32[2,512,512]{2,1,0:T(8,128)S(1)} %gains.1.gains_hbm, f32[8,2,64,512]{3,2,1,0:T(8,128)} %all-to-all-done.refs_0_), custom_call_target="tpu_custom_call" | custom-call | tf_op jit(solution)/shard_map/multiples/pallas_call | solution.py:361
  52.4 4.6 %all-to-all-start.1 = ((f32[32,2,64,128]{3,2,1,0:T(8,128)}), f32[32,2,64,128]{3,2,1,0:T(8,128)}, u32[]{:S(2)}, u32[]{:S(2)}) async-start(f32[32,2,64,128]{3,2,1,0:T(8,128)} %bitcast.23), calls=%async_computation.1 | async-start | bytes 4194304 | tf_op jit(solution)/shard_map/all_to_all | solution.py:404
  57.3 2.6 %collective-permute-start.12 = (f32[2,64,512]{2,1,0:T(8,128)}, f32[2,64,512]{2,1,0:T(8,128)S(1)}, u32[]{:S(2)}, u32[]{:S(2)}) collective-permute-start(f32[2,64,512]{2,1,0:T(8,128)} %get-tuple-element.56), channel_id=1, source_target_pairs={{0,6},{1,7},{2,4},{3,5},{4,2},{5,3},{6,0},{7,1},{8,14},{9,15},{10,... | collective-permute-start | bytes 786440 | tf_op jit(solution)/shard_map/ppermute | solution.py:268
  59.9 26.5 %collective-permute-done.12.refs_5_ = f32[2,64,512]{2,1,0:T(8,128)S(1)} collective-permute-done((f32[2,64,512]{2,1,0:T(8,128)}, f32[2,64,512]{2,1,0:T(8,128)S(1)}, u32[]{:S(2)}, u32[]{:S(2)}) %collective-permute-start.12) | collective-permute-done | bytes 262176 | tf_op jit(solution)/shard_map/ppermute | solution.py:268
  86.4 6.0 %collective-permute-done.13.refs_6_ = f32[2,64,512]{2,1,0:T(8,128)S(1)} collective-permute-done((f32[2,64,512]{2,1,0:T(8,128)}, f32[2,64,512]{2,1,0:T(8,128)S(1)}, u32[]{:S(2)}, u32[]{:S(2)}) %collective-permute-start.13) | collective-permute-done | bytes 262176 | tf_op jit(solution)/shard_map/ppermute | solution.py:268
  92.4 12.2 %multiples.3 = (f32[4,8,2,48,128]{4,3,2,1,0:T(8,128)}, f32[4,8,2,16,128]{4,3,2,1,0:T(8,128)}) custom-call(s32[4]{0:T(128)S(1)} %copy-done.1, s32[512,1]{1,0:T(8,128)S(1)} %copy.17.column_ref, s32[1,512]{1,0:T(1,128)S(1)} %bitcast.22, f32[16,2,64,512]{3,2,1,0:T(8,128)} %spectra_ref.7, f32[2,512,512]{2,1,0:T(8,128)S(1)} %gains.1.gains_hbm, ...), custom_call_target="tpu_custom_call" | custom-call | tf_op jit(solution)/shard_map/multiples/pallas_call | solution.py:361
  106.2 3.7 %all-to-all-start.3 = ((f32[32,2,48,128]{3,2,1,0:T(8,128)}), f32[32,2,48,128]{3,2,1,0:T(8,128)S(1)}, u32[]{:S(2)}, u32[]{:S(2)}) async-start(f32[32,2,48,128]{3,2,1,0:T(8,128)} %bitcast.24), calls=%async_computation.3 | async-start | bytes 3145728 | tf_op jit(solution)/shard_map/all_to_all | solution.py:404
  110.8 16.4 %synthesis.3.refs_0_.refs_1_.refs_2_.refs_3_ = f32[128,64,512]{2,1,0:T(8,128)} custom-call(f32[64,512]{1,0:T(8,128)S(1)} %reshape.258.table_ref, f32[128,64,512]{2,1,0:T(8,128)} %refs_3_.1, f32[128,64,512]{2,1,0:T(8,128)} %refs_3_.1, f32[128,64,512]{2,1,0:T(8,128)} %refs_3_.1, f32[128,64,512]{2,1,0:T(8,128)} %refs_3_.1, f32[4096,128]{1,0:T(8,128)} %bitcast.14.refs_4_), custom_call_target="tpu_custom_call" | custom-call | tf_op jit(solution)/shard_map/synthesis/pallas_call | solution.py:309
  127.2 20.5 %all-to-all-done.3 = f32[32,2,48,128]{3,2,1,0:T(8,128)S(1)} async-done(((f32[32,2,48,128]{3,2,1,0:T(8,128)}), f32[32,2,48,128]{3,2,1,0:T(8,128)S(1)}, u32[]{:S(2)}, u32[]{:S(2)}) %all-to-all-start.3) | async-done | bytes 1572896 | tf_op jit(solution)/shard_map/all_to_all | solution.py:404
  147.7 3.8 %all-to-all-start.2 = ((f32[32,2,16,128]{3,2,1,0:T(8,128)}), f32[32,2,16,128]{3,2,1,0:T(8,128)S(1)}, u32[]{:S(2)}, u32[]{:S(2)}) async-start(f32[32,2,16,128]{3,2,1,0:T(8,128)} %bitcast.11), calls=%async_computation.2 | async-start | bytes 1048576 | tf_op jit(solution)/shard_map/all_to_all | solution.py:404
  152.2 11.1 %synthesis.4.refs_5_ = f32[128,64,512]{2,1,0:T(8,128)} custom-call(f32[64,512]{1,0:T(8,128)S(1)} %reshape.256.table_ref, f32[128,64,512]{2,1,0:T(8,128)} %synthesis.3.refs_0_.refs_1_.refs_2_.refs_3_, f32[128,64,512]{2,1,0:T(8,128)} %synthesis.3.refs_0_.refs_1_.refs_2_.refs_3_, f32[128,64,512]{2,1,0:T(8,128)} %synthesis.3.refs_0_.refs_1_.refs_2_.refs_3_, ...), custom_call_target="tpu_custom_call" | custom-call | tf_op jit(solution)/shard_map/synthesis/pallas_call | solution.py:309
  163.3 3.7 %all-to-all-done.2 = f32[32,2,16,128]{3,2,1,0:T(8,128)S(1)} async-done(((f32[32,2,16,128]{3,2,1,0:T(8,128)}), f32[32,2,16,128]{3,2,1,0:T(8,128)S(1)}, u32[]{:S(2)}, u32[]{:S(2)}) %all-to-all-start.2) | async-done | bytes 524320 | tf_op jit(solution)/shard_map/all_to_all | solution.py:404
  167.0 4.1 %synthesis.5 = f32[128,64,512]{2,1,0:T(8,128)} custom-call(f32[64,512]{1,0:T(8,128)S(1)} %reshape.256.table_ref, f32[128,64,512]{2,1,0:T(8,128)} %synthesis.3.refs_0_.refs_1_.refs_2_.refs_3_, f32[128,64,512]{2,1,0:T(8,128)} %synthesis.3.refs_0_.refs_1_.refs_2_.refs_3_, ...), custom_call_target="tpu_custom_call", output_to_operand_aliasing={{}: (6, {})} | custom-call | tf_op jit(solution)/shard_map/synthesis/pallas_call | solution.py:309
  (45 shorter events, 9.2 us)
Async XLA Ops:
  0.0 9.5 %copy-start.3 = (s32[128,64]{0,1:T(8,128)S(1)}, s32[128,64]{0,1:T(8,128)}, u32[]{:S(2)}) copy-start(s32[128,64]{0,1:T(8,128)} %param.10) | copy-start | bytes 98308
  0.0 6.9 %collective-permute-start.1 = (s32[64,128]{1,0:T(8,128)}, s32[64,128]{1,0:T(8,128)S(1)}, u32[]{:S(2)}, u32[]{:S(2)}) collective-permute-start(s32[64,128]{1,0:T(8,128)} %bitcast.29), channel_id=1, source_target_pairs={{0,4},{1,5},{2,6},{3,7},{4,0},{5,1},{6,2},{7,3},{8,12},{9,13},{10,... | collective-permute-start | bytes 98312 | tf_op jit(solution)/shard_map/ppermute | solution.py:268
  3.0 4.2 %collective-permute-start = (s32[64,128]{1,0:T(8,128)}, s32[64,128]{1,0:T(8,128)S(1)}, u32[]{:S(2)}, u32[]{:S(2)}) collective-permute-start(s32[64,128]{1,0:T(8,128)} %bitcast.30), channel_id=1, source_target_pairs={{0,2},{1,3},{2,0},{3,1},{4,6},{5,7},{6,4},{7,5},{8,10},{9,11},{10,... | collective-permute-start | bytes 98312 | tf_op jit(solution)/shard_map/ppermute | solution.py:268
  4.5 5.0 %collective-permute-start.2 = (s32[64,128]{1,0:T(8,128)}, s32[64,128]{1,0:T(8,128)S(1)}, u32[]{:S(2)}, u32[]{:S(2)}) collective-permute-start(s32[64,128]{1,0:T(8,128)} %bitcast.31), channel_id=1, source_target_pairs={{0,6},{1,7},{2,4},{3,5},{4,2},{5,3},{6,0},{7,1},{8,14},{9,15},{10,... | collective-permute-start | bytes 98312 | tf_op jit(solution)/shard_map/ppermute | solution.py:268
  9.5 31.2 %all-to-all-start = ((f32[8,2,64,512]{3,2,1,0:T(8,128)}), f32[8,2,64,512]{3,2,1,0:T(8,128)}, u32[]{:S(2)}, u32[]{:S(2)}) async-start(f32[8,2,64,512]{3,2,1,0:T(8,128)} %pack.2), calls=%async_computation | async-start | bytes 4194304 | tf_op jit(solution)/shard_map/all_to_all | solution.py:332
  13.9 17.8 %copy-start = (s32[512]{0:T(512)S(1)}, s32[512]{0:T(512)}, u32[]{:S(2)}) copy-start(s32[512]{0:T(512)} %param.8) | copy-start | bytes 6148
  13.9 19.7 %copy-start.2 = (f32[2,16]{1,0:T(2,128)S(1)}, f32[2,16]{1,0:T(2,128)}, u32[]{:S(2)}) copy-start(f32[2,16]{1,0:T(2,128)} %table_ref.1) | copy-start | bytes 388
  16.2 8.3 %collective-permute-start.5 = (s32[4,64,128]{2,1,0:T(8,128)S(1)}, s32[4,64,128]{2,1,0:T(8,128)S(1)}, u32[]{:S(2)}, u32[]{:S(2)}) collective-permute-start(s32[4,64,128]{2,1,0:T(8,128)S(1)} %pad_add_fusion.1), channel_id=1, source_target_pairs={{0,24},{8,16},{16,8},{24,0},{1,25},{9,17},{17,9},{25,1},{2,26},{10... | collective-permute-start | bytes 393224 | tf_op jit(solution)/shard_map/ppermute | solution.py:268
  19.9 11.6 %collective-permute-start.4 = (s32[4,64,128]{2,1,0:T(8,128)S(1)}, s32[4,64,128]{2,1,0:T(8,128)S(1)}, u32[]{:S(2)}, u32[]{:S(2)}) collective-permute-start(s32[4,64,128]{2,1,0:T(8,128)S(1)} %pad_add_fusion.1), channel_id=1, source_target_pairs={{0,16},{8,24},{16,0},{24,8},{1,17},{9,25},{17,1},{25,9},{2,18},{10... | collective-permute-start | bytes 393224 | tf_op jit(solution)/shard_map/ppermute | solution.py:268
  19.9 11.6 %collective-permute-start.3 = (s32[4,64,128]{2,1,0:T(8,128)S(1)}, s32[4,64,128]{2,1,0:T(8,128)S(1)}, u32[]{:S(2)}, u32[]{:S(2)}) collective-permute-start(s32[4,64,128]{2,1,0:T(8,128)S(1)} %pad_add_fusion.1), channel_id=1, source_target_pairs={{0,8},{8,0},{16,24},{24,16},{1,9},{9,1},{17,25},{25,17},{2,10},{10... | collective-permute-start | bytes 393224 | tf_op jit(solution)/shard_map/ppermute | solution.py:268
  31.5 9.1 %copy-start.1 = (s32[4]{0:T(128)S(1)}, s32[4]{0:T(128)}, u32[]{:S(2)}) copy-start(s32[4]{0:T(128)} %counts_ref.3) | copy-start | bytes 52
  31.6 2.0 %collective-permute-start.6 = (s32[4,4,64,128]{3,2,1,0:T(8,128)S(1)}, s32[4,4,64,128]{3,2,1,0:T(8,128)S(1)}, u32[]{:S(2)}, u32[]{:S(2)}) collective-permute-start(s32[4,4,64,128]{3,2,1,0:T(8,128)S(1)} %pad_add_fusion.near_ref), channel_id=1, source_target_pairs={{0,1},{1,0},{2,3},{3,2},{4,5},{5,4},{6,7},{7,6},{8,9},{9,8},{10,11... | collective-permute-start | bytes 1572872 | tf_op jit(solution)/shard_map/ppermute | solution.py:268
  36.1 16.3 %collective-permute-start.7 = (f32[2,64,512]{2,1,0:T(8,128)}, f32[2,64,512]{2,1,0:T(8,128)S(1)}, u32[]{:S(2)}, u32[]{:S(2)}) collective-permute-start(f32[2,64,512]{2,1,0:T(8,128)} %get-tuple-element.44), channel_id=1, source_target_pairs={{0,2},{1,3},{2,0},{3,1},{4,6},{5,7},{6,4},{7,5},{8,10},{9,11},{10,... | collective-permute-start | bytes 786440 | tf_op jit(solution)/shard_map/ppermute | solution.py:268
  37.8 14.6 %collective-permute-start.8 = (f32[2,64,512]{2,1,0:T(8,128)}, f32[2,64,512]{2,1,0:T(8,128)S(1)}, u32[]{:S(2)}, u32[]{:S(2)}) collective-permute-start(f32[2,64,512]{2,1,0:T(8,128)} %get-tuple-element.45), channel_id=1, source_target_pairs={{0,3},{1,2},{2,1},{3,0},{4,7},{5,6},{6,5},{7,4},{8,11},{9,10},{10,... | collective-permute-start | bytes 786440 | tf_op jit(solution)/shard_map/ppermute | solution.py:268
  37.8 14.6 %collective-permute-start.9 = (f32[2,64,512]{2,1,0:T(8,128)}, f32[2,64,512]{2,1,0:T(8,128)S(1)}, u32[]{:S(2)}, u32[]{:S(2)}) collective-permute-start(f32[2,64,512]{2,1,0:T(8,128)} %get-tuple-element.46), channel_id=1, source_target_pairs={{0,4},{1,5},{2,6},{3,7},{4,0},{5,1},{6,2},{7,3},{8,12},{9,13},{10,... | collective-permute-start | bytes 786440 | tf_op jit(solution)/shard_map/ppermute | solution.py:268
  39.3 13.1 %collective-permute-start.10 = (f32[2,64,512]{2,1,0:T(8,128)}, f32[2,64,512]{2,1,0:T(8,128)S(1)}, u32[]{:S(2)}, u32[]{:S(2)}) collective-permute-start(f32[2,64,512]{2,1,0:T(8,128)} %get-tuple-element.47), channel_id=1, source_target_pairs={{0,5},{1,4},{2,7},{3,6},{4,1},{5,0},{6,3},{7,2},{8,13},{9,12},{10,... | collective-permute-start | bytes 786440 | tf_op jit(solution)/shard_map/ppermute | solution.py:268
  52.4 53.8 %all-to-all-start.1 = ((f32[32,2,64,128]{3,2,1,0:T(8,128)}), f32[32,2,64,128]{3,2,1,0:T(8,128)}, u32[]{:S(2)}, u32[]{:S(2)}) async-start(f32[32,2,64,128]{3,2,1,0:T(8,128)} %bitcast.23), calls=%async_computation.1 | async-start | bytes 4194304 | tf_op jit(solution)/shard_map/all_to_all | solution.py:404
  57.0 2.8 %collective-permute-start.11 = (f32[2,64,512]{2,1,0:T(8,128)}, f32[2,64,512]{2,1,0:T(8,128)S(1)}, u32[]{:S(2)}, u32[]{:S(2)}) collective-permute-start(f32[2,64,512]{2,1,0:T(8,128)} %get-tuple-element.51), channel_id=1, source_target_pairs={{0,1},{1,0},{2,3},{3,2},{4,5},{5,4},{6,7},{7,6},{8,9},{9,8},{10,11... | collective-permute-start | bytes 786440 | tf_op jit(solution)/shard_map/ppermute | solution.py:268
  57.3 29.1 %collective-permute-start.12 = (f32[2,64,512]{2,1,0:T(8,128)}, f32[2,64,512]{2,1,0:T(8,128)S(1)}, u32[]{:S(2)}, u32[]{:S(2)}) collective-permute-start(f32[2,64,512]{2,1,0:T(8,128)} %get-tuple-element.56), channel_id=1, source_target_pairs={{0,6},{1,7},{2,4},{3,5},{4,2},{5,3},{6,0},{7,1},{8,14},{9,15},{10,... | collective-permute-start | bytes 786440 | tf_op jit(solution)/shard_map/ppermute | solution.py:268
  59.9 32.5 %collective-permute-start.13 = (f32[2,64,512]{2,1,0:T(8,128)}, f32[2,64,512]{2,1,0:T(8,128)S(1)}, u32[]{:S(2)}, u32[]{:S(2)}) collective-permute-start(f32[2,64,512]{2,1,0:T(8,128)} %get-tuple-element.57), channel_id=1, source_target_pairs={{0,7},{1,6},{2,5},{3,4},{4,3},{5,2},{6,1},{7,0},{8,15},{9,14},{10,... | collective-permute-start | bytes 786440 | tf_op jit(solution)/shard_map/ppermute | solution.py:268
  106.2 41.4 %all-to-all-start.3 = ((f32[32,2,48,128]{3,2,1,0:T(8,128)}), f32[32,2,48,128]{3,2,1,0:T(8,128)S(1)}, u32[]{:S(2)}, u32[]{:S(2)}) async-start(f32[32,2,48,128]{3,2,1,0:T(8,128)} %bitcast.24), calls=%async_computation.3 | async-start | bytes 3145728 | tf_op jit(solution)/shard_map/all_to_all | solution.py:404
  147.7 19.3 %all-to-all-start.2 = ((f32[32,2,16,128]{3,2,1,0:T(8,128)}), f32[32,2,16,128]{3,2,1,0:T(8,128)S(1)}, u32[]{:S(2)}, u32[]{:S(2)}) async-start(f32[32,2,16,128]{3,2,1,0:T(8,128)} %bitcast.11), calls=%async_computation.2 | async-start | bytes 1048576 | tf_op jit(solution)/shard_map/all_to_all | solution.py:404

commit v7 on v6

--- a/solution.py
+++ b/solution.py
@@ -87,7 +87,7 @@
 
 def multiples_kernel(counts_ref, column_ref, row_ref, spectra_ref, gains_hbm, *refs, first_slot, cuts):
     result, data, gains, u, w, y1, y2, tile_sems, gain_sem, out_sems = refs[-10:]
-    source_tiles, receiver_tiles, _, receiver_tile, source_tile = result.shape
+    receiver_tiles, source_tiles, _, receiver_tile, source_tile = result.shape
     tiles, outs = refs[: -10 - len(cuts)], refs[-10 - len(cuts) : -10]
     side = data.shape[3]
     pick = min(PICK, side)
@@ -99,10 +99,9 @@
         span = pl.ds(first, count)
         return [
             pltpu.make_async_copy(
-                result.at[a, span, :, pl.ds(row, rows)], outs[n].at[a, span], out_sems.at[n, a, first // count]
+                result.at[span, :, :, pl.ds(row, rows)], outs[n].at[span], out_sems.at[n, first // count]
             )
             for n, (row, rows) in enumerate(cuts)
-            for a in range(source_tiles)
         ]
 
     at_once = pick // receiver_tile
@@ -125,7 +124,6 @@
         for copy in copies:
             copy.start()
         gain_copy = pltpu.make_async_copy(gains_hbm, gains, gain_sem)
-        gain_copy.start()
         for n, copy in enumerate(copies):
             copy.wait()
             first_row = origins[n] * receiver_tile
@@ -139,6 +137,7 @@
                 w[top, side:] = imag[part]
                 w[low, :side] = -imag[part]
                 w[low, side:] = real[part]
+        gain_copy.start()
         high, again, low = (slice(n * 2 * side, (n + 1) * 2 * side) for n in range(3))
         for start in range(0, side, pick):
             rows = slice(start, start + pick)
@@ -187,7 +186,7 @@
                 for i in range(pick // receiver_tile):
                     tile = start // receiver_tile + i
                     for a in range(source_tiles):
-                        result[a, tile, c] = natural[
+                        result[tile, a, c] = natural[
                             i * receiver_tile : (i + 1) * receiver_tile, a * source_tile : (a + 1) * source_tile
                         ]
             for copy in send(start // receiver_tile, at_once):
@@ -360,11 +359,11 @@
         cuts = cuts_of(part)
         result = pl.pallas_call(
             functools.partial(multiples_kernel, first_slot=part * rcv_count, cuts=cuts),
-            out_shape=[pltpu.HBM((freq_count, rcv_count, 2, rows, source_tile), jnp.float32) for _, rows in cuts],
+            out_shape=[pltpu.HBM((rcv_count, freq_count, 2, rows, source_tile), jnp.float32) for _, rows in cuts],
             in_specs=[smem, whole_in(), whole_in()] + [hbm] * (2 + len(gathered[part])),
             out_specs=[hbm] * len(cuts),
             scratch_shapes=[
-                pltpu.VMEM((freq_count, rcv_count, 2, receiver_tile, source_tile), jnp.float32),
+                pltpu.VMEM((rcv_count, freq_count, 2, receiver_tile, source_tile), jnp.float32),
                 pltpu.VMEM((rcv_count, 2, receiver_tile, side), jnp.float32),
                 pltpu.VMEM((2, side, side), jnp.float32),
                 pltpu.VMEM((side, 6 * side), jnp.bfloat16),
@@ -373,7 +372,7 @@
                 pltpu.VMEM((side, 2 * side), jnp.float32),
                 pltpu.SemaphoreType.DMA((rcv_count,)),
                 pltpu.SemaphoreType.DMA,
-                pltpu.SemaphoreType.DMA((len(cuts), freq_count, rcv_count)),
+                pltpu.SemaphoreType.DMA((len(cuts), rcv_count)),
             ],
             compiler_params=params(32),
             name="multiples",
@@ -395,13 +394,13 @@
     ranks = jnp.arange(rcv_count, dtype=jnp.int32)
     base = recorded
     for part, pieces in enumerate(results):
-        bins = offsets[:, None] + part * rcv_count + ranks[None, :] + 1
+        bins = offsets[None, :] + part * rcv_count + ranks[:, None] + 1
         table = time_table(bins.reshape(-1), samples).reshape(-1, samples)
         out = None
         for n, cut in enumerate(cuts_of(part)):
             if part and n:
                 pieces[n], base = lax.optimization_barrier((pieces[n], base))
-            came = lax.all_to_all(pieces[n], ("freq", "rcv"), split_axis=0, concat_axis=0, tiled=True)
+            came = lax.all_to_all(pieces[n], ("rcv", "freq"), split_axis=0, concat_axis=0, tiled=True)
             if part < parts - 1:
                 came, results[part + 1][0] = lax.optimization_barrier((came, results[part + 1][0]))
             out = synthesis(came.reshape(-1, source_tile), table, base, cut, out)

time: 172 us -> 169 us (0.983)
  Pallas kernels: 62.7 us -> 52.9 us
  waiting for transfers between devices: 74.5 us -> 79.8 us
    pallas_call x2, Pallas kernels: 23.9 us -> 14.1 us  [on_device(): pl.pallas_call(functools.partial(multiples_kernel, first_slot=part * rcv_...]
    all_to_all x3, waiting for transfers between devices: 25.8 us -> 30.2 us  [on_device(): lax.all_to_all(pieces[n], ('rcv', 'freq'), split_axis=0, concat_axis=0, t...]
  transfers between devices with their start and end apart: 18 -> 18, of which waited for: 11 -> 11; matrix products, arithmetic and copies ran while one was open for 1% -> 1% of each run, Pallas kernels for 34% -> 29%
where the time goes in v7:
time: 169 us; the launch traced here: 168 us
  waiting for transfers between devices  79.8 us (47%)
  Pallas kernels  52.9 us (31%)
  starting transfers between devices  33.1 us (20%)
    ppermute x14, waiting for transfers between devices, exchange(): lax.ppermute(array, axis, [(i, i ^ distance) for i in range(lax.axis_size...  48.5 us
    pallas_call x3, Pallas kernels, synthesis(): pl.pallas_call(functools.partial(synthesis_kernel, receiver_tile=rows, pi...  31.6 us
    all_to_all x3, waiting for transfers between devices, on_device(): lax.all_to_all(pieces[n], ('rcv', 'freq'), split_axis=0, concat_axis=0, t...  30.2 us
    ppermute x14, starting transfers between devices, exchange(): lax.ppermute(array, axis, [(i, i ^ distance) for i in range(lax.axis_size...  15.4 us
    pallas_call x2, Pallas kernels, on_device(): pl.pallas_call(functools.partial(multiples_kernel, first_slot=part * rcv_...  14.1 us
    all_to_all x3, starting transfers between devices, on_device(): lax.all_to_all(pieces[n], ('rcv', 'freq'), split_axis=0, concat_axis=0, t...  13.3 us
    pallas_call x2, Pallas kernels, pack(): pl.pallas_call(functools.partial(pack_kernel, first_slot=part * rcv_count...  4.71 us
    all_to_all x1, starting transfers between devices, on_device(): lax.all_to_all(packed, 'rcv', split_axis=0, concat_axis=0, tiled=True)  4.36 us
  transfers between devices with their start and end apart: 18, of which 11 were waited for; matrix products, arithmetic and copies ran while one was open for 1% of the time, Pallas kernels for 29%

profile of v7, /device:TPU:0, one launch (start us, length us, event | category | flops | bytes accessed | tf_op | source)
XLA Modules:
  0.0 167.8 jit_solution(5715921206776787266)
XLA Ops:
  0.0 3.0 %collective-permute-start.1 = (s32[64,128]{1,0:T(8,128)}, s32[64,128]{1,0:T(8,128)S(1)}, u32[]{:S(2)}, u32[]{:S(2)}) collective-permute-start(s32[64,128]{1,0:T(8,128)} %bitcast.29), channel_id=1, source_target_pairs={{0,4},{1,5},{2,6},{3,7},{4,0},{5,1},{6,2},{7,3},{8,12},{9,13},{10,... | collective-permute-start | bytes 98312 | tf_op jit(solution)/shard_map/ppermute | solution.py:267
  4.5 2.4 %pack.2 = f32[8,2,64,512]{3,2,1,0:T(8,128)} custom-call(f32[16,2,64,512]{3,2,1,0:T(8,128)} %spectra_ref.7), custom_call_target="tpu_custom_call" | custom-call | tf_op jit(solution)/shard_map/pack/pallas_call | solution.py:286
  7.2 2.3 %collective-permute-done.2 = s32[64,128]{1,0:T(8,128)S(1)} collective-permute-done((s32[64,128]{1,0:T(8,128)}, s32[64,128]{1,0:T(8,128)S(1)}, u32[]{:S(2)}, u32[]{:S(2)}) %collective-permute-start.2) | collective-permute-done | bytes 32800 | tf_op jit(solution)/shard_map/ppermute | solution.py:267
  9.5 4.4 %all-to-all-start = ((f32[8,2,64,512]{3,2,1,0:T(8,128)}), f32[8,2,64,512]{3,2,1,0:T(8,128)}, u32[]{:S(2)}, u32[]{:S(2)}) async-start(f32[8,2,64,512]{3,2,1,0:T(8,128)} %pack.2), calls=%async_computation | async-start | bytes 4194304 | tf_op jit(solution)/shard_map/all_to_all | solution.py:331
  13.9 2.3 %pack.3 = (f32[2,64,512]{2,1,0:T(8,128)}, f32[2,64,512]{2,1,0:T(8,128)}, f32[2,64,512]{2,1,0:T(8,128)}, f32[2,64,512]{2,1,0:T(8,128)}, f32[2,64,512]{2,1,0:T(8,1...) custom-call(f32[16,2,64,512]{3,2,1,0:T(8,128)} %spectra_ref.7), custom_call_target="tpu_custom_call" | custom-call | tf_op jit(solution)/shard_map/pack/pallas_call | solution.py:286
  16.2 3.7 %collective-permute-start.5 = (s32[4,64,128]{2,1,0:T(8,128)S(1)}, s32[4,64,128]{2,1,0:T(8,128)S(1)}, u32[]{:S(2)}, u32[]{:S(2)}) collective-permute-start(s32[4,64,128]{2,1,0:T(8,128)S(1)} %pad_add_fusion.1), channel_id=1, source_target_pairs={{0,24},{8,16},{16,8},{24,0},{1,25},{9,17},{17,9},{25,1},{2,26},{10... | collective-permute-start | bytes 393224 | tf_op jit(solution)/shard_map/ppermute | solution.py:267
  20.7 3.8 %collective-permute-done.5 = s32[4,64,128]{2,1,0:T(8,128)S(1)} collective-permute-done((s32[4,64,128]{2,1,0:T(8,128)S(1)}, s32[4,64,128]{2,1,0:T(8,128)S(1)}, u32[]{:S(2)}, u32[]{:S(2)}) %collective-permute-start.5) | collective-permute-done | bytes 131104 | tf_op jit(solution)/shard_map/ppermute | solution.py:267
  24.5 7.0 %collective-permute-done.4 = s32[4,64,128]{2,1,0:T(8,128)S(1)} collective-permute-done((s32[4,64,128]{2,1,0:T(8,128)S(1)}, s32[4,64,128]{2,1,0:T(8,128)S(1)}, u32[]{:S(2)}, u32[]{:S(2)}) %collective-permute-start.4) | collective-permute-done | bytes 131104 | tf_op jit(solution)/shard_map/ppermute | solution.py:267
  33.5 2.5 %gains.1.gains_hbm = f32[2,512,512]{2,1,0:T(8,128)S(1)} custom-call(f32[2,16]{1,0:T(2,128)S(1)} %copy-done.2, s32[4,4,64,128]{3,2,1,0:T(8,128)S(1)} %pad_add_fusion.near_ref, s32[4,4,64,128]{3,2,1,0:T(8,128)S(1)} %collective-permute-done.6.far_ref, s32[512,1]{1,0:T(8,128)S(1)} %copy.17.column_ref), custom_call_target="tpu_custom_call" | custom-call | tf_op jit(solution)/shard_map/gains/pallas_call | solution.py:337
  36.1 1.7 %collective-permute-start.7 = (f32[2,64,512]{2,1,0:T(8,128)}, f32[2,64,512]{2,1,0:T(8,128)S(1)}, u32[]{:S(2)}, u32[]{:S(2)}) collective-permute-start(f32[2,64,512]{2,1,0:T(8,128)} %get-tuple-element.44), channel_id=1, source_target_pairs={{0,2},{1,3},{2,0},{3,1},{4,6},{5,7},{6,4},{7,5},{8,10},{9,11},{10,... | collective-permute-start | bytes 786440 | tf_op jit(solution)/shard_map/ppermute | solution.py:267
  40.7 11.7 %multiples.2 = f32[8,4,2,64,128]{4,3,2,1,0:T(8,128)} custom-call(s32[4]{0:T(128)S(1)} %copy-done.1, s32[512,1]{1,0:T(8,128)S(1)} %copy.17.column_ref, s32[1,512]{1,0:T(1,128)S(1)} %bitcast.21, f32[16,2,64,512]{3,2,1,0:T(8,128)} %spectra_ref.7, f32[2,512,512]{2,1,0:T(8,128)S(1)} %gains.1.gains_hbm, f32[8,2,64,512]{3,2,1,0:T(8,128)} %all-to-all-done.refs_0_), custom_call_target="tpu_custom_call" | custom-call | tf_op jit(solution)/shard_map/multiples/pallas_call | solution.py:360
  52.4 4.6 %all-to-all-start.1 = ((f32[32,2,64,128]{3,2,1,0:T(8,128)}), f32[32,2,64,128]{3,2,1,0:T(8,128)}, u32[]{:S(2)}, u32[]{:S(2)}) async-start(f32[32,2,64,128]{3,2,1,0:T(8,128)} %bitcast.23), calls=%async_computation.1 | async-start | bytes 4194304 | tf_op jit(solution)/shard_map/all_to_all | solution.py:403
  57.3 2.6 %collective-permute-start.12 = (f32[2,64,512]{2,1,0:T(8,128)}, f32[2,64,512]{2,1,0:T(8,128)S(1)}, u32[]{:S(2)}, u32[]{:S(2)}) collective-permute-start(f32[2,64,512]{2,1,0:T(8,128)} %get-tuple-element.56), channel_id=1, source_target_pairs={{0,6},{1,7},{2,4},{3,5},{4,2},{5,3},{6,0},{7,1},{8,14},{9,15},{10,... | collective-permute-start | bytes 786440 | tf_op jit(solution)/shard_map/ppermute | solution.py:267
  59.9 25.8 %collective-permute-done.12.refs_5_ = f32[2,64,512]{2,1,0:T(8,128)S(1)} collective-permute-done((f32[2,64,512]{2,1,0:T(8,128)}, f32[2,64,512]{2,1,0:T(8,128)S(1)}, u32[]{:S(2)}, u32[]{:S(2)}) %collective-permute-start.12) | collective-permute-done | bytes 262176 | tf_op jit(solution)/shard_map/ppermute | solution.py:267
  85.7 7.5 %collective-permute-done.13.refs_6_ = f32[2,64,512]{2,1,0:T(8,128)S(1)} collective-permute-done((f32[2,64,512]{2,1,0:T(8,128)}, f32[2,64,512]{2,1,0:T(8,128)S(1)}, u32[]{:S(2)}, u32[]{:S(2)}) %collective-permute-start.13) | collective-permute-done | bytes 262176 | tf_op jit(solution)/shard_map/ppermute | solution.py:267
  93.2 2.4 %multiples.3 = (f32[8,4,2,48,128]{4,3,2,1,0:T(8,128)}, f32[8,4,2,16,128]{4,3,2,1,0:T(8,128)}) custom-call(s32[4]{0:T(128)S(1)} %copy-done.1, s32[512,1]{1,0:T(8,128)S(1)} %copy.17.column_ref, s32[1,512]{1,0:T(1,128)S(1)} %bitcast.22, f32[16,2,64,512]{3,2,1,0:T(8,128)} %spectra_ref.7, f32[2,512,512]{2,1,0:T(8,128)S(1)} %gains.1.gains_hbm, ...), custom_call_target="tpu_custom_call" | custom-call | tf_op jit(solution)/shard_map/multiples/pallas_call | solution.py:360
  95.6 8.9 %all-to-all-done.1 = f32[32,2,64,128]{3,2,1,0:T(8,128)} async-done(((f32[32,2,64,128]{3,2,1,0:T(8,128)}), f32[32,2,64,128]{3,2,1,0:T(8,128)}, u32[]{:S(2)}, u32[]{:S(2)}) %all-to-all-start.1) | async-done | bytes 2097184 | tf_op jit(solution)/shard_map/all_to_all | solution.py:403
  104.5 4.1 %all-to-all-start.3 = ((f32[32,2,48,128]{3,2,1,0:T(8,128)}), f32[32,2,48,128]{3,2,1,0:T(8,128)S(1)}, u32[]{:S(2)}, u32[]{:S(2)}) async-start(f32[32,2,48,128]{3,2,1,0:T(8,128)} %bitcast.24), calls=%async_computation.3 | async-start | bytes 3145728 | tf_op jit(solution)/shard_map/all_to_all | solution.py:403
  109.5 16.4 %synthesis.3.refs_0_.refs_1_.refs_2_.refs_3_ = f32[128,64,512]{2,1,0:T(8,128)} custom-call(f32[64,512]{1,0:T(8,128)S(1)} %reshape.258.table_ref, f32[128,64,512]{2,1,0:T(8,128)} %refs_3_.1, f32[128,64,512]{2,1,0:T(8,128)} %refs_3_.1, f32[128,64,512]{2,1,0:T(8,128)} %refs_3_.1, f32[128,64,512]{2,1,0:T(8,128)} %refs_3_.1, f32[4096,128]{1,0:T(8,128)} %bitcast.14.refs_4_), custom_call_target="tpu_custom_call" | custom-call | tf_op jit(solution)/shard_map/synthesis/pallas_call | solution.py:308
  125.9 18.8 %all-to-all-done.3 = f32[32,2,48,128]{3,2,1,0:T(8,128)S(1)} async-done(((f32[32,2,48,128]{3,2,1,0:T(8,128)}), f32[32,2,48,128]{3,2,1,0:T(8,128)S(1)}, u32[]{:S(2)}, u32[]{:S(2)}) %all-to-all-start.3) | async-done | bytes 1572896 | tf_op jit(solution)/shard_map/all_to_all | solution.py:403
  144.6 4.6 %all-to-all-start.2 = ((f32[32,2,16,128]{3,2,1,0:T(8,128)}), f32[32,2,16,128]{3,2,1,0:T(8,128)S(1)}, u32[]{:S(2)}, u32[]{:S(2)}) async-start(f32[32,2,16,128]{3,2,1,0:T(8,128)} %bitcast.11), calls=%async_computation.2 | async-start | bytes 1048576 | tf_op jit(solution)/shard_map/all_to_all | solution.py:403
  149.9 11.1 %synthesis.4.refs_5_ = f32[128,64,512]{2,1,0:T(8,128)} custom-call(f32[64,512]{1,0:T(8,128)S(1)} %reshape.256.table_ref, f32[128,64,512]{2,1,0:T(8,128)} %synthesis.3.refs_0_.refs_1_.refs_2_.refs_3_, f32[128,64,512]{2,1,0:T(8,128)} %synthesis.3.refs_0_.refs_1_.refs_2_.refs_3_, f32[128,64,512]{2,1,0:T(8,128)} %synthesis.3.refs_0_.refs_1_.refs_2_.refs_3_, ...), custom_call_target="tpu_custom_call" | custom-call | tf_op jit(solution)/shard_map/synthesis/pallas_call | solution.py:308
  161.0 2.6 %all-to-all-done.2 = f32[32,2,16,128]{3,2,1,0:T(8,128)S(1)} async-done(((f32[32,2,16,128]{3,2,1,0:T(8,128)}), f32[32,2,16,128]{3,2,1,0:T(8,128)S(1)}, u32[]{:S(2)}, u32[]{:S(2)}) %all-to-all-start.2) | async-done | bytes 524320 | tf_op jit(solution)/shard_map/all_to_all | solution.py:403
  163.6 4.1 %synthesis.5 = f32[128,64,512]{2,1,0:T(8,128)} custom-call(f32[64,512]{1,0:T(8,128)S(1)} %reshape.256.table_ref, f32[128,64,512]{2,1,0:T(8,128)} %synthesis.3.refs_0_.refs_1_.refs_2_.refs_3_, f32[128,64,512]{2,1,0:T(8,128)} %synthesis.3.refs_0_.refs_1_.refs_2_.refs_3_, ...), custom_call_target="tpu_custom_call", output_to_operand_aliasing={{}: (6, {})} | custom-call | tf_op jit(solution)/shard_map/synthesis/pallas_call | solution.py:308
  (45 shorter events, 9.1 us)
Async XLA Ops:
  0.0 9.5 %copy-start.3 = (s32[128,64]{0,1:T(8,128)S(1)}, s32[128,64]{0,1:T(8,128)}, u32[]{:S(2)}) copy-start(s32[128,64]{0,1:T(8,128)} %param.10) | copy-start | bytes 98308
  0.0 6.9 %collective-permute-start.1 = (s32[64,128]{1,0:T(8,128)}, s32[64,128]{1,0:T(8,128)S(1)}, u32[]{:S(2)}, u32[]{:S(2)}) collective-permute-start(s32[64,128]{1,0:T(8,128)} %bitcast.29), channel_id=1, source_target_pairs={{0,4},{1,5},{2,6},{3,7},{4,0},{5,1},{6,2},{7,3},{8,12},{9,13},{10,... | collective-permute-start | bytes 98312 | tf_op jit(solution)/shard_map/ppermute | solution.py:267
  3.0 4.2 %collective-permute-start = (s32[64,128]{1,0:T(8,128)}, s32[64,128]{1,0:T(8,128)S(1)}, u32[]{:S(2)}, u32[]{:S(2)}) collective-permute-start(s32[64,128]{1,0:T(8,128)} %bitcast.30), channel_id=1, source_target_pairs={{0,2},{1,3},{2,0},{3,1},{4,6},{5,7},{6,4},{7,5},{8,10},{9,11},{10,... | collective-permute-start | bytes 98312 | tf_op jit(solution)/shard_map/ppermute | solution.py:267
  4.5 5.0 %collective-permute-start.2 = (s32[64,128]{1,0:T(8,128)}, s32[64,128]{1,0:T(8,128)S(1)}, u32[]{:S(2)}, u32[]{:S(2)}) collective-permute-start(s32[64,128]{1,0:T(8,128)} %bitcast.31), channel_id=1, source_target_pairs={{0,6},{1,7},{2,4},{3,5},{4,2},{5,3},{6,0},{7,1},{8,14},{9,15},{10,... | collective-permute-start | bytes 98312 | tf_op jit(solution)/shard_map/ppermute | solution.py:267
  9.5 31.2 %all-to-all-start = ((f32[8,2,64,512]{3,2,1,0:T(8,128)}), f32[8,2,64,512]{3,2,1,0:T(8,128)}, u32[]{:S(2)}, u32[]{:S(2)}) async-start(f32[8,2,64,512]{3,2,1,0:T(8,128)} %pack.2), calls=%async_computation | async-start | bytes 4194304 | tf_op jit(solution)/shard_map/all_to_all | solution.py:331
  13.9 17.8 %copy-start = (s32[512]{0:T(512)S(1)}, s32[512]{0:T(512)}, u32[]{:S(2)}) copy-start(s32[512]{0:T(512)} %param.8) | copy-start | bytes 6148
  13.9 19.7 %copy-start.2 = (f32[2,16]{1,0:T(2,128)S(1)}, f32[2,16]{1,0:T(2,128)}, u32[]{:S(2)}) copy-start(f32[2,16]{1,0:T(2,128)} %table_ref.1) | copy-start | bytes 388
  16.2 8.3 %collective-permute-start.5 = (s32[4,64,128]{2,1,0:T(8,128)S(1)}, s32[4,64,128]{2,1,0:T(8,128)S(1)}, u32[]{:S(2)}, u32[]{:S(2)}) collective-permute-start(s32[4,64,128]{2,1,0:T(8,128)S(1)} %pad_add_fusion.1), channel_id=1, source_target_pairs={{0,24},{8,16},{16,8},{24,0},{1,25},{9,17},{17,9},{25,1},{2,26},{10... | collective-permute-start | bytes 393224 | tf_op jit(solution)/shard_map/ppermute | solution.py:267
  19.9 11.6 %collective-permute-start.4 = (s32[4,64,128]{2,1,0:T(8,128)S(1)}, s32[4,64,128]{2,1,0:T(8,128)S(1)}, u32[]{:S(2)}, u32[]{:S(2)}) collective-permute-start(s32[4,64,128]{2,1,0:T(8,128)S(1)} %pad_add_fusion.1), channel_id=1, source_target_pairs={{0,16},{8,24},{16,0},{24,8},{1,17},{9,25},{17,1},{25,9},{2,18},{10... | collective-permute-start | bytes 393224 | tf_op jit(solution)/shard_map/ppermute | solution.py:267
  19.9 11.6 %collective-permute-start.3 = (s32[4,64,128]{2,1,0:T(8,128)S(1)}, s32[4,64,128]{2,1,0:T(8,128)S(1)}, u32[]{:S(2)}, u32[]{:S(2)}) collective-permute-start(s32[4,64,128]{2,1,0:T(8,128)S(1)} %pad_add_fusion.1), channel_id=1, source_target_pairs={{0,8},{8,0},{16,24},{24,16},{1,9},{9,1},{17,25},{25,17},{2,10},{10... | collective-permute-start | bytes 393224 | tf_op jit(solution)/shard_map/ppermute | solution.py:267
  31.5 9.1 %copy-start.1 = (s32[4]{0:T(128)S(1)}, s32[4]{0:T(128)}, u32[]{:S(2)}) copy-start(s32[4]{0:T(128)} %counts_ref.3) | copy-start | bytes 52
  31.6 2.0 %collective-permute-start.6 = (s32[4,4,64,128]{3,2,1,0:T(8,128)S(1)}, s32[4,4,64,128]{3,2,1,0:T(8,128)S(1)}, u32[]{:S(2)}, u32[]{:S(2)}) collective-permute-start(s32[4,4,64,128]{3,2,1,0:T(8,128)S(1)} %pad_add_fusion.near_ref), channel_id=1, source_target_pairs={{0,1},{1,0},{2,3},{3,2},{4,5},{5,4},{6,7},{7,6},{8,9},{9,8},{10,11... | collective-permute-start | bytes 1572872 | tf_op jit(solution)/shard_map/ppermute | solution.py:267
  36.1 16.3 %collective-permute-start.7 = (f32[2,64,512]{2,1,0:T(8,128)}, f32[2,64,512]{2,1,0:T(8,128)S(1)}, u32[]{:S(2)}, u32[]{:S(2)}) collective-permute-start(f32[2,64,512]{2,1,0:T(8,128)} %get-tuple-element.44), channel_id=1, source_target_pairs={{0,2},{1,3},{2,0},{3,1},{4,6},{5,7},{6,4},{7,5},{8,10},{9,11},{10,... | collective-permute-start | bytes 786440 | tf_op jit(solution)/shard_map/ppermute | solution.py:267
  37.8 14.6 %collective-permute-start.8 = (f32[2,64,512]{2,1,0:T(8,128)}, f32[2,64,512]{2,1,0:T(8,128)S(1)}, u32[]{:S(2)}, u32[]{:S(2)}) collective-permute-start(f32[2,64,512]{2,1,0:T(8,128)} %get-tuple-element.45), channel_id=1, source_target_pairs={{0,3},{1,2},{2,1},{3,0},{4,7},{5,6},{6,5},{7,4},{8,11},{9,10},{10,... | collective-permute-start | bytes 786440 | tf_op jit(solution)/shard_map/ppermute | solution.py:267
  37.8 14.6 %collective-permute-start.9 = (f32[2,64,512]{2,1,0:T(8,128)}, f32[2,64,512]{2,1,0:T(8,128)S(1)}, u32[]{:S(2)}, u32[]{:S(2)}) collective-permute-start(f32[2,64,512]{2,1,0:T(8,128)} %get-tuple-element.46), channel_id=1, source_target_pairs={{0,4},{1,5},{2,6},{3,7},{4,0},{5,1},{6,2},{7,3},{8,12},{9,13},{10,... | collective-permute-start | bytes 786440 | tf_op jit(solution)/shard_map/ppermute | solution.py:267
  39.3 13.1 %collective-permute-start.10 = (f32[2,64,512]{2,1,0:T(8,128)}, f32[2,64,512]{2,1,0:T(8,128)S(1)}, u32[]{:S(2)}, u32[]{:S(2)}) collective-permute-start(f32[2,64,512]{2,1,0:T(8,128)} %get-tuple-element.47), channel_id=1, source_target_pairs={{0,5},{1,4},{2,7},{3,6},{4,1},{5,0},{6,3},{7,2},{8,13},{9,12},{10,... | collective-permute-start | bytes 786440 | tf_op jit(solution)/shard_map/ppermute | solution.py:267
  52.4 52.1 %all-to-all-start.1 = ((f32[32,2,64,128]{3,2,1,0:T(8,128)}), f32[32,2,64,128]{3,2,1,0:T(8,128)}, u32[]{:S(2)}, u32[]{:S(2)}) async-start(f32[32,2,64,128]{3,2,1,0:T(8,128)} %bitcast.23), calls=%async_computation.1 | async-start | bytes 4194304 | tf_op jit(solution)/shard_map/all_to_all | solution.py:403
  57.0 2.8 %collective-permute-start.11 = (f32[2,64,512]{2,1,0:T(8,128)}, f32[2,64,512]{2,1,0:T(8,128)S(1)}, u32[]{:S(2)}, u32[]{:S(2)}) collective-permute-start(f32[2,64,512]{2,1,0:T(8,128)} %get-tuple-element.51), channel_id=1, source_target_pairs={{0,1},{1,0},{2,3},{3,2},{4,5},{5,4},{6,7},{7,6},{8,9},{9,8},{10,11... | collective-permute-start | bytes 786440 | tf_op jit(solution)/shard_map/ppermute | solution.py:267
  57.3 28.4 %collective-permute-start.12 = (f32[2,64,512]{2,1,0:T(8,128)}, f32[2,64,512]{2,1,0:T(8,128)S(1)}, u32[]{:S(2)}, u32[]{:S(2)}) collective-permute-start(f32[2,64,512]{2,1,0:T(8,128)} %get-tuple-element.56), channel_id=1, source_target_pairs={{0,6},{1,7},{2,4},{3,5},{4,2},{5,3},{6,0},{7,1},{8,14},{9,15},{10,... | collective-permute-start | bytes 786440 | tf_op jit(solution)/shard_map/ppermute | solution.py:267
  59.9 33.4 %collective-permute-start.13 = (f32[2,64,512]{2,1,0:T(8,128)}, f32[2,64,512]{2,1,0:T(8,128)S(1)}, u32[]{:S(2)}, u32[]{:S(2)}) collective-permute-start(f32[2,64,512]{2,1,0:T(8,128)} %get-tuple-element.57), channel_id=1, source_target_pairs={{0,7},{1,6},{2,5},{3,4},{4,3},{5,2},{6,1},{7,0},{8,15},{9,14},{10,... | collective-permute-start | bytes 786440 | tf_op jit(solution)/shard_map/ppermute | solution.py:267
  104.5 40.1 %all-to-all-start.3 = ((f32[32,2,48,128]{3,2,1,0:T(8,128)}), f32[32,2,48,128]{3,2,1,0:T(8,128)S(1)}, u32[]{:S(2)}, u32[]{:S(2)}) async-start(f32[32,2,48,128]{3,2,1,0:T(8,128)} %bitcast.24), calls=%async_computation.3 | async-start | bytes 3145728 | tf_op jit(solution)/shard_map/all_to_all | solution.py:403
  144.6 18.9 %all-to-all-start.2 = ((f32[32,2,16,128]{3,2,1,0:T(8,128)}), f32[32,2,16,128]{3,2,1,0:T(8,128)S(1)}, u32[]{:S(2)}, u32[]{:S(2)}) async-start(f32[32,2,16,128]{3,2,1,0:T(8,128)} %bitcast.11), calls=%async_computation.2 | async-start | bytes 1048576 | tf_op jit(solution)/shard_map/all_to_all | solution.py:403

commit v8 on v7

--- a/solution.py
+++ b/solution.py
@@ -31,6 +31,10 @@
 def gather_table(partner_column, start, size):
     columns = lax.broadcasted_iota(jnp.int32, (size, size), 1) + start
     return jnp.where(partner_column == columns, 1.0, 0.0).astype(jnp.bfloat16)
+
+
+def ring(count):
+    return [2 * ((n // 2) ^ (n // 4)) + n % 2 for n in range(count)]
 
 
 def scatter_table(partner_row, start, size):
@@ -72,7 +76,7 @@
     rank = lax.axis_index("rcv")
     loads, stores = [], []
     for n in range(stage.shape[0]):
-        slot = n if len(outs) == 1 else rank ^ (n + 1)
+        slot = ring(stage.shape[0])[n] if len(outs) == 1 else rank ^ (n + 1)
         out = outs[0].at[n] if len(outs) == 1 else outs[n]
         loads.append(pltpu.make_async_copy(spectra_ref.at[first_slot + slot], stage.at[n], in_sems.at[n]))
         stores.append(pltpu.make_async_copy(stage.at[n], out, out_sems.at[n]))
@@ -116,7 +120,7 @@
     @pl.when(live)
     def _():
         if len(tiles) == 1:
-            sources, origins = [tiles[0].at[n] for n in range(receiver_tiles)], range(receiver_tiles)
+            sources, origins = [tiles[0].at[n] for n in range(receiver_tiles)], ring(receiver_tiles)
         else:
             sources = [spectra_ref.at[first_slot + rank]] + list(tiles)
             origins = [rank ^ n for n in range(receiver_tiles)]
@@ -328,7 +332,10 @@
     near = jnp.stack([tile if n == 0 else exchange(tile, "rcv", 2 * n) for n in range(rcv_count // 2)])
     packed = pack(0, spectra, 1, (rcv_count,) + spectra.shape[1:])[0]
     packed, near = lax.optimization_barrier((packed, near))
-    gathered = [[lax.all_to_all(packed, "rcv", split_axis=0, concat_axis=0, tiled=True)]]
+    circle = [ring(rcv_count)]
+    gathered = [
+        [lax.all_to_all(packed, "rcv", split_axis=0, concat_axis=0, tiled=True, axis_index_groups=circle)]
+    ]
     later = [list(pack(part, spectra, rcv_count - 1, spectra.shape[1:])) for part in range(1, parts)]
     for packed in later:
         near, packed[0] = lax.optimization_barrier((near, packed[0]))

time: 169 us -> 169 us (level)
  no operation moved by 1% of the time
where the time goes in v8:
time: 169 us; the launch traced here: 168 us
  waiting for transfers between devices  79.6 us (47%)
  Pallas kernels  52.9 us (31%)
  starting transfers between devices  33.2 us (20%)
    ppermute x14, waiting for transfers between devices, exchange(): lax.ppermute(array, axis, [(i, i ^ distance) for i in range(lax.axis_size...  48.5 us
    pallas_call x3, Pallas kernels, synthesis(): pl.pallas_call(functools.partial(synthesis_kernel, receiver_tile=rows, pi...  31.6 us
    all_to_all x3, waiting for transfers between devices, on_device(): lax.all_to_all(pieces[n], ('rcv', 'freq'), split_axis=0, concat_axis=0, t...  30.2 us
    ppermute x14, starting transfers between devices, exchange(): lax.ppermute(array, axis, [(i, i ^ distance) for i in range(lax.axis_size...  15.4 us
    pallas_call x2, Pallas kernels, on_device(): pl.pallas_call(functools.partial(multiples_kernel, first_slot=part * rcv_...  14.1 us
    all_to_all x3, starting transfers between devices, on_device(): lax.all_to_all(pieces[n], ('rcv', 'freq'), split_axis=0, concat_axis=0, t...  13.5 us
    pallas_call x2, Pallas kernels, pack(): pl.pallas_call(functools.partial(pack_kernel, first_slot=part * rcv_count...  4.71 us
    all_to_all x1, starting transfers between devices, on_device(): lax.all_to_all(packed, 'rcv', split_axis=0, concat_axis=0, tiled=True, ax...  4.36 us
  transfers between devices with their start and end apart: 18, of which 11 were waited for; matrix products, arithmetic and copies ran while one was open for 1% of the time, Pallas kernels for 29%

profile of v8, /device:TPU:0, one launch (start us, length us, event | category | flops | bytes accessed | tf_op | source)
XLA Modules:
  0.0 167.8 jit_solution(1078743125571044278)
XLA Ops:
  0.0 3.0 %collective-permute-start.1 = (s32[64,128]{1,0:T(8,128)}, s32[64,128]{1,0:T(8,128)S(1)}, u32[]{:S(2)}, u32[]{:S(2)}) collective-permute-start(s32[64,128]{1,0:T(8,128)} %bitcast.29), channel_id=1, source_target_pairs={{0,4},{1,5},{2,6},{3,7},{4,0},{5,1},{6,2},{7,3},{8,12},{9,13},{10,... | collective-permute-start | bytes 98312 | tf_op jit(solution)/shard_map/ppermute | solution.py:271
  4.5 2.4 %pack.2 = f32[8,2,64,512]{3,2,1,0:T(8,128)} custom-call(f32[16,2,64,512]{3,2,1,0:T(8,128)} %spectra_ref.7), custom_call_target="tpu_custom_call" | custom-call | tf_op jit(solution)/shard_map/pack/pallas_call | solution.py:290
  7.2 2.3 %collective-permute-done.2 = s32[64,128]{1,0:T(8,128)S(1)} collective-permute-done((s32[64,128]{1,0:T(8,128)}, s32[64,128]{1,0:T(8,128)S(1)}, u32[]{:S(2)}, u32[]{:S(2)}) %collective-permute-start.2) | collective-permute-done | bytes 32800 | tf_op jit(solution)/shard_map/ppermute | solution.py:271
  9.5 4.4 %all-to-all-start = ((f32[8,2,64,512]{3,2,1,0:T(8,128)}), f32[8,2,64,512]{3,2,1,0:T(8,128)}, u32[]{:S(2)}, u32[]{:S(2)}) async-start(f32[8,2,64,512]{3,2,1,0:T(8,128)} %pack.2), calls=%async_computation | async-start | bytes 4194304 | tf_op jit(solution)/shard_map/all_to_all | solution.py:337
  13.9 2.3 %pack.3 = (f32[2,64,512]{2,1,0:T(8,128)}, f32[2,64,512]{2,1,0:T(8,128)}, f32[2,64,512]{2,1,0:T(8,128)}, f32[2,64,512]{2,1,0:T(8,128)}, f32[2,64,512]{2,1,0:T(8,1...) custom-call(f32[16,2,64,512]{3,2,1,0:T(8,128)} %spectra_ref.7), custom_call_target="tpu_custom_call" | custom-call | tf_op jit(solution)/shard_map/pack/pallas_call | solution.py:290
  16.2 3.7 %collective-permute-start.5 = (s32[4,64,128]{2,1,0:T(8,128)S(1)}, s32[4,64,128]{2,1,0:T(8,128)S(1)}, u32[]{:S(2)}, u32[]{:S(2)}) collective-permute-start(s32[4,64,128]{2,1,0:T(8,128)S(1)} %pad_add_fusion.1), channel_id=1, source_target_pairs={{0,24},{8,16},{16,8},{24,0},{1,25},{9,17},{17,9},{25,1},{2,26},{10... | collective-permute-start | bytes 393224 | tf_op jit(solution)/shard_map/ppermute | solution.py:271
  20.7 3.8 %collective-permute-done.5 = s32[4,64,128]{2,1,0:T(8,128)S(1)} collective-permute-done((s32[4,64,128]{2,1,0:T(8,128)S(1)}, s32[4,64,128]{2,1,0:T(8,128)S(1)}, u32[]{:S(2)}, u32[]{:S(2)}) %collective-permute-start.5) | collective-permute-done | bytes 131104 | tf_op jit(solution)/shard_map/ppermute | solution.py:271
  24.5 7.0 %collective-permute-done.4 = s32[4,64,128]{2,1,0:T(8,128)S(1)} collective-permute-done((s32[4,64,128]{2,1,0:T(8,128)S(1)}, s32[4,64,128]{2,1,0:T(8,128)S(1)}, u32[]{:S(2)}, u32[]{:S(2)}) %collective-permute-start.4) | collective-permute-done | bytes 131104 | tf_op jit(solution)/shard_map/ppermute | solution.py:271
  33.5 2.5 %gains.1.gains_hbm = f32[2,512,512]{2,1,0:T(8,128)S(1)} custom-call(f32[2,16]{1,0:T(2,128)S(1)} %copy-done.2, s32[4,4,64,128]{3,2,1,0:T(8,128)S(1)} %pad_add_fusion.near_ref, s32[4,4,64,128]{3,2,1,0:T(8,128)S(1)} %collective-permute-done.6.far_ref, s32[512,1]{1,0:T(8,128)S(1)} %copy.17.column_ref), custom_call_target="tpu_custom_call" | custom-call | tf_op jit(solution)/shard_map/gains/pallas_call | solution.py:344
  36.1 1.7 %collective-permute-start.7 = (f32[2,64,512]{2,1,0:T(8,128)}, f32[2,64,512]{2,1,0:T(8,128)S(1)}, u32[]{:S(2)}, u32[]{:S(2)}) collective-permute-start(f32[2,64,512]{2,1,0:T(8,128)} %get-tuple-element.44), channel_id=1, source_target_pairs={{0,2},{1,3},{2,0},{3,1},{4,6},{5,7},{6,4},{7,5},{8,10},{9,11},{10,... | collective-permute-start | bytes 786440 | tf_op jit(solution)/shard_map/ppermute | solution.py:271
  40.5 11.7 %multiples.2 = f32[8,4,2,64,128]{4,3,2,1,0:T(8,128)} custom-call(s32[4]{0:T(128)S(1)} %copy-done.1, s32[512,1]{1,0:T(8,128)S(1)} %copy.17.column_ref, s32[1,512]{1,0:T(1,128)S(1)} %bitcast.21, f32[16,2,64,512]{3,2,1,0:T(8,128)} %spectra_ref.7, f32[2,512,512]{2,1,0:T(8,128)S(1)} %gains.1.gains_hbm, f32[8,2,64,512]{3,2,1,0:T(8,128)} %all-to-all-done.refs_0_), custom_call_target="tpu_custom_call" | custom-call | tf_op jit(solution)/shard_map/multiples/pallas_call | solution.py:367
  52.3 4.8 %all-to-all-start.1 = ((f32[32,2,64,128]{3,2,1,0:T(8,128)}), f32[32,2,64,128]{3,2,1,0:T(8,128)}, u32[]{:S(2)}, u32[]{:S(2)}) async-start(f32[32,2,64,128]{3,2,1,0:T(8,128)} %bitcast.23), calls=%async_computation.1 | async-start | bytes 4194304 | tf_op jit(solution)/shard_map/all_to_all | solution.py:410
  57.3 2.6 %collective-permute-start.12 = (f32[2,64,512]{2,1,0:T(8,128)}, f32[2,64,512]{2,1,0:T(8,128)S(1)}, u32[]{:S(2)}, u32[]{:S(2)}) collective-permute-start(f32[2,64,512]{2,1,0:T(8,128)} %get-tuple-element.56), channel_id=1, source_target_pairs={{0,6},{1,7},{2,4},{3,5},{4,2},{5,3},{6,0},{7,1},{8,14},{9,15},{10,... | collective-permute-start | bytes 786440 | tf_op jit(solution)/shard_map/ppermute | solution.py:271
  59.9 25.8 %collective-permute-done.12.refs_5_ = f32[2,64,512]{2,1,0:T(8,128)S(1)} collective-permute-done((f32[2,64,512]{2,1,0:T(8,128)}, f32[2,64,512]{2,1,0:T(8,128)S(1)}, u32[]{:S(2)}, u32[]{:S(2)}) %collective-permute-start.12) | collective-permute-done | bytes 262176 | tf_op jit(solution)/shard_map/ppermute | solution.py:271
  85.7 7.5 %collective-permute-done.13.refs_6_ = f32[2,64,512]{2,1,0:T(8,128)S(1)} collective-permute-done((f32[2,64,512]{2,1,0:T(8,128)}, f32[2,64,512]{2,1,0:T(8,128)S(1)}, u32[]{:S(2)}, u32[]{:S(2)}) %collective-permute-start.13) | collective-permute-done | bytes 262176 | tf_op jit(solution)/shard_map/ppermute | solution.py:271
  93.2 2.4 %multiples.3 = (f32[8,4,2,48,128]{4,3,2,1,0:T(8,128)}, f32[8,4,2,16,128]{4,3,2,1,0:T(8,128)}) custom-call(s32[4]{0:T(128)S(1)} %copy-done.1, s32[512,1]{1,0:T(8,128)S(1)} %copy.17.column_ref, s32[1,512]{1,0:T(1,128)S(1)} %bitcast.22, f32[16,2,64,512]{3,2,1,0:T(8,128)} %spectra_ref.7, f32[2,512,512]{2,1,0:T(8,128)S(1)} %gains.1.gains_hbm, ...), custom_call_target="tpu_custom_call" | custom-call | tf_op jit(solution)/shard_map/multiples/pallas_call | solution.py:367
  95.6 8.9 %all-to-all-done.1 = f32[32,2,64,128]{3,2,1,0:T(8,128)} async-done(((f32[32,2,64,128]{3,2,1,0:T(8,128)}), f32[32,2,64,128]{3,2,1,0:T(8,128)}, u32[]{:S(2)}, u32[]{:S(2)}) %all-to-all-start.1) | async-done | bytes 2097184 | tf_op jit(solution)/shard_map/all_to_all | solution.py:410
  104.5 4.1 %all-to-all-start.3 = ((f32[32,2,48,128]{3,2,1,0:T(8,128)}), f32[32,2,48,128]{3,2,1,0:T(8,128)S(1)}, u32[]{:S(2)}, u32[]{:S(2)}) async-start(f32[32,2,48,128]{3,2,1,0:T(8,128)} %bitcast.24), calls=%async_computation.3 | async-start | bytes 3145728 | tf_op jit(solution)/shard_map/all_to_all | solution.py:410
  109.5 16.4 %synthesis.3.refs_0_.refs_1_.refs_2_.refs_3_ = f32[128,64,512]{2,1,0:T(8,128)} custom-call(f32[64,512]{1,0:T(8,128)S(1)} %reshape.258.table_ref, f32[128,64,512]{2,1,0:T(8,128)} %refs_3_.1, f32[128,64,512]{2,1,0:T(8,128)} %refs_3_.1, f32[128,64,512]{2,1,0:T(8,128)} %refs_3_.1, f32[128,64,512]{2,1,0:T(8,128)} %refs_3_.1, f32[4096,128]{1,0:T(8,128)} %bitcast.14.refs_4_), custom_call_target="tpu_custom_call" | custom-call | tf_op jit(solution)/shard_map/synthesis/pallas_call | solution.py:312
  125.9 18.8 %all-to-all-done.3 = f32[32,2,48,128]{3,2,1,0:T(8,128)S(1)} async-done(((f32[32,2,48,128]{3,2,1,0:T(8,128)}), f32[32,2,48,128]{3,2,1,0:T(8,128)S(1)}, u32[]{:S(2)}, u32[]{:S(2)}) %all-to-all-start.3) | async-done | bytes 1572896 | tf_op jit(solution)/shard_map/all_to_all | solution.py:410
  144.6 4.6 %all-to-all-start.2 = ((f32[32,2,16,128]{3,2,1,0:T(8,128)}), f32[32,2,16,128]{3,2,1,0:T(8,128)S(1)}, u32[]{:S(2)}, u32[]{:S(2)}) async-start(f32[32,2,16,128]{3,2,1,0:T(8,128)} %bitcast.11), calls=%async_computation.2 | async-start | bytes 1048576 | tf_op jit(solution)/shard_map/all_to_all | solution.py:410
  149.9 11.1 %synthesis.4.refs_5_ = f32[128,64,512]{2,1,0:T(8,128)} custom-call(f32[64,512]{1,0:T(8,128)S(1)} %reshape.256.table_ref, f32[128,64,512]{2,1,0:T(8,128)} %synthesis.3.refs_0_.refs_1_.refs_2_.refs_3_, f32[128,64,512]{2,1,0:T(8,128)} %synthesis.3.refs_0_.refs_1_.refs_2_.refs_3_, f32[128,64,512]{2,1,0:T(8,128)} %synthesis.3.refs_0_.refs_1_.refs_2_.refs_3_, ...), custom_call_target="tpu_custom_call" | custom-call | tf_op jit(solution)/shard_map/synthesis/pallas_call | solution.py:312
  161.0 2.6 %all-to-all-done.2 = f32[32,2,16,128]{3,2,1,0:T(8,128)S(1)} async-done(((f32[32,2,16,128]{3,2,1,0:T(8,128)}), f32[32,2,16,128]{3,2,1,0:T(8,128)S(1)}, u32[]{:S(2)}, u32[]{:S(2)}) %all-to-all-start.2) | async-done | bytes 524320 | tf_op jit(solution)/shard_map/all_to_all | solution.py:410
  163.6 4.1 %synthesis.5 = f32[128,64,512]{2,1,0:T(8,128)} custom-call(f32[64,512]{1,0:T(8,128)S(1)} %reshape.256.table_ref, f32[128,64,512]{2,1,0:T(8,128)} %synthesis.3.refs_0_.refs_1_.refs_2_.refs_3_, f32[128,64,512]{2,1,0:T(8,128)} %synthesis.3.refs_0_.refs_1_.refs_2_.refs_3_, ...), custom_call_target="tpu_custom_call", output_to_operand_aliasing={{}: (6, {})} | custom-call | tf_op jit(solution)/shard_map/synthesis/pallas_call | solution.py:312
  (45 shorter events, 9.0 us)
Async XLA Ops:
  0.0 9.5 %copy-start.3 = (s32[128,64]{0,1:T(8,128)S(1)}, s32[128,64]{0,1:T(8,128)}, u32[]{:S(2)}) copy-start(s32[128,64]{0,1:T(8,128)} %param.10) | copy-start | bytes 98308
  0.0 6.9 %collective-permute-start.1 = (s32[64,128]{1,0:T(8,128)}, s32[64,128]{1,0:T(8,128)S(1)}, u32[]{:S(2)}, u32[]{:S(2)}) collective-permute-start(s32[64,128]{1,0:T(8,128)} %bitcast.29), channel_id=1, source_target_pairs={{0,4},{1,5},{2,6},{3,7},{4,0},{5,1},{6,2},{7,3},{8,12},{9,13},{10,... | collective-permute-start | bytes 98312 | tf_op jit(solution)/shard_map/ppermute | solution.py:271
  3.0 4.2 %collective-permute-start = (s32[64,128]{1,0:T(8,128)}, s32[64,128]{1,0:T(8,128)S(1)}, u32[]{:S(2)}, u32[]{:S(2)}) collective-permute-start(s32[64,128]{1,0:T(8,128)} %bitcast.30), channel_id=1, source_target_pairs={{0,2},{1,3},{2,0},{3,1},{4,6},{5,7},{6,4},{7,5},{8,10},{9,11},{10,... | collective-permute-start | bytes 98312 | tf_op jit(solution)/shard_map/ppermute | solution.py:271
  4.5 5.0 %collective-permute-start.2 = (s32[64,128]{1,0:T(8,128)}, s32[64,128]{1,0:T(8,128)S(1)}, u32[]{:S(2)}, u32[]{:S(2)}) collective-permute-start(s32[64,128]{1,0:T(8,128)} %bitcast.31), channel_id=1, source_target_pairs={{0,6},{1,7},{2,4},{3,5},{4,2},{5,3},{6,0},{7,1},{8,14},{9,15},{10,... | collective-permute-start | bytes 98312 | tf_op jit(solution)/shard_map/ppermute | solution.py:271
  9.5 31.0 %all-to-all-start = ((f32[8,2,64,512]{3,2,1,0:T(8,128)}), f32[8,2,64,512]{3,2,1,0:T(8,128)}, u32[]{:S(2)}, u32[]{:S(2)}) async-start(f32[8,2,64,512]{3,2,1,0:T(8,128)} %pack.2), calls=%async_computation | async-start | bytes 4194304 | tf_op jit(solution)/shard_map/all_to_all | solution.py:337
  13.9 17.8 %copy-start = (s32[512]{0:T(512)S(1)}, s32[512]{0:T(512)}, u32[]{:S(2)}) copy-start(s32[512]{0:T(512)} %param.8) | copy-start | bytes 6148
  13.9 19.7 %copy-start.2 = (f32[2,16]{1,0:T(2,128)S(1)}, f32[2,16]{1,0:T(2,128)}, u32[]{:S(2)}) copy-start(f32[2,16]{1,0:T(2,128)} %table_ref.1) | copy-start | bytes 388
  16.2 8.3 %collective-permute-start.5 = (s32[4,64,128]{2,1,0:T(8,128)S(1)}, s32[4,64,128]{2,1,0:T(8,128)S(1)}, u32[]{:S(2)}, u32[]{:S(2)}) collective-permute-start(s32[4,64,128]{2,1,0:T(8,128)S(1)} %pad_add_fusion.1), channel_id=1, source_target_pairs={{0,24},{8,16},{16,8},{24,0},{1,25},{9,17},{17,9},{25,1},{2,26},{10... | collective-permute-start | bytes 393224 | tf_op jit(solution)/shard_map/ppermute | solution.py:271
  19.9 11.6 %collective-permute-start.4 = (s32[4,64,128]{2,1,0:T(8,128)S(1)}, s32[4,64,128]{2,1,0:T(8,128)S(1)}, u32[]{:S(2)}, u32[]{:S(2)}) collective-permute-start(s32[4,64,128]{2,1,0:T(8,128)S(1)} %pad_add_fusion.1), channel_id=1, source_target_pairs={{0,16},{8,24},{16,0},{24,8},{1,17},{9,25},{17,1},{25,9},{2,18},{10... | collective-permute-start | bytes 393224 | tf_op jit(solution)/shard_map/ppermute | solution.py:271
  19.9 11.6 %collective-permute-start.3 = (s32[4,64,128]{2,1,0:T(8,128)S(1)}, s32[4,64,128]{2,1,0:T(8,128)S(1)}, u32[]{:S(2)}, u32[]{:S(2)}) collective-permute-start(s32[4,64,128]{2,1,0:T(8,128)S(1)} %pad_add_fusion.1), channel_id=1, source_target_pairs={{0,8},{8,0},{16,24},{24,16},{1,9},{9,1},{17,25},{25,17},{2,10},{10... | collective-permute-start | bytes 393224 | tf_op jit(solution)/shard_map/ppermute | solution.py:271
  31.5 9.0 %copy-start.1 = (s32[4]{0:T(128)S(1)}, s32[4]{0:T(128)}, u32[]{:S(2)}) copy-start(s32[4]{0:T(128)} %counts_ref.3) | copy-start | bytes 52
  31.6 2.0 %collective-permute-start.6 = (s32[4,4,64,128]{3,2,1,0:T(8,128)S(1)}, s32[4,4,64,128]{3,2,1,0:T(8,128)S(1)}, u32[]{:S(2)}, u32[]{:S(2)}) collective-permute-start(s32[4,4,64,128]{3,2,1,0:T(8,128)S(1)} %pad_add_fusion.near_ref), channel_id=1, source_target_pairs={{0,1},{1,0},{2,3},{3,2},{4,5},{5,4},{6,7},{7,6},{8,9},{9,8},{10,11... | collective-permute-start | bytes 1572872 | tf_op jit(solution)/shard_map/ppermute | solution.py:271
  36.1 16.2 %collective-permute-start.7 = (f32[2,64,512]{2,1,0:T(8,128)}, f32[2,64,512]{2,1,0:T(8,128)S(1)}, u32[]{:S(2)}, u32[]{:S(2)}) collective-permute-start(f32[2,64,512]{2,1,0:T(8,128)} %get-tuple-element.44), channel_id=1, source_target_pairs={{0,2},{1,3},{2,0},{3,1},{4,6},{5,7},{6,4},{7,5},{8,10},{9,11},{10,... | collective-permute-start | bytes 786440 | tf_op jit(solution)/shard_map/ppermute | solution.py:271
  37.8 14.4 %collective-permute-start.8 = (f32[2,64,512]{2,1,0:T(8,128)}, f32[2,64,512]{2,1,0:T(8,128)S(1)}, u32[]{:S(2)}, u32[]{:S(2)}) collective-permute-start(f32[2,64,512]{2,1,0:T(8,128)} %get-tuple-element.45), channel_id=1, source_target_pairs={{0,3},{1,2},{2,1},{3,0},{4,7},{5,6},{6,5},{7,4},{8,11},{9,10},{10,... | collective-permute-start | bytes 786440 | tf_op jit(solution)/shard_map/ppermute | solution.py:271
  37.8 14.4 %collective-permute-start.9 = (f32[2,64,512]{2,1,0:T(8,128)}, f32[2,64,512]{2,1,0:T(8,128)S(1)}, u32[]{:S(2)}, u32[]{:S(2)}) collective-permute-start(f32[2,64,512]{2,1,0:T(8,128)} %get-tuple-element.46), channel_id=1, source_target_pairs={{0,4},{1,5},{2,6},{3,7},{4,0},{5,1},{6,2},{7,3},{8,12},{9,13},{10,... | collective-permute-start | bytes 786440 | tf_op jit(solution)/shard_map/ppermute | solution.py:271
  39.3 12.9 %collective-permute-start.10 = (f32[2,64,512]{2,1,0:T(8,128)}, f32[2,64,512]{2,1,0:T(8,128)S(1)}, u32[]{:S(2)}, u32[]{:S(2)}) collective-permute-start(f32[2,64,512]{2,1,0:T(8,128)} %get-tuple-element.47), channel_id=1, source_target_pairs={{0,5},{1,4},{2,7},{3,6},{4,1},{5,0},{6,3},{7,2},{8,13},{9,12},{10,... | collective-permute-start | bytes 786440 | tf_op jit(solution)/shard_map/ppermute | solution.py:271
  52.3 52.3 %all-to-all-start.1 = ((f32[32,2,64,128]{3,2,1,0:T(8,128)}), f32[32,2,64,128]{3,2,1,0:T(8,128)}, u32[]{:S(2)}, u32[]{:S(2)}) async-start(f32[32,2,64,128]{3,2,1,0:T(8,128)} %bitcast.23), calls=%async_computation.1 | async-start | bytes 4194304 | tf_op jit(solution)/shard_map/all_to_all | solution.py:410
  57.0 2.8 %collective-permute-start.11 = (f32[2,64,512]{2,1,0:T(8,128)}, f32[2,64,512]{2,1,0:T(8,128)S(1)}, u32[]{:S(2)}, u32[]{:S(2)}) collective-permute-start(f32[2,64,512]{2,1,0:T(8,128)} %get-tuple-element.51), channel_id=1, source_target_pairs={{0,1},{1,0},{2,3},{3,2},{4,5},{5,4},{6,7},{7,6},{8,9},{9,8},{10,11... | collective-permute-start | bytes 786440 | tf_op jit(solution)/shard_map/ppermute | solution.py:271
  57.3 28.4 %collective-permute-start.12 = (f32[2,64,512]{2,1,0:T(8,128)}, f32[2,64,512]{2,1,0:T(8,128)S(1)}, u32[]{:S(2)}, u32[]{:S(2)}) collective-permute-start(f32[2,64,512]{2,1,0:T(8,128)} %get-tuple-element.56), channel_id=1, source_target_pairs={{0,6},{1,7},{2,4},{3,5},{4,2},{5,3},{6,0},{7,1},{8,14},{9,15},{10,... | collective-permute-start | bytes 786440 | tf_op jit(solution)/shard_map/ppermute | solution.py:271
  59.9 33.4 %collective-permute-start.13 = (f32[2,64,512]{2,1,0:T(8,128)}, f32[2,64,512]{2,1,0:T(8,128)S(1)}, u32[]{:S(2)}, u32[]{:S(2)}) collective-permute-start(f32[2,64,512]{2,1,0:T(8,128)} %get-tuple-element.57), channel_id=1, source_target_pairs={{0,7},{1,6},{2,5},{3,4},{4,3},{5,2},{6,1},{7,0},{8,15},{9,14},{10,... | collective-permute-start | bytes 786440 | tf_op jit(solution)/shard_map/ppermute | solution.py:271
  104.5 40.1 %all-to-all-start.3 = ((f32[32,2,48,128]{3,2,1,0:T(8,128)}), f32[32,2,48,128]{3,2,1,0:T(8,128)S(1)}, u32[]{:S(2)}, u32[]{:S(2)}) async-start(f32[32,2,48,128]{3,2,1,0:T(8,128)} %bitcast.24), calls=%async_computation.3 | async-start | bytes 3145728 | tf_op jit(solution)/shard_map/all_to_all | solution.py:410
  144.6 18.9 %all-to-all-start.2 = ((f32[32,2,16,128]{3,2,1,0:T(8,128)}), f32[32,2,16,128]{3,2,1,0:T(8,128)S(1)}, u32[]{:S(2)}, u32[]{:S(2)}) async-start(f32[32,2,16,128]{3,2,1,0:T(8,128)} %bitcast.11), calls=%async_computation.2 | async-start | bytes 1048576 | tf_op jit(solution)/shard_map/all_to_all | solution.py:410

commit v9 on v7

--- a/solution.py
+++ b/solution.py
@@ -86,9 +86,9 @@
 
 
 def multiples_kernel(counts_ref, column_ref, row_ref, spectra_ref, gains_hbm, *refs, first_slot, cuts):
-    result, data, gains, u, w, y1, y2, tile_sems, gain_sem, out_sems = refs[-10:]
+    result, data, gains, own, u, w, y1, y2, tile_sems, gain_sem, out_sems = refs[-11:]
     receiver_tiles, source_tiles, _, receiver_tile, source_tile = result.shape
-    tiles, outs = refs[: -10 - len(cuts)], refs[-10 - len(cuts) : -10]
+    tiles, outs = refs[: -11 - len(cuts)], refs[-11 - len(cuts) : -11]
     side = data.shape[3]
     pick = min(PICK, side)
     rank = lax.axis_index("rcv")
@@ -127,31 +127,34 @@
         for n, copy in enumerate(copies):
             copy.wait()
             first_row = origins[n] * receiver_tile
-            real, imag = split(data[n, 0]), split(data[n, 1])
-            for place, part in ((0, 0), (1, 1), (2, 0)):
-                top, low = (
-                    pl.ds(pl.multiple_of(first_row + at * side, receiver_tile), receiver_tile)
-                    for at in (2 * place, 2 * place + 1)
-                )
-                w[top, :side] = real[part]
-                w[top, side:] = imag[part]
-                w[low, :side] = -imag[part]
-                w[low, side:] = real[part]
+            real, imag = data[n, 0], data[n, 1]
+            for g, value in enumerate((real, imag - real, real + imag)):
+                high, low = split(value)
+                for at, part in enumerate((high, low, high)):
+                    w[g, pl.ds(pl.multiple_of(first_row + at * side, receiver_tile), receiver_tile), :] = part
+            span = pl.ds(pl.multiple_of(first_row, receiver_tile), receiver_tile)
+            own[0, span, :], own[1, span, :] = split(imag)
         gain_copy.start()
-        high, again, low = (slice(n * 2 * side, (n + 1) * 2 * side) for n in range(3))
+        def put(g, rows, high, low):
+            u[g, rows, :side] = high
+            u[g, rows, side : 2 * side] = high
+            u[g, rows, 2 * side :] = low
+
         for start in range(0, side, pick):
-            rows = slice(start, start + pick)
+            rows, lows = slice(start, start + pick), slice(side + start, side + start + pick)
             table = gather_table(column_ref[rows, :], start, pick)
-            u[rows, high] = mm(table, w[rows, :]).astype(jnp.bfloat16)
-            u[rows, again] = u[rows, high]
-            u[rows, low] = mm(table, w[2 * side + start : 2 * side + start + pick, :]).astype(jnp.bfloat16)
+            pairs = ((w[2, rows, :], w[2, lows, :]), (w[0, rows, :], w[0, lows, :]), (own[0, rows, :], own[1, rows, :]))
+            for g, pair in enumerate(pairs):
+                put(g, rows, *(mm(table, half).astype(jnp.bfloat16) for half in pair))
 
         def product(result, beside=()):
-            columns = range(0, 2 * side, PICK)
+            columns = range(0, side, PICK)
             each = -(-len(beside) // len(columns))
             for n, start in enumerate(columns):
                 cols = slice(start, start + PICK)
-                result[:, cols] = mm(u[...], w[:, cols])
+                both, left, right = (mm(u[g], w[g, :, cols]) for g in range(3))
+                result[:, cols] = both - right
+                result[:, side + start : side + start + PICK] = both + left
                 for work in beside[n * each : (n + 1) * each]:
                     work()
 
@@ -170,8 +173,9 @@
         product(y1)
         for start in range(0, side, 64):
             rows = slice(start, start + 64)
-            u[rows, high], u[rows, low] = split(y1[rows, :])
-            u[rows, again] = u[rows, high]
+            real, imag = y1[rows, :side], y1[rows, side:]
+            for g, value in enumerate((real + imag, real, imag)):
+                put(g, rows, *split(value))
         gain_copy.wait()
         product(y2, [functools.partial(weigh, y1, 0, q, s) for q, s in pairs])
         for q, s in pairs:
@@ -366,8 +370,9 @@
                 pltpu.VMEM((rcv_count, freq_count, 2, receiver_tile, source_tile), jnp.float32),
                 pltpu.VMEM((rcv_count, 2, receiver_tile, side), jnp.float32),
                 pltpu.VMEM((2, side, side), jnp.float32),
-                pltpu.VMEM((side, 6 * side), jnp.bfloat16),
-                pltpu.VMEM((6 * side, 2 * side), jnp.bfloat16),
+                pltpu.VMEM((2, side, side), jnp.bfloat16),
+                pltpu.VMEM((3, side, 3 * side), jnp.bfloat16),
+                pltpu.VMEM((3, 3 * side, side), jnp.bfloat16),
                 pltpu.VMEM((side, 2 * side), jnp.float32),
                 pltpu.VMEM((side, 2 * side), jnp.float32),
                 pltpu.SemaphoreType.DMA((rcv_count,)),

time: 169 us -> 169 us (level)
  transfers between devices with their start and end apart: 18 -> 18, of which waited for: 11 -> 12; matrix products, arithmetic and copies ran while one was open for 1% -> 1% of each run, Pallas kernels for 29% -> 28%
where the time goes in v9:
time: 169 us; the launch traced here: 168 us
  waiting for transfers between devices  80.5 us (48%)
  Pallas kernels  51.7 us (31%)
  starting transfers between devices  33.6 us (20%)
    ppermute x14, waiting for transfers between devices, exchange(): lax.ppermute(array, axis, [(i, i ^ distance) for i in range(lax.axis_size...  49.2 us
    pallas_call x3, Pallas kernels, synthesis(): pl.pallas_call(functools.partial(synthesis_kernel, receiver_tile=rows, pi...  31.6 us
    all_to_all x3, waiting for transfers between devices, on_device(): lax.all_to_all(pieces[n], ('rcv', 'freq'), split_axis=0, concat_axis=0, t...  30.2 us
    ppermute x14, starting transfers between devices, exchange(): lax.ppermute(array, axis, [(i, i ^ distance) for i in range(lax.axis_size...  15.4 us
    all_to_all x3, starting transfers between devices, on_device(): lax.all_to_all(pieces[n], ('rcv', 'freq'), split_axis=0, concat_axis=0, t...  13.9 us
    pallas_call x2, Pallas kernels, on_device(): pl.pallas_call(functools.partial(multiples_kernel, first_slot=part * rcv_...  12.9 us
    pallas_call x2, Pallas kernels, pack(): pl.pallas_call(functools.partial(pack_kernel, first_slot=part * rcv_count...  4.71 us
    all_to_all x1, starting transfers between devices, on_device(): lax.all_to_all(packed, 'rcv', split_axis=0, concat_axis=0, tiled=True)  4.36 us
  transfers between devices with their start and end apart: 18, of which 12 were waited for; matrix products, arithmetic and copies ran while one was open for 1% of the time, Pallas kernels for 28%

profile of v9, /device:TPU:0, one launch (start us, length us, event | category | flops | bytes accessed | tf_op | source)
XLA Modules:
  0.0 167.8 jit_solution(15525777241940434570)
XLA Ops:
  0.0 3.0 %collective-permute-start.1 = (s32[64,128]{1,0:T(8,128)}, s32[64,128]{1,0:T(8,128)S(1)}, u32[]{:S(2)}, u32[]{:S(2)}) collective-permute-start(s32[64,128]{1,0:T(8,128)} %bitcast.29), channel_id=1, source_target_pairs={{0,4},{1,5},{2,6},{3,7},{4,0},{5,1},{6,2},{7,3},{8,12},{9,13},{10,... | collective-permute-start | bytes 98312 | tf_op jit(solution)/shard_map/ppermute | solution.py:271
  4.5 2.4 %pack.2 = f32[8,2,64,512]{3,2,1,0:T(8,128)} custom-call(f32[16,2,64,512]{3,2,1,0:T(8,128)} %spectra_ref.7), custom_call_target="tpu_custom_call" | custom-call | tf_op jit(solution)/shard_map/pack/pallas_call | solution.py:290
  7.2 2.3 %collective-permute-done.2 = s32[64,128]{1,0:T(8,128)S(1)} collective-permute-done((s32[64,128]{1,0:T(8,128)}, s32[64,128]{1,0:T(8,128)S(1)}, u32[]{:S(2)}, u32[]{:S(2)}) %collective-permute-start.2) | collective-permute-done | bytes 32800 | tf_op jit(solution)/shard_map/ppermute | solution.py:271
  9.5 4.4 %all-to-all-start = ((f32[8,2,64,512]{3,2,1,0:T(8,128)}), f32[8,2,64,512]{3,2,1,0:T(8,128)}, u32[]{:S(2)}, u32[]{:S(2)}) async-start(f32[8,2,64,512]{3,2,1,0:T(8,128)} %pack.2), calls=%async_computation | async-start | bytes 4194304 | tf_op jit(solution)/shard_map/all_to_all | solution.py:335
  13.9 2.3 %pack.3 = (f32[2,64,512]{2,1,0:T(8,128)}, f32[2,64,512]{2,1,0:T(8,128)}, f32[2,64,512]{2,1,0:T(8,128)}, f32[2,64,512]{2,1,0:T(8,128)}, f32[2,64,512]{2,1,0:T(8,1...) custom-call(f32[16,2,64,512]{3,2,1,0:T(8,128)} %spectra_ref.7), custom_call_target="tpu_custom_call" | custom-call | tf_op jit(solution)/shard_map/pack/pallas_call | solution.py:290
  16.2 3.7 %collective-permute-start.5 = (s32[4,64,128]{2,1,0:T(8,128)S(1)}, s32[4,64,128]{2,1,0:T(8,128)S(1)}, u32[]{:S(2)}, u32[]{:S(2)}) collective-permute-start(s32[4,64,128]{2,1,0:T(8,128)S(1)} %pad_add_fusion.1), channel_id=1, source_target_pairs={{0,24},{8,16},{16,8},{24,0},{1,25},{9,17},{17,9},{25,1},{2,26},{10... | collective-permute-start | bytes 393224 | tf_op jit(solution)/shard_map/ppermute | solution.py:271
  20.7 3.8 %collective-permute-done.5 = s32[4,64,128]{2,1,0:T(8,128)S(1)} collective-permute-done((s32[4,64,128]{2,1,0:T(8,128)S(1)}, s32[4,64,128]{2,1,0:T(8,128)S(1)}, u32[]{:S(2)}, u32[]{:S(2)}) %collective-permute-start.5) | collective-permute-done | bytes 131104 | tf_op jit(solution)/shard_map/ppermute | solution.py:271
  24.5 7.0 %collective-permute-done.4 = s32[4,64,128]{2,1,0:T(8,128)S(1)} collective-permute-done((s32[4,64,128]{2,1,0:T(8,128)S(1)}, s32[4,64,128]{2,1,0:T(8,128)S(1)}, u32[]{:S(2)}, u32[]{:S(2)}) %collective-permute-start.4) | collective-permute-done | bytes 131104 | tf_op jit(solution)/shard_map/ppermute | solution.py:271
  33.5 2.5 %gains.1.gains_hbm = f32[2,512,512]{2,1,0:T(8,128)S(1)} custom-call(f32[2,16]{1,0:T(2,128)S(1)} %copy-done.2, s32[4,4,64,128]{3,2,1,0:T(8,128)S(1)} %pad_add_fusion.near_ref, s32[4,4,64,128]{3,2,1,0:T(8,128)S(1)} %collective-permute-done.6.far_ref, s32[512,1]{1,0:T(8,128)S(1)} %copy.17.column_ref), custom_call_target="tpu_custom_call" | custom-call | tf_op jit(solution)/shard_map/gains/pallas_call | solution.py:341
  36.1 1.7 %collective-permute-start.7 = (f32[2,64,512]{2,1,0:T(8,128)}, f32[2,64,512]{2,1,0:T(8,128)S(1)}, u32[]{:S(2)}, u32[]{:S(2)}) collective-permute-start(f32[2,64,512]{2,1,0:T(8,128)} %get-tuple-element.44), channel_id=1, source_target_pairs={{0,2},{1,3},{2,0},{3,1},{4,6},{5,7},{6,4},{7,5},{8,10},{9,11},{10,... | collective-permute-start | bytes 786440 | tf_op jit(solution)/shard_map/ppermute | solution.py:271
  40.7 10.5 %multiples.2 = f32[8,4,2,64,128]{4,3,2,1,0:T(8,128)} custom-call(s32[4]{0:T(128)S(1)} %copy-done.1, s32[512,1]{1,0:T(8,128)S(1)} %copy.17.column_ref, s32[1,512]{1,0:T(1,128)S(1)} %bitcast.21, f32[16,2,64,512]{3,2,1,0:T(8,128)} %spectra_ref.7, f32[2,512,512]{2,1,0:T(8,128)S(1)} %gains.1.gains_hbm, f32[8,2,64,512]{3,2,1,0:T(8,128)} %all-to-all-done.refs_0_), custom_call_target="tpu_custom_call" | custom-call | tf_op jit(solution)/shard_map/multiples/pallas_call | solution.py:364
  51.9 5.2 %all-to-all-start.1 = ((f32[32,2,64,128]{3,2,1,0:T(8,128)}), f32[32,2,64,128]{3,2,1,0:T(8,128)}, u32[]{:S(2)}, u32[]{:S(2)}) async-start(f32[32,2,64,128]{3,2,1,0:T(8,128)} %bitcast.23), calls=%async_computation.1 | async-start | bytes 4194304 | tf_op jit(solution)/shard_map/all_to_all | solution.py:408
  57.3 2.6 %collective-permute-start.12 = (f32[2,64,512]{2,1,0:T(8,128)}, f32[2,64,512]{2,1,0:T(8,128)S(1)}, u32[]{:S(2)}, u32[]{:S(2)}) collective-permute-start(f32[2,64,512]{2,1,0:T(8,128)} %get-tuple-element.56), channel_id=1, source_target_pairs={{0,6},{1,7},{2,4},{3,5},{4,2},{5,3},{6,0},{7,1},{8,14},{9,15},{10,... | collective-permute-start | bytes 786440 | tf_op jit(solution)/shard_map/ppermute | solution.py:271
  59.9 25.8 %collective-permute-done.12.refs_5_ = f32[2,64,512]{2,1,0:T(8,128)S(1)} collective-permute-done((f32[2,64,512]{2,1,0:T(8,128)}, f32[2,64,512]{2,1,0:T(8,128)S(1)}, u32[]{:S(2)}, u32[]{:S(2)}) %collective-permute-start.12) | collective-permute-done | bytes 262176 | tf_op jit(solution)/shard_map/ppermute | solution.py:271
  85.7 7.5 %collective-permute-done.13.refs_6_ = f32[2,64,512]{2,1,0:T(8,128)S(1)} collective-permute-done((f32[2,64,512]{2,1,0:T(8,128)}, f32[2,64,512]{2,1,0:T(8,128)S(1)}, u32[]{:S(2)}, u32[]{:S(2)}) %collective-permute-start.13) | collective-permute-done | bytes 262176 | tf_op jit(solution)/shard_map/ppermute | solution.py:271
  93.2 2.4 %multiples.3 = (f32[8,4,2,48,128]{4,3,2,1,0:T(8,128)}, f32[8,4,2,16,128]{4,3,2,1,0:T(8,128)}) custom-call(s32[4]{0:T(128)S(1)} %copy-done.1, s32[512,1]{1,0:T(8,128)S(1)} %copy.17.column_ref, s32[1,512]{1,0:T(1,128)S(1)} %bitcast.22, f32[16,2,64,512]{3,2,1,0:T(8,128)} %spectra_ref.7, f32[2,512,512]{2,1,0:T(8,128)S(1)} %gains.1.gains_hbm, ...), custom_call_target="tpu_custom_call" | custom-call | tf_op jit(solution)/shard_map/multiples/pallas_call | solution.py:364
  95.6 8.9 %all-to-all-done.1 = f32[32,2,64,128]{3,2,1,0:T(8,128)} async-done(((f32[32,2,64,128]{3,2,1,0:T(8,128)}), f32[32,2,64,128]{3,2,1,0:T(8,128)}, u32[]{:S(2)}, u32[]{:S(2)}) %all-to-all-start.1) | async-done | bytes 2097184 | tf_op jit(solution)/shard_map/all_to_all | solution.py:408
  104.5 4.1 %all-to-all-start.3 = ((f32[32,2,48,128]{3,2,1,0:T(8,128)}), f32[32,2,48,128]{3,2,1,0:T(8,128)S(1)}, u32[]{:S(2)}, u32[]{:S(2)}) async-start(f32[32,2,48,128]{3,2,1,0:T(8,128)} %bitcast.24), calls=%async_computation.3 | async-start | bytes 3145728 | tf_op jit(solution)/shard_map/all_to_all | solution.py:408
  109.5 16.4 %synthesis.3.refs_0_.refs_1_.refs_2_.refs_3_ = f32[128,64,512]{2,1,0:T(8,128)} custom-call(f32[64,512]{1,0:T(8,128)S(1)} %reshape.258.table_ref, f32[128,64,512]{2,1,0:T(8,128)} %refs_3_.1, f32[128,64,512]{2,1,0:T(8,128)} %refs_3_.1, f32[128,64,512]{2,1,0:T(8,128)} %refs_3_.1, f32[128,64,512]{2,1,0:T(8,128)} %refs_3_.1, f32[4096,128]{1,0:T(8,128)} %bitcast.14.refs_4_), custom_call_target="tpu_custom_call" | custom-call | tf_op jit(solution)/shard_map/synthesis/pallas_call | solution.py:312
  125.9 18.8 %all-to-all-done.3 = f32[32,2,48,128]{3,2,1,0:T(8,128)S(1)} async-done(((f32[32,2,48,128]{3,2,1,0:T(8,128)}), f32[32,2,48,128]{3,2,1,0:T(8,128)S(1)}, u32[]{:S(2)}, u32[]{:S(2)}) %all-to-all-start.3) | async-done | bytes 1572896 | tf_op jit(solution)/shard_map/all_to_all | solution.py:408
  144.6 4.6 %all-to-all-start.2 = ((f32[32,2,16,128]{3,2,1,0:T(8,128)}), f32[32,2,16,128]{3,2,1,0:T(8,128)S(1)}, u32[]{:S(2)}, u32[]{:S(2)}) async-start(f32[32,2,16,128]{3,2,1,0:T(8,128)} %bitcast.11), calls=%async_computation.2 | async-start | bytes 1048576 | tf_op jit(solution)/shard_map/all_to_all | solution.py:408
  149.9 11.1 %synthesis.4.refs_5_ = f32[128,64,512]{2,1,0:T(8,128)} custom-call(f32[64,512]{1,0:T(8,128)S(1)} %reshape.256.table_ref, f32[128,64,512]{2,1,0:T(8,128)} %synthesis.3.refs_0_.refs_1_.refs_2_.refs_3_, f32[128,64,512]{2,1,0:T(8,128)} %synthesis.3.refs_0_.refs_1_.refs_2_.refs_3_, f32[128,64,512]{2,1,0:T(8,128)} %synthesis.3.refs_0_.refs_1_.refs_2_.refs_3_, ...), custom_call_target="tpu_custom_call" | custom-call | tf_op jit(solution)/shard_map/synthesis/pallas_call | solution.py:312
  161.0 2.6 %all-to-all-done.2 = f32[32,2,16,128]{3,2,1,0:T(8,128)S(1)} async-done(((f32[32,2,16,128]{3,2,1,0:T(8,128)}), f32[32,2,16,128]{3,2,1,0:T(8,128)S(1)}, u32[]{:S(2)}, u32[]{:S(2)}) %all-to-all-start.2) | async-done | bytes 524320 | tf_op jit(solution)/shard_map/all_to_all | solution.py:408
  163.6 4.1 %synthesis.5 = f32[128,64,512]{2,1,0:T(8,128)} custom-call(f32[64,512]{1,0:T(8,128)S(1)} %reshape.256.table_ref, f32[128,64,512]{2,1,0:T(8,128)} %synthesis.3.refs_0_.refs_1_.refs_2_.refs_3_, f32[128,64,512]{2,1,0:T(8,128)} %synthesis.3.refs_0_.refs_1_.refs_2_.refs_3_, ...), custom_call_target="tpu_custom_call", output_to_operand_aliasing={{}: (6, {})} | custom-call | tf_op jit(solution)/shard_map/synthesis/pallas_call | solution.py:312
  (45 shorter events, 9.8 us)
Async XLA Ops:
  0.0 9.5 %copy-start.3 = (s32[128,64]{0,1:T(8,128)S(1)}, s32[128,64]{0,1:T(8,128)}, u32[]{:S(2)}) copy-start(s32[128,64]{0,1:T(8,128)} %param.10) | copy-start | bytes 98308
  0.0 6.9 %collective-permute-start.1 = (s32[64,128]{1,0:T(8,128)}, s32[64,128]{1,0:T(8,128)S(1)}, u32[]{:S(2)}, u32[]{:S(2)}) collective-permute-start(s32[64,128]{1,0:T(8,128)} %bitcast.29), channel_id=1, source_target_pairs={{0,4},{1,5},{2,6},{3,7},{4,0},{5,1},{6,2},{7,3},{8,12},{9,13},{10,... | collective-permute-start | bytes 98312 | tf_op jit(solution)/shard_map/ppermute | solution.py:271
  3.0 4.2 %collective-permute-start = (s32[64,128]{1,0:T(8,128)}, s32[64,128]{1,0:T(8,128)S(1)}, u32[]{:S(2)}, u32[]{:S(2)}) collective-permute-start(s32[64,128]{1,0:T(8,128)} %bitcast.30), channel_id=1, source_target_pairs={{0,2},{1,3},{2,0},{3,1},{4,6},{5,7},{6,4},{7,5},{8,10},{9,11},{10,... | collective-permute-start | bytes 98312 | tf_op jit(solution)/shard_map/ppermute | solution.py:271
  4.5 5.0 %collective-permute-start.2 = (s32[64,128]{1,0:T(8,128)}, s32[64,128]{1,0:T(8,128)S(1)}, u32[]{:S(2)}, u32[]{:S(2)}) collective-permute-start(s32[64,128]{1,0:T(8,128)} %bitcast.31), channel_id=1, source_target_pairs={{0,6},{1,7},{2,4},{3,5},{4,2},{5,3},{6,0},{7,1},{8,14},{9,15},{10,... | collective-permute-start | bytes 98312 | tf_op jit(solution)/shard_map/ppermute | solution.py:271
  9.5 31.2 %all-to-all-start = ((f32[8,2,64,512]{3,2,1,0:T(8,128)}), f32[8,2,64,512]{3,2,1,0:T(8,128)}, u32[]{:S(2)}, u32[]{:S(2)}) async-start(f32[8,2,64,512]{3,2,1,0:T(8,128)} %pack.2), calls=%async_computation | async-start | bytes 4194304 | tf_op jit(solution)/shard_map/all_to_all | solution.py:335
  13.9 17.8 %copy-start = (s32[512]{0:T(512)S(1)}, s32[512]{0:T(512)}, u32[]{:S(2)}) copy-start(s32[512]{0:T(512)} %param.8) | copy-start | bytes 6148
  13.9 19.7 %copy-start.2 = (f32[2,16]{1,0:T(2,128)S(1)}, f32[2,16]{1,0:T(2,128)}, u32[]{:S(2)}) copy-start(f32[2,16]{1,0:T(2,128)} %table_ref.1) | copy-start | bytes 388
  16.2 8.3 %collective-permute-start.5 = (s32[4,64,128]{2,1,0:T(8,128)S(1)}, s32[4,64,128]{2,1,0:T(8,128)S(1)}, u32[]{:S(2)}, u32[]{:S(2)}) collective-permute-start(s32[4,64,128]{2,1,0:T(8,128)S(1)} %pad_add_fusion.1), channel_id=1, source_target_pairs={{0,24},{8,16},{16,8},{24,0},{1,25},{9,17},{17,9},{25,1},{2,26},{10... | collective-permute-start | bytes 393224 | tf_op jit(solution)/shard_map/ppermute | solution.py:271
  19.9 11.6 %collective-permute-start.4 = (s32[4,64,128]{2,1,0:T(8,128)S(1)}, s32[4,64,128]{2,1,0:T(8,128)S(1)}, u32[]{:S(2)}, u32[]{:S(2)}) collective-permute-start(s32[4,64,128]{2,1,0:T(8,128)S(1)} %pad_add_fusion.1), channel_id=1, source_target_pairs={{0,16},{8,24},{16,0},{24,8},{1,17},{9,25},{17,1},{25,9},{2,18},{10... | collective-permute-start | bytes 393224 | tf_op jit(solution)/shard_map/ppermute | solution.py:271
  19.9 11.6 %collective-permute-start.3 = (s32[4,64,128]{2,1,0:T(8,128)S(1)}, s32[4,64,128]{2,1,0:T(8,128)S(1)}, u32[]{:S(2)}, u32[]{:S(2)}) collective-permute-start(s32[4,64,128]{2,1,0:T(8,128)S(1)} %pad_add_fusion.1), channel_id=1, source_target_pairs={{0,8},{8,0},{16,24},{24,16},{1,9},{9,1},{17,25},{25,17},{2,10},{10... | collective-permute-start | bytes 393224 | tf_op jit(solution)/shard_map/ppermute | solution.py:271
  31.5 9.1 %copy-start.1 = (s32[4]{0:T(128)S(1)}, s32[4]{0:T(128)}, u32[]{:S(2)}) copy-start(s32[4]{0:T(128)} %counts_ref.3) | copy-start | bytes 52
  31.6 2.0 %collective-permute-start.6 = (s32[4,4,64,128]{3,2,1,0:T(8,128)S(1)}, s32[4,4,64,128]{3,2,1,0:T(8,128)S(1)}, u32[]{:S(2)}, u32[]{:S(2)}) collective-permute-start(s32[4,4,64,128]{3,2,1,0:T(8,128)S(1)} %pad_add_fusion.near_ref), channel_id=1, source_target_pairs={{0,1},{1,0},{2,3},{3,2},{4,5},{5,4},{6,7},{7,6},{8,9},{9,8},{10,11... | collective-permute-start | bytes 1572872 | tf_op jit(solution)/shard_map/ppermute | solution.py:271
  36.1 15.1 %collective-permute-start.7 = (f32[2,64,512]{2,1,0:T(8,128)}, f32[2,64,512]{2,1,0:T(8,128)S(1)}, u32[]{:S(2)}, u32[]{:S(2)}) collective-permute-start(f32[2,64,512]{2,1,0:T(8,128)} %get-tuple-element.44), channel_id=1, source_target_pairs={{0,2},{1,3},{2,0},{3,1},{4,6},{5,7},{6,4},{7,5},{8,10},{9,11},{10,... | collective-permute-start | bytes 786440 | tf_op jit(solution)/shard_map/ppermute | solution.py:271
  37.8 13.4 %collective-permute-start.8 = (f32[2,64,512]{2,1,0:T(8,128)}, f32[2,64,512]{2,1,0:T(8,128)S(1)}, u32[]{:S(2)}, u32[]{:S(2)}) collective-permute-start(f32[2,64,512]{2,1,0:T(8,128)} %get-tuple-element.45), channel_id=1, source_target_pairs={{0,3},{1,2},{2,1},{3,0},{4,7},{5,6},{6,5},{7,4},{8,11},{9,10},{10,... | collective-permute-start | bytes 786440 | tf_op jit(solution)/shard_map/ppermute | solution.py:271
  37.8 13.4 %collective-permute-start.9 = (f32[2,64,512]{2,1,0:T(8,128)}, f32[2,64,512]{2,1,0:T(8,128)S(1)}, u32[]{:S(2)}, u32[]{:S(2)}) collective-permute-start(f32[2,64,512]{2,1,0:T(8,128)} %get-tuple-element.46), channel_id=1, source_target_pairs={{0,4},{1,5},{2,6},{3,7},{4,0},{5,1},{6,2},{7,3},{8,12},{9,13},{10,... | collective-permute-start | bytes 786440 | tf_op jit(solution)/shard_map/ppermute | solution.py:271
  39.3 12.5 %collective-permute-start.10 = (f32[2,64,512]{2,1,0:T(8,128)}, f32[2,64,512]{2,1,0:T(8,128)S(1)}, u32[]{:S(2)}, u32[]{:S(2)}) collective-permute-start(f32[2,64,512]{2,1,0:T(8,128)} %get-tuple-element.47), channel_id=1, source_target_pairs={{0,5},{1,4},{2,7},{3,6},{4,1},{5,0},{6,3},{7,2},{8,13},{9,12},{10,... | collective-permute-start | bytes 786440 | tf_op jit(solution)/shard_map/ppermute | solution.py:271
  51.9 52.7 %all-to-all-start.1 = ((f32[32,2,64,128]{3,2,1,0:T(8,128)}), f32[32,2,64,128]{3,2,1,0:T(8,128)}, u32[]{:S(2)}, u32[]{:S(2)}) async-start(f32[32,2,64,128]{3,2,1,0:T(8,128)} %bitcast.23), calls=%async_computation.1 | async-start | bytes 4194304 | tf_op jit(solution)/shard_map/all_to_all | solution.py:408
  57.0 2.8 %collective-permute-start.11 = (f32[2,64,512]{2,1,0:T(8,128)}, f32[2,64,512]{2,1,0:T(8,128)S(1)}, u32[]{:S(2)}, u32[]{:S(2)}) collective-permute-start(f32[2,64,512]{2,1,0:T(8,128)} %get-tuple-element.51), channel_id=1, source_target_pairs={{0,1},{1,0},{2,3},{3,2},{4,5},{5,4},{6,7},{7,6},{8,9},{9,8},{10,11... | collective-permute-start | bytes 786440 | tf_op jit(solution)/shard_map/ppermute | solution.py:271
  57.3 28.4 %collective-permute-start.12 = (f32[2,64,512]{2,1,0:T(8,128)}, f32[2,64,512]{2,1,0:T(8,128)S(1)}, u32[]{:S(2)}, u32[]{:S(2)}) collective-permute-start(f32[2,64,512]{2,1,0:T(8,128)} %get-tuple-element.56), channel_id=1, source_target_pairs={{0,6},{1,7},{2,4},{3,5},{4,2},{5,3},{6,0},{7,1},{8,14},{9,15},{10,... | collective-permute-start | bytes 786440 | tf_op jit(solution)/shard_map/ppermute | solution.py:271
  59.9 33.4 %collective-permute-start.13 = (f32[2,64,512]{2,1,0:T(8,128)}, f32[2,64,512]{2,1,0:T(8,128)S(1)}, u32[]{:S(2)}, u32[]{:S(2)}) collective-permute-start(f32[2,64,512]{2,1,0:T(8,128)} %get-tuple-element.57), channel_id=1, source_target_pairs={{0,7},{1,6},{2,5},{3,4},{4,3},{5,2},{6,1},{7,0},{8,15},{9,14},{10,... | collective-permute-start | bytes 786440 | tf_op jit(solution)/shard_map/ppermute | solution.py:271
  104.5 40.1 %all-to-all-start.3 = ((f32[32,2,48,128]{3,2,1,0:T(8,128)}), f32[32,2,48,128]{3,2,1,0:T(8,128)S(1)}, u32[]{:S(2)}, u32[]{:S(2)}) async-start(f32[32,2,48,128]{3,2,1,0:T(8,128)} %bitcast.24), calls=%async_computation.3 | async-start | bytes 3145728 | tf_op jit(solution)/shard_map/all_to_all | solution.py:408
  144.6 18.9 %all-to-all-start.2 = ((f32[32,2,16,128]{3,2,1,0:T(8,128)}), f32[32,2,16,128]{3,2,1,0:T(8,128)S(1)}, u32[]{:S(2)}, u32[]{:S(2)}) async-start(f32[32,2,16,128]{3,2,1,0:T(8,128)} %bitcast.11), calls=%async_computation.2 | async-start | bytes 1048576 | tf_op jit(solution)/shard_map/all_to_all | solution.py:408

commit v10 on v9

--- a/solution.py
+++ b/solution.py
@@ -387,8 +387,9 @@
             packed = later[part]
             near_tiles = [exchange(tile, "rcv", n + 2) for n, tile in enumerate(packed[nearest])]
             far_tiles = [packed[0]] + packed[nearest.stop :]
-            result[0], *both = lax.optimization_barrier((result[0], *near_tiles, *far_tiles))
-            near_tiles, far_tiles = both[: len(near_tiles)], both[len(near_tiles) :]
+            tied = near_tiles[::2]
+            result[0], *both = lax.optimization_barrier((result[0], *tied, *far_tiles))
+            near_tiles[::2], far_tiles = both[: len(tied)], both[len(tied) :]
             distances = [1] + list(range(nearest.stop + 1, rcv_count))
             far_tiles = [exchange(tile, "rcv", n) for n, tile in zip(distances, far_tiles)]
             gathered.append(far_tiles[:1] + near_tiles + far_tiles[1:])

time: 169 us -> 173 us (1.024)
  starting transfers between devices: 33.6 us -> 41.6 us
  waiting for transfers between devices: 80.5 us -> 77.2 us
    all_to_all x3, starting transfers between devices: 13.9 us -> 19.3 us  [on_device(): lax.all_to_all(pieces[n], ('rcv', 'freq'), split_axis=0, concat_axis=0, t...]
    all_to_all x3, waiting for transfers between devices: 30.2 us -> 25 us  [on_device(): lax.all_to_all(pieces[n], ('rcv', 'freq'), split_axis=0, concat_axis=0, t...]
    ppermute x14, starting transfers between devices: 15.4 us -> 18 us  [exchange(): lax.ppermute(array, axis, [(i, i ^ distance) for i in range(lax.axis_size...]
  transfers between devices with their start and end apart: 18 -> 18, of which waited for: 12 -> 13; matrix products, arithmetic and copies ran while one was open for 1% -> 1% of each run, Pallas kernels for 28% -> 28%
where the time goes in v10:
time: 173 us
  waiting for transfers between devices  77.2 us (45%)
  Pallas kernels  51.7 us (30%)
  starting transfers between devices  41.6 us (24%)
    ppermute x14, waiting for transfers between devices, exchange(): lax.ppermute(array, axis, [(i, i ^ distance) for i in range(lax.axis_size...  50.8 us
    pallas_call x3, Pallas kernels, synthesis(): pl.pallas_call(functools.partial(synthesis_kernel, receiver_tile=rows, pi...  31.6 us
    all_to_all x3, waiting for transfers between devices, on_device(): lax.all_to_all(pieces[n], ('rcv', 'freq'), split_axis=0, concat_axis=0, t...  25 us
    all_to_all x3, starting transfers between devices, on_device(): lax.all_to_all(pieces[n], ('rcv', 'freq'), split_axis=0, concat_axis=0, t...  19.3 us
    ppermute x14, starting transfers between devices, exchange(): lax.ppermute(array, axis, [(i, i ^ distance) for i in range(lax.axis_size...  18 us
    pallas_call x2, Pallas kernels, on_device(): pl.pallas_call(functools.partial(multiples_kernel, first_slot=part * rcv_...  12.9 us
    pallas_call x2, Pallas kernels, pack(): pl.pallas_call(functools.partial(pack_kernel, first_slot=part * rcv_count...  4.72 us
    all_to_all x1, starting transfers between devices, on_device(): lax.all_to_all(packed, 'rcv', split_axis=0, concat_axis=0, tiled=True)  4.36 us
  transfers between devices with their start and end apart: 18, of which 13 were waited for; matrix products, arithmetic and copies ran while one was open for 1% of the time, Pallas kernels for 28%

profile of v10, /device:TPU:0, one launch (start us, length us, event | category | flops | bytes accessed | tf_op | source)
XLA Modules:
  0.0 172.6 jit_solution(270309402455005976)
XLA Ops:
  0.0 3.0 %collective-permute-start.1 = (s32[64,128]{1,0:T(8,128)}, s32[64,128]{1,0:T(8,128)S(1)}, u32[]{:S(2)}, u32[]{:S(2)}) collective-permute-start(s32[64,128]{1,0:T(8,128)} %bitcast.29), channel_id=1, source_target_pairs={{0,4},{1,5},{2,6},{3,7},{4,0},{5,1},{6,2},{7,3},{8,12},{9,13},{10,... | collective-permute-start | bytes 98312 | tf_op jit(solution)/shard_map/ppermute | solution.py:271
  4.5 2.4 %pack.2 = f32[8,2,64,512]{3,2,1,0:T(8,128)} custom-call(f32[16,2,64,512]{3,2,1,0:T(8,128)} %spectra_ref.7), custom_call_target="tpu_custom_call" | custom-call | tf_op jit(solution)/shard_map/pack/pallas_call | solution.py:290
  7.2 2.3 %collective-permute-done.2 = s32[64,128]{1,0:T(8,128)S(1)} collective-permute-done((s32[64,128]{1,0:T(8,128)}, s32[64,128]{1,0:T(8,128)S(1)}, u32[]{:S(2)}, u32[]{:S(2)}) %collective-permute-start.2) | collective-permute-done | bytes 32800 | tf_op jit(solution)/shard_map/ppermute | solution.py:271
  9.5 4.4 %all-to-all-start = ((f32[8,2,64,512]{3,2,1,0:T(8,128)}), f32[8,2,64,512]{3,2,1,0:T(8,128)}, u32[]{:S(2)}, u32[]{:S(2)}) async-start(f32[8,2,64,512]{3,2,1,0:T(8,128)} %pack.2), calls=%async_computation | async-start | bytes 4194304 | tf_op jit(solution)/shard_map/all_to_all | solution.py:335
  13.9 2.3 %pack.3 = (f32[2,64,512]{2,1,0:T(8,128)}, f32[2,64,512]{2,1,0:T(8,128)}, f32[2,64,512]{2,1,0:T(8,128)}, f32[2,64,512]{2,1,0:T(8,128)}, f32[2,64,512]{2,1,0:T(8,1...) custom-call(f32[16,2,64,512]{3,2,1,0:T(8,128)} %spectra_ref.7), custom_call_target="tpu_custom_call" | custom-call | tf_op jit(solution)/shard_map/pack/pallas_call | solution.py:290
  16.2 3.7 %collective-permute-start.5 = (s32[4,64,128]{2,1,0:T(8,128)S(1)}, s32[4,64,128]{2,1,0:T(8,128)S(1)}, u32[]{:S(2)}, u32[]{:S(2)}) collective-permute-start(s32[4,64,128]{2,1,0:T(8,128)S(1)} %pad_add_fusion.1), channel_id=1, source_target_pairs={{0,24},{8,16},{16,8},{24,0},{1,25},{9,17},{17,9},{25,1},{2,26},{10... | collective-permute-start | bytes 393224 | tf_op jit(solution)/shard_map/ppermute | solution.py:271
  20.7 3.8 %collective-permute-done.5 = s32[4,64,128]{2,1,0:T(8,128)S(1)} collective-permute-done((s32[4,64,128]{2,1,0:T(8,128)S(1)}, s32[4,64,128]{2,1,0:T(8,128)S(1)}, u32[]{:S(2)}, u32[]{:S(2)}) %collective-permute-start.5) | collective-permute-done | bytes 131104 | tf_op jit(solution)/shard_map/ppermute | solution.py:271
  24.5 7.0 %collective-permute-done.4 = s32[4,64,128]{2,1,0:T(8,128)S(1)} collective-permute-done((s32[4,64,128]{2,1,0:T(8,128)S(1)}, s32[4,64,128]{2,1,0:T(8,128)S(1)}, u32[]{:S(2)}, u32[]{:S(2)}) %collective-permute-start.4) | collective-permute-done | bytes 131104 | tf_op jit(solution)/shard_map/ppermute | solution.py:271
  33.5 2.5 %gains.1.gains_hbm = f32[2,512,512]{2,1,0:T(8,128)S(1)} custom-call(f32[2,16]{1,0:T(2,128)S(1)} %copy-done.2, s32[4,4,64,128]{3,2,1,0:T(8,128)S(1)} %pad_add_fusion.near_ref, s32[4,4,64,128]{3,2,1,0:T(8,128)S(1)} %collective-permute-done.6.far_ref, s32[512,1]{1,0:T(8,128)S(1)} %copy.17.column_ref), custom_call_target="tpu_custom_call" | custom-call | tf_op jit(solution)/shard_map/gains/pallas_call | solution.py:341
  40.7 10.5 %multiples.2 = f32[8,4,2,64,128]{4,3,2,1,0:T(8,128)} custom-call(s32[4]{0:T(128)S(1)} %copy-done.1, s32[512,1]{1,0:T(8,128)S(1)} %copy.17.column_ref, s32[1,512]{1,0:T(1,128)S(1)} %bitcast.21, f32[16,2,64,512]{3,2,1,0:T(8,128)} %spectra_ref.7, f32[2,512,512]{2,1,0:T(8,128)S(1)} %gains.1.gains_hbm, f32[8,2,64,512]{3,2,1,0:T(8,128)} %all-to-all-done.refs_0_), custom_call_target="tpu_custom_call" | custom-call | tf_op jit(solution)/shard_map/multiples/pallas_call | solution.py:364
  51.2 4.4 %all-to-all-start.1 = ((f32[32,2,64,128]{3,2,1,0:T(8,128)}), f32[32,2,64,128]{3,2,1,0:T(8,128)}, u32[]{:S(2)}, u32[]{:S(2)}) async-start(f32[32,2,64,128]{3,2,1,0:T(8,128)} %bitcast.23), calls=%async_computation.1 | async-start | bytes 4194304 | tf_op jit(solution)/shard_map/all_to_all | solution.py:409
  61.3 16.8 %collective-permute-done.10.refs_2_ = f32[2,64,512]{2,1,0:T(8,128)S(1)} collective-permute-done((f32[2,64,512]{2,1,0:T(8,128)}, f32[2,64,512]{2,1,0:T(8,128)S(1)}, u32[]{:S(2)}, u32[]{:S(2)}) %collective-permute-start.10) | collective-permute-done | bytes 262176 | tf_op jit(solution)/shard_map/ppermute | solution.py:271
  78.1 2.7 %collective-permute-done.11.refs_4_ = f32[2,64,512]{2,1,0:T(8,128)S(1)} collective-permute-done((f32[2,64,512]{2,1,0:T(8,128)}, f32[2,64,512]{2,1,0:T(8,128)S(1)}, u32[]{:S(2)}, u32[]{:S(2)}) %collective-permute-start.11) | collective-permute-done | bytes 262176 | tf_op jit(solution)/shard_map/ppermute | solution.py:271
  80.8 8.4 %collective-permute-done.12.refs_5_ = f32[2,64,512]{2,1,0:T(8,128)S(1)} collective-permute-done((f32[2,64,512]{2,1,0:T(8,128)S(1)}, f32[2,64,512]{2,1,0:T(8,128)S(1)}, u32[]{:S(2)}, u32[]{:S(2)}) %collective-permute-start.12) | collective-permute-done | bytes 262176 | tf_op jit(solution)/shard_map/ppermute | solution.py:271
  89.2 7.7 %collective-permute-done.13.refs_6_ = f32[2,64,512]{2,1,0:T(8,128)S(1)} collective-permute-done((f32[2,64,512]{2,1,0:T(8,128)S(1)}, f32[2,64,512]{2,1,0:T(8,128)S(1)}, u32[]{:S(2)}, u32[]{:S(2)}) %collective-permute-start.13) | collective-permute-done | bytes 262176 | tf_op jit(solution)/shard_map/ppermute | solution.py:271
  97.0 2.4 %multiples.3 = (f32[8,4,2,48,128]{4,3,2,1,0:T(8,128)}, f32[8,4,2,16,128]{4,3,2,1,0:T(8,128)}) custom-call(s32[4]{0:T(128)S(1)} %copy-done.1, s32[512,1]{1,0:T(8,128)S(1)} %copy.17.column_ref, s32[1,512]{1,0:T(1,128)S(1)} %bitcast.22, f32[16,2,64,512]{3,2,1,0:T(8,128)} %spectra_ref.7, f32[2,512,512]{2,1,0:T(8,128)S(1)} %gains.1.gains_hbm, ...), custom_call_target="tpu_custom_call" | custom-call | tf_op jit(solution)/shard_map/multiples/pallas_call | solution.py:364
  99.4 3.7 %all-to-all-done.1 = f32[32,2,64,128]{3,2,1,0:T(8,128)} async-done(((f32[32,2,64,128]{3,2,1,0:T(8,128)}), f32[32,2,64,128]{3,2,1,0:T(8,128)}, u32[]{:S(2)}, u32[]{:S(2)}) %all-to-all-start.1) | async-done | bytes 2097184 | tf_op jit(solution)/shard_map/all_to_all | solution.py:409
  103.1 10.3 %all-to-all-start.3 = ((f32[32,2,48,128]{3,2,1,0:T(8,128)}), f32[32,2,48,128]{3,2,1,0:T(8,128)S(1)}, u32[]{:S(2)}, u32[]{:S(2)}) async-start(f32[32,2,48,128]{3,2,1,0:T(8,128)} %bitcast.24), calls=%async_computation.3 | async-start | bytes 3145728 | tf_op jit(solution)/shard_map/all_to_all | solution.py:409
  114.2 16.4 %synthesis.3.refs_0_.refs_1_.refs_2_.refs_3_ = f32[128,64,512]{2,1,0:T(8,128)} custom-call(f32[64,512]{1,0:T(8,128)S(1)} %reshape.258.table_ref, f32[128,64,512]{2,1,0:T(8,128)} %refs_3_.1, f32[128,64,512]{2,1,0:T(8,128)} %refs_3_.1, f32[128,64,512]{2,1,0:T(8,128)} %refs_3_.1, f32[128,64,512]{2,1,0:T(8,128)} %refs_3_.1, f32[4096,128]{1,0:T(8,128)} %bitcast.14.refs_4_), custom_call_target="tpu_custom_call" | custom-call | tf_op jit(solution)/shard_map/synthesis/pallas_call | solution.py:312
  130.6 18.7 %all-to-all-done.3 = f32[32,2,48,128]{3,2,1,0:T(8,128)S(1)} async-done(((f32[32,2,48,128]{3,2,1,0:T(8,128)}), f32[32,2,48,128]{3,2,1,0:T(8,128)S(1)}, u32[]{:S(2)}, u32[]{:S(2)}) %all-to-all-start.3) | async-done | bytes 1572896 | tf_op jit(solution)/shard_map/all_to_all | solution.py:409
  149.4 4.6 %all-to-all-start.2 = ((f32[32,2,16,128]{3,2,1,0:T(8,128)}), f32[32,2,16,128]{3,2,1,0:T(8,128)S(1)}, u32[]{:S(2)}, u32[]{:S(2)}) async-start(f32[32,2,16,128]{3,2,1,0:T(8,128)} %bitcast.11), calls=%async_computation.2 | async-start | bytes 1048576 | tf_op jit(solution)/shard_map/all_to_all | solution.py:409
  154.6 11.1 %synthesis.4.refs_5_ = f32[128,64,512]{2,1,0:T(8,128)} custom-call(f32[64,512]{1,0:T(8,128)S(1)} %reshape.256.table_ref, f32[128,64,512]{2,1,0:T(8,128)} %synthesis.3.refs_0_.refs_1_.refs_2_.refs_3_, f32[128,64,512]{2,1,0:T(8,128)} %synthesis.3.refs_0_.refs_1_.refs_2_.refs_3_, f32[128,64,512]{2,1,0:T(8,128)} %synthesis.3.refs_0_.refs_1_.refs_2_.refs_3_, ...), custom_call_target="tpu_custom_call" | custom-call | tf_op jit(solution)/shard_map/synthesis/pallas_call | solution.py:312
  165.8 2.6 %all-to-all-done.2 = f32[32,2,16,128]{3,2,1,0:T(8,128)S(1)} async-done(((f32[32,2,16,128]{3,2,1,0:T(8,128)}), f32[32,2,16,128]{3,2,1,0:T(8,128)S(1)}, u32[]{:S(2)}, u32[]{:S(2)}) %all-to-all-start.2) | async-done | bytes 524320 | tf_op jit(solution)/shard_map/all_to_all | solution.py:409
  168.3 4.1 %synthesis.5 = f32[128,64,512]{2,1,0:T(8,128)} custom-call(f32[64,512]{1,0:T(8,128)S(1)} %reshape.256.table_ref, f32[128,64,512]{2,1,0:T(8,128)} %synthesis.3.refs_0_.refs_1_.refs_2_.refs_3_, f32[128,64,512]{2,1,0:T(8,128)} %synthesis.3.refs_0_.refs_1_.refs_2_.refs_3_, ...), custom_call_target="tpu_custom_call", output_to_operand_aliasing={{}: (6, {})} | custom-call | tf_op jit(solution)/shard_map/synthesis/pallas_call | solution.py:312
  (49 shorter events, 16.3 us)
Async XLA Ops:
  0.0 9.5 %copy-start.3 = (s32[128,64]{0,1:T(8,128)S(1)}, s32[128,64]{0,1:T(8,128)}, u32[]{:S(2)}) copy-start(s32[128,64]{0,1:T(8,128)} %param.10) | copy-start | bytes 98308
  0.0 6.9 %collective-permute-start.1 = (s32[64,128]{1,0:T(8,128)}, s32[64,128]{1,0:T(8,128)S(1)}, u32[]{:S(2)}, u32[]{:S(2)}) collective-permute-start(s32[64,128]{1,0:T(8,128)} %bitcast.29), channel_id=1, source_target_pairs={{0,4},{1,5},{2,6},{3,7},{4,0},{5,1},{6,2},{7,3},{8,12},{9,13},{10,... | collective-permute-start | bytes 98312 | tf_op jit(solution)/shard_map/ppermute | solution.py:271
  3.0 4.2 %collective-permute-start = (s32[64,128]{1,0:T(8,128)}, s32[64,128]{1,0:T(8,128)S(1)}, u32[]{:S(2)}, u32[]{:S(2)}) collective-permute-start(s32[64,128]{1,0:T(8,128)} %bitcast.30), channel_id=1, source_target_pairs={{0,2},{1,3},{2,0},{3,1},{4,6},{5,7},{6,4},{7,5},{8,10},{9,11},{10,... | collective-permute-start | bytes 98312 | tf_op jit(solution)/shard_map/ppermute | solution.py:271
  4.5 5.0 %collective-permute-start.2 = (s32[64,128]{1,0:T(8,128)}, s32[64,128]{1,0:T(8,128)S(1)}, u32[]{:S(2)}, u32[]{:S(2)}) collective-permute-start(s32[64,128]{1,0:T(8,128)} %bitcast.31), channel_id=1, source_target_pairs={{0,6},{1,7},{2,4},{3,5},{4,2},{5,3},{6,0},{7,1},{8,14},{9,15},{10,... | collective-permute-start | bytes 98312 | tf_op jit(solution)/shard_map/ppermute | solution.py:271
  9.5 31.2 %all-to-all-start = ((f32[8,2,64,512]{3,2,1,0:T(8,128)}), f32[8,2,64,512]{3,2,1,0:T(8,128)}, u32[]{:S(2)}, u32[]{:S(2)}) async-start(f32[8,2,64,512]{3,2,1,0:T(8,128)} %pack.2), calls=%async_computation | async-start | bytes 4194304 | tf_op jit(solution)/shard_map/all_to_all | solution.py:335
  13.9 17.8 %copy-start = (s32[512]{0:T(512)S(1)}, s32[512]{0:T(512)}, u32[]{:S(2)}) copy-start(s32[512]{0:T(512)} %param.8) | copy-start | bytes 6148
  13.9 19.7 %copy-start.2 = (f32[2,16]{1,0:T(2,128)S(1)}, f32[2,16]{1,0:T(2,128)}, u32[]{:S(2)}) copy-start(f32[2,16]{1,0:T(2,128)} %table_ref.1) | copy-start | bytes 388
  16.2 8.3 %collective-permute-start.5 = (s32[4,64,128]{2,1,0:T(8,128)S(1)}, s32[4,64,128]{2,1,0:T(8,128)S(1)}, u32[]{:S(2)}, u32[]{:S(2)}) collective-permute-start(s32[4,64,128]{2,1,0:T(8,128)S(1)} %pad_add_fusion.1), channel_id=1, source_target_pairs={{0,24},{8,16},{16,8},{24,0},{1,25},{9,17},{17,9},{25,1},{2,26},{10... | collective-permute-start | bytes 393224 | tf_op jit(solution)/shard_map/ppermute | solution.py:271
  19.9 11.6 %collective-permute-start.4 = (s32[4,64,128]{2,1,0:T(8,128)S(1)}, s32[4,64,128]{2,1,0:T(8,128)S(1)}, u32[]{:S(2)}, u32[]{:S(2)}) collective-permute-start(s32[4,64,128]{2,1,0:T(8,128)S(1)} %pad_add_fusion.1), channel_id=1, source_target_pairs={{0,16},{8,24},{16,0},{24,8},{1,17},{9,25},{17,1},{25,9},{2,18},{10... | collective-permute-start | bytes 393224 | tf_op jit(solution)/shard_map/ppermute | solution.py:271
  19.9 11.6 %collective-permute-start.3 = (s32[4,64,128]{2,1,0:T(8,128)S(1)}, s32[4,64,128]{2,1,0:T(8,128)S(1)}, u32[]{:S(2)}, u32[]{:S(2)}) collective-permute-start(s32[4,64,128]{2,1,0:T(8,128)S(1)} %pad_add_fusion.1), channel_id=1, source_target_pairs={{0,8},{8,0},{16,24},{24,16},{1,9},{9,1},{17,25},{25,17},{2,10},{10... | collective-permute-start | bytes 393224 | tf_op jit(solution)/shard_map/ppermute | solution.py:271
  31.6 9.1 %copy-start.1 = (s32[4]{0:T(128)S(1)}, s32[4]{0:T(128)}, u32[]{:S(2)}) copy-start(s32[4]{0:T(128)} %counts_ref.3) | copy-start | bytes 52
  31.6 2.0 %collective-permute-start.6 = (s32[4,4,64,128]{3,2,1,0:T(8,128)S(1)}, s32[4,4,64,128]{3,2,1,0:T(8,128)S(1)}, u32[]{:S(2)}, u32[]{:S(2)}) collective-permute-start(s32[4,4,64,128]{3,2,1,0:T(8,128)S(1)} %pad_add_fusion.near_ref), channel_id=1, source_target_pairs={{0,1},{1,0},{2,3},{3,2},{4,5},{5,4},{6,7},{7,6},{8,9},{9,8},{10,11... | collective-permute-start | bytes 1572872 | tf_op jit(solution)/shard_map/ppermute | solution.py:271
  36.1 15.1 %collective-permute-start.7 = (f32[2,64,512]{2,1,0:T(8,128)}, f32[2,64,512]{2,1,0:T(8,128)S(1)}, u32[]{:S(2)}, u32[]{:S(2)}) collective-permute-start(f32[2,64,512]{2,1,0:T(8,128)} %get-tuple-element.42), channel_id=1, source_target_pairs={{0,2},{1,3},{2,0},{3,1},{4,6},{5,7},{6,4},{7,5},{8,10},{9,11},{10,... | collective-permute-start | bytes 786440 | tf_op jit(solution)/shard_map/ppermute | solution.py:271
  37.8 13.4 %collective-permute-start.8 = (f32[2,64,512]{2,1,0:T(8,128)}, f32[2,64,512]{2,1,0:T(8,128)S(1)}, u32[]{:S(2)}, u32[]{:S(2)}) collective-permute-start(f32[2,64,512]{2,1,0:T(8,128)} %get-tuple-element.43), channel_id=1, source_target_pairs={{0,4},{1,5},{2,6},{3,7},{4,0},{5,1},{6,2},{7,3},{8,12},{9,13},{10,... | collective-permute-start | bytes 786440 | tf_op jit(solution)/shard_map/ppermute | solution.py:271
  51.2 7.6 %copy-start.5 = (f32[2,64,512]{2,1,0:T(8,128)S(1)}, f32[2,64,512]{2,1,0:T(8,128)}, u32[]{:S(2)}) copy-start(f32[2,64,512]{2,1,0:T(8,128)} %get-tuple-element.52) | copy-start | bytes 786436
  51.2 7.9 %copy-start.4 = (f32[2,64,512]{2,1,0:T(8,128)S(1)}, f32[2,64,512]{2,1,0:T(8,128)}, u32[]{:S(2)}) copy-start(f32[2,64,512]{2,1,0:T(8,128)} %get-tuple-element.53) | copy-start | bytes 786436
  51.2 51.9 %all-to-all-start.1 = ((f32[32,2,64,128]{3,2,1,0:T(8,128)}), f32[32,2,64,128]{3,2,1,0:T(8,128)}, u32[]{:S(2)}, u32[]{:S(2)}) async-start(f32[32,2,64,128]{3,2,1,0:T(8,128)} %bitcast.23), calls=%async_computation.1 | async-start | bytes 4194304 | tf_op jit(solution)/shard_map/all_to_all | solution.py:409
  55.6 22.5 %collective-permute-start.10 = (f32[2,64,512]{2,1,0:T(8,128)}, f32[2,64,512]{2,1,0:T(8,128)S(1)}, u32[]{:S(2)}, u32[]{:S(2)}) collective-permute-start(f32[2,64,512]{2,1,0:T(8,128)} %get-tuple-element.49), channel_id=1, source_target_pairs={{0,3},{1,2},{2,1},{3,0},{4,7},{5,6},{6,5},{7,4},{8,11},{9,10},{10,... | collective-permute-start | bytes 786440 | tf_op jit(solution)/shard_map/ppermute | solution.py:271
  57.1 23.7 %collective-permute-start.11 = (f32[2,64,512]{2,1,0:T(8,128)}, f32[2,64,512]{2,1,0:T(8,128)S(1)}, u32[]{:S(2)}, u32[]{:S(2)}) collective-permute-start(f32[2,64,512]{2,1,0:T(8,128)} %get-tuple-element.51), channel_id=1, source_target_pairs={{0,5},{1,4},{2,7},{3,6},{4,1},{5,0},{6,3},{7,2},{8,13},{9,12},{10,... | collective-permute-start | bytes 786440 | tf_op jit(solution)/shard_map/ppermute | solution.py:271
  58.6 22.2 %collective-permute-start.9 = (f32[2,64,512]{2,1,0:T(8,128)}, f32[2,64,512]{2,1,0:T(8,128)S(1)}, u32[]{:S(2)}, u32[]{:S(2)}) collective-permute-start(f32[2,64,512]{2,1,0:T(8,128)} %get-tuple-element.47), channel_id=1, source_target_pairs={{0,1},{1,0},{2,3},{3,2},{4,5},{5,4},{6,7},{7,6},{8,9},{9,8},{10,11... | collective-permute-start | bytes 786440 | tf_op jit(solution)/shard_map/ppermute | solution.py:271
  58.7 30.5 %collective-permute-start.12 = (f32[2,64,512]{2,1,0:T(8,128)S(1)}, f32[2,64,512]{2,1,0:T(8,128)S(1)}, u32[]{:S(2)}, u32[]{:S(2)}) collective-permute-start(f32[2,64,512]{2,1,0:T(8,128)S(1)} %copy-done.5), channel_id=1, source_target_pairs={{0,6},{1,7},{2,4},{3,5},{4,2},{5,3},{6,0},{7,1},{8,14},{9,15},{10,... | collective-permute-start | bytes 786440 | tf_op jit(solution)/shard_map/ppermute | solution.py:271
  59.1 37.9 %collective-permute-start.13 = (f32[2,64,512]{2,1,0:T(8,128)S(1)}, f32[2,64,512]{2,1,0:T(8,128)S(1)}, u32[]{:S(2)}, u32[]{:S(2)}) collective-permute-start(f32[2,64,512]{2,1,0:T(8,128)S(1)} %copy-done.4), channel_id=1, source_target_pairs={{0,7},{1,6},{2,5},{3,4},{4,3},{5,2},{6,1},{7,0},{8,15},{9,14},{10,... | collective-permute-start | bytes 786440 | tf_op jit(solution)/shard_map/ppermute | solution.py:271
  103.1 46.3 %all-to-all-start.3 = ((f32[32,2,48,128]{3,2,1,0:T(8,128)}), f32[32,2,48,128]{3,2,1,0:T(8,128)S(1)}, u32[]{:S(2)}, u32[]{:S(2)}) async-start(f32[32,2,48,128]{3,2,1,0:T(8,128)} %bitcast.24), calls=%async_computation.3 | async-start | bytes 3145728 | tf_op jit(solution)/shard_map/all_to_all | solution.py:409
  149.4 18.9 %all-to-all-start.2 = ((f32[32,2,16,128]{3,2,1,0:T(8,128)}), f32[32,2,16,128]{3,2,1,0:T(8,128)S(1)}, u32[]{:S(2)}, u32[]{:S(2)}) async-start(f32[32,2,16,128]{3,2,1,0:T(8,128)} %bitcast.11), calls=%async_computation.2 | async-start | bytes 1048576 | tf_op jit(solution)/shard_map/all_to_all | solution.py:409
